TPU v7x, 128 devices: a whole 4x4x4 slice. The times are simulated.
128 devices in a mesh: dp: 2 (over y_lo), row: 2 (over y_hi), col: 32 (over z, x, core).
Axes of the slice: x: 4, y: 4 (y_hi: 2, y_lo: 2; y = y_hi * 2 + y_lo), z: 4, core: 2. Of those that a mesh axis runs over, the one named last changes fastest.
Arguments:
- expanded: bfloat16 [4, 64, 32, 32, 1024], P('dp', ('row', 'col')), may hold values from -6 to 6
- skip: bfloat16 [4, 64, 32, 32, 256], P('dp', ('row', 'col')), may hold values from -6 to 6
- cotangent: bfloat16 [4, 64, 32, 32, 256], P('dp', ('row', 'col')), may hold values from -6 to 6
- depth_kernel: float32 [3, 3, 1024], replicated, may hold values from -2 to 2
- w_proj: bfloat16 [1024, 256], replicated, may hold values from -0.1875 to 0.1875
- norm_gain: float32 [256], replicated, may hold values from 0.5 to 1.5
- w_qkv: bfloat16 [256, 768], replicated, may hold values from -1 to 1
- w_out: bfloat16 [256, 256], replicated, may hold values from -0.375 to 0.375
Outputs:
- grad_expanded: bfloat16 [4, 64, 32, 32, 1024], P('dp', ('row', 'col'))
- grad_skip: bfloat16 [4, 64, 32, 32, 256], P('dp', ('row', 'col'))
- grad_kernel: float32 [3, 3, 1024], replicated
- grad_proj: float32 [1024, 256], replicated
- grad_wqkv: float32 [256, 768], replicated
- grad_out: float32 [256, 256], replicated
- grad_gain: float32 [256], replicated
All inputs are finite; a program needn't handle non-finite values.
Results may differ from a plain program's by a relative error of at most 0.023.
The roundings to bfloat16 on the way count: a program that leaves them out, or rounds other values in their place, can miss the bound.
Values may be sent and summed in bfloat16 or wider, within the bound.
A program may use at most 192 MiB of HBM per device.

v0:
```python
import math

import jax
import jax.numpy as jnp
from jax import lax
from jax.sharding import PartitionSpec as P

HEADS = 8
GRID = 8


def passed_along(block, axis, distance):
    devices = range(lax.axis_size(axis))
    route = [(i - distance, i) for i in devices if i - distance in devices]
    return lax.ppermute(block, axis, route)


def contract(pattern, left_op, right_op):
    return jnp.einsum(pattern, left_op, right_op, preferred_element_type=jnp.float32)


def transposed_dot(left_op, right_op):
    return lax.dot_general(
        left_op, right_op, (((0,), (0,)), ((), ())), preferred_element_type=jnp.float32
    )


def smooth(inside):
    return jax.nn.gelu(inside, approximate=True)


def depthwise(padded, kernel, n_rows, n_cols):
    summed = jnp.zeros(padded.shape[:-3] + (n_rows, n_cols, padded.shape[-1]), jnp.float32)
    for row_off in range(3):
        for col_off in range(3):
            summed = summed + kernel[row_off, col_off] * padded[
                ..., row_off : row_off + n_rows, col_off : col_off + n_cols, :
            ].astype(jnp.float32)
    return summed


def depthwise_back(padded_grad, kernel, n_rows, n_cols):
    summed = jnp.zeros(
        padded_grad.shape[:-3] + (n_rows, n_cols, padded_grad.shape[-1]), jnp.float32
    )
    for row_off in range(3):
        for col_off in range(3):
            summed = summed + kernel[row_off, col_off] * padded_grad[
                ..., 2 - row_off : 2 - row_off + n_rows, 2 - col_off : 2 - col_off + n_cols, :
            ].astype(jnp.float32)
    return summed


def kernel_grad(grad_pre, padded, n_rows, n_cols):
    grad_float = grad_pre.astype(jnp.float32)
    lead_axes = tuple(range(grad_float.ndim - 1))
    stacked = []
    for row_off in range(3):
        row_terms = []
        for col_off in range(3):
            window = padded[..., row_off : row_off + n_rows, col_off : col_off + n_cols, :].astype(
                jnp.float32
            )
            row_terms.append(jnp.sum(grad_float * window, axis=lead_axes))
        stacked.append(jnp.stack(row_terms))
    return jnp.stack(stacked)


def attend_back(mixture, cotangent, norm_gain, w_qkv, w_out, n_heads):
    groups, length, model_dim = mixture.shape
    head_size = model_dim // n_heads
    score_scale = 1.0 / math.sqrt(head_size)
    mix_float = mixture.astype(jnp.float32)
    inverse = lax.rsqrt(jnp.mean(mix_float * mix_float, axis=-1, keepdims=True) + 1e-06)
    normed = (mix_float * inverse * norm_gain).astype(jnp.bfloat16)
    flat_norm = normed.reshape(groups * length, model_dim)
    proj_qkv = jnp.dot(flat_norm, w_qkv, preferred_element_type=jnp.float32).astype(jnp.bfloat16)
    proj_qkv = proj_qkv.reshape(groups, length, 3, n_heads, head_size)
    queries = proj_qkv[:, :, 0]
    key_rows = proj_qkv[:, :, 1]
    values = proj_qkv[:, :, 2]
    scores = contract("gqhd,gkhd->ghqk", queries, key_rows) * score_scale
    attn_probs = jax.nn.softmax(scores, axis=-1)
    weights_bf = attn_probs.astype(jnp.bfloat16)
    attended = contract("ghqk,gkhd->gqhd", weights_bf, values).astype(jnp.bfloat16)
    attended = attended.reshape(groups * length, model_dim)
    flat_cot = cotangent.reshape(groups * length, model_dim)
    grad_out = transposed_dot(attended, flat_cot)
    grad_att = jnp.dot(flat_cot, w_out.T, preferred_element_type=jnp.float32).astype(jnp.bfloat16)
    grad_att = grad_att.reshape(groups, length, n_heads, head_size)
    grad_values = contract("ghqk,gqhd->gkhd", weights_bf, grad_att)
    grad_probs = contract("gqhd,gkhd->ghqk", grad_att, values)
    grad_scores = (
        attn_probs
        * (grad_probs - jnp.sum(grad_probs * attn_probs, axis=-1, keepdims=True))
        * score_scale
    )
    grad_scores = grad_scores.astype(jnp.bfloat16)
    grad_query = contract("ghqk,gkhd->gqhd", grad_scores, key_rows)
    grad_keys = contract("ghqk,gqhd->gkhd", grad_scores, queries)
    grad_qkv = jnp.stack([grad_query, grad_keys, grad_values], axis=2).astype(jnp.bfloat16)
    grad_qkv = grad_qkv.reshape(groups * length, 3 * model_dim)
    grad_wqkv = transposed_dot(flat_norm, grad_qkv)
    grad_normed = jnp.dot(grad_qkv, w_qkv.T, preferred_element_type=jnp.float32).reshape(
        groups, length, model_dim
    )
    grad_gain = jnp.sum(grad_normed * mix_float * inverse, axis=(0, 1))
    scaled = grad_normed * norm_gain
    grad_mix = inverse * scaled - mix_float * inverse * inverse * inverse * jnp.mean(
        scaled * mix_float, axis=-1, keepdims=True
    )
    summed = (cotangent.astype(jnp.float32) + grad_mix).astype(jnp.bfloat16)
    return (summed, grad_wqkv, grad_out, grad_gain)


def pad_tile(tile, width):
    tile_col = lax.axis_index(("row", "col")) % GRID
    from_left = passed_along(tile[:, :, -width:], ("row", "col"), 1)
    from_right = passed_along(tile[:, :, :width], ("row", "col"), -1)
    from_left = jnp.where(tile_col == 0, jnp.zeros_like(from_left), from_left)
    from_right = jnp.where(tile_col == GRID - 1, jnp.zeros_like(from_right), from_right)
    sided = jnp.concatenate([from_left, tile, from_right], axis=2)
    from_above = passed_along(sided[:, -width:], ("row", "col"), GRID)
    from_below = passed_along(sided[:, :width], ("row", "col"), -GRID)
    return jnp.concatenate([from_above, sided, from_below], axis=1)


def to_targets(tile, n_tiles, per_tile, group_part):
    pictures, rows_here, cols_here, channels = tile.shape
    tile = tile.reshape(pictures, per_tile, n_tiles, group_part, channels)
    tile = tile.transpose(2, 0, 1, 3, 4)
    return tile.reshape(n_tiles, 1, pictures, per_tile, group_part, channels)


def received_to_groups(tensor, row_tiles, per_tile, group_part):
    pictures = tensor.shape[2]
    channels = tensor.shape[-1]
    tensor = tensor.reshape(row_tiles, GRID, pictures, per_tile, group_part, channels)
    tensor = tensor.transpose(2, 4, 0, 3, 1, 5)
    return tensor.reshape(pictures * group_part, GRID * GRID, channels)


def groups_to_targets(tensor, pictures, row_tiles, per_tile, group_part):
    channels = tensor.shape[-1]
    tensor = tensor.reshape(pictures, group_part, row_tiles, per_tile, GRID, channels)
    tensor = tensor.transpose(2, 4, 0, 3, 1, 5)
    return tensor.reshape(row_tiles * GRID, 1, pictures, per_tile, group_part, channels)


def returned_to_tile(tensor, n_tiles, rows_here, cols_here):
    pictures, per_tile, group_part, channels = tensor.shape[2:]
    tensor = tensor.reshape(n_tiles, pictures, per_tile, group_part, channels).transpose(
        1, 2, 0, 3, 4
    )
    return tensor.reshape(pictures, rows_here, cols_here, channels)


def on_device(expanded, skip, cotangent, depth_kernel, w_proj, norm_gain, w_qkv, w_out):
    expanded = expanded[:, 0]
    skip = skip[:, 0]
    cotangent = cotangent[:, 0]
    pictures, rows_here, cols_here, expand_dim = expanded.shape
    model_dim = skip.shape[3]
    n_row = lax.axis_size("row")
    n_col = lax.axis_size("col")
    n_tiles = n_row * n_col
    row_tiles = n_tiles // GRID
    span_a = rows_here * row_tiles // GRID
    per_tile = GRID // row_tiles
    group_part = span_a * cols_here // n_tiles
    token_count = pictures * lax.axis_size("dp") * rows_here * cols_here * n_tiles
    factor = 1.0 / math.sqrt(token_count)
    padded = pad_tile(expanded, 1)
    pre_act = depthwise(padded, depth_kernel, rows_here, cols_here)
    activated = smooth(pre_act).astype(jnp.bfloat16)
    flat_act = activated.reshape(-1, expand_dim)
    projected = jnp.dot(flat_act, w_proj, preferred_element_type=jnp.float32).reshape(
        pictures, rows_here, cols_here, model_dim
    )
    mixture = (skip.astype(jnp.float32) + projected).astype(jnp.bfloat16)
    send_mix = to_targets(mixture, n_tiles, per_tile, group_part)
    send_cot = to_targets(cotangent, n_tiles, per_tile, group_part)
    got_mix, got_cot = (
        lax.all_to_all(send_mix, ("row", "col"), split_axis=0, concat_axis=1, tiled=True),
        lax.all_to_all(send_cot, ("row", "col"), split_axis=0, concat_axis=1, tiled=True),
    )
    summed, grad_wqkv, grad_out, grad_gain = attend_back(
        received_to_groups(got_mix, row_tiles, per_tile, group_part),
        received_to_groups(got_cot, row_tiles, per_tile, group_part),
        norm_gain,
        w_qkv,
        w_out,
        HEADS,
    )
    back_parts = groups_to_targets(summed, pictures, row_tiles, per_tile, group_part)
    returned = lax.all_to_all(back_parts, ("row", "col"), split_axis=0, concat_axis=1, tiled=True)
    grad_skip = returned_to_tile(returned, n_tiles, rows_here, cols_here)
    flat_grad = grad_skip.reshape(-1, model_dim)
    grad_proj = transposed_dot(flat_act, flat_grad)
    grad_act = jnp.dot(flat_grad, w_proj.T, preferred_element_type=jnp.float32)
    grad_act = grad_act.reshape(pictures, rows_here, cols_here, expand_dim)
    _, pullback = jax.vjp(smooth, pre_act)
    grad_pre = pullback(grad_act)[0].astype(jnp.bfloat16)
    grad_pre_pad = pad_tile(grad_pre, 1)
    grad_kernel = kernel_grad(grad_pre, padded, rows_here, cols_here)
    grad_expanded = depthwise_back(grad_pre_pad, depth_kernel, rows_here, cols_here).astype(
        jnp.bfloat16
    )
    grad_kernel, grad_proj, grad_wqkv, grad_out, grad_gain = lax.psum(
        (grad_kernel, grad_proj, grad_wqkv, grad_out, grad_gain), ("dp", "row", "col")
    )
    return (
        grad_expanded[:, None],
        grad_skip[:, None],
        grad_kernel * factor,
        grad_proj * factor,
        grad_wqkv * factor,
        grad_out * factor,
        grad_gain * factor,
    )


def solution(mesh):
    placed = (
        P("dp", ("row", "col"), None, None, None),
        P("dp", ("row", "col"), None, None, None),
        P("dp", ("row", "col"), None, None, None),
        P(),
        P(),
        P(),
        P(),
        P(),
    )
    return jax.shard_map(
        on_device,
        mesh=mesh,
        in_specs=placed,
        out_specs=(
            P("dp", ("row", "col"), None, None, None),
            P("dp", ("row", "col"), None, None, None),
            P(),
            P(),
            P(),
            P(),
            P(),
        ),
        check_vma=False,
    )
```

profile of v0, /device:TPU:1, one launch (start us, length us, event | category | flops | bytes accessed | tf_op | source)
XLA Modules:
  0.0 516.7 jit_solution(13955091710161633405)
XLA Ops:
  7.2 2.1 fusion.80
  9.3 4.5 collective-permute-start
  13.8 1.9 collective-permute-start.1
  15.7 2.4 copy.75
  18.1 11.6 %all-to-all-start = ((bf16[64,1,2,1,16,256]{5,4,2,3,1,0:T(8,128)(2,1)}), bf16[64,1,2,1,16,256]{5,4,2,3,1,0:T(8,128)(2,1)S(1)}, u32[]{:S(2)}, u32[]{:S(2)}) async-start(bf16[64,1,2,1,16,256]{5,4,2,3,1,0:T(8,128)(2,1)} %copy.75), calls=%async_computation | async-start | bytes 2097152 | tf_op jit(solution)/shard_map/all_to_all | solution.py:185
  30.3 1.4 pad_maximum_fusion.11
  31.7 3.3 collective-permute-start.2
  35.0 1.3 collective-permute-start.3
  36.4 9.5 %collective-permute-done.2 = bf16[2,1,34,1024]{3,2,1,0:T(8,128)(2,1)S(1)} collective-permute-done((bf16[2,1,34,1024]{3,2,1,0:T(8,128)(2,1)S(1)}, bf16[2,1,34,1024]{3,2,1,0:T(8,128)(2,1)S(1)}, u32[]{:S(2)}, u32[]{:S(2)}) %collective-permute-start.2) | collective-permute-done | bytes 139296 | tf_op jit(solution)/shard_map/ppermute | solution.py:15
  45.9 2.3 collective-permute-done.3
  48.2 6.8 %maximum_maximum_fusion = (bf16[2,33,34,1024]{3,2,1,0:T(8,128)(2,1)S(1)}, bf16[2,33,34,1024]{3,2,1,0:T(8,128)(2,1)S(1)}) fusion(bf16[2,32,1,1024]{3,2,1,0:T(2,128)(2,1)S(1)} %broadcast_select_fusion.1, bf16[2,32,32,1024]{3,2,1,0:T(8,128)(2,1)S(1)} %bitcast.163, bf16[2,32,1,1024]{3,2,1,0:T(2,128)(2,1)S(1)} %broadcast_select_fusion.3, ...), kind=kLoop, calls=%fused_computation.61 | loop fusion | flops 36765696 | bytes 13926400 | tf_op jit(solution)/shard_map/concatenate | solution.py:125
  55.0 15.9 %multiply_convert_fusion.1 = (bf16[2,32,32,1024]{3,2,1,0:T(8,128)(2,1)S(1)}, f32[2,32,32,1024]{3,2,1,0:T(8,128)}) fusion(bf16[2,33,34,1024]{3,2,1,0:T(8,128)(2,1)S(1)} %get-tuple-element.66, f32[1024]{0:T(1024)S(1)} %bitcast.197, f32[1024]{0:T(1024)S(1)} %bitcast.199, f32[1024]{0:T(1024)S(1)} %bitcast.185, ...), kind=kLoop, calls=%fused_computation.58 | loop fusion | flops 85983232 | bytes 42242048 | tf_op jit(solution)/shard_map/convert_element_type | solution.py:175
  71.0 2.0 copy-done.16
  73.0 1.3 fusion.54
  74.2 1.1 copy.127
  75.3 8.8 %all-to-all-start.1 = ((bf16[64,1,2,1,16,256]{5,4,2,3,1,0:T(8,128)(2,1)}), bf16[64,1,2,1,16,256]{5,4,2,3,1,0:T(8,128)(2,1)S(1)}, u32[]{:S(2)}, u32[]{:S(2)}) async-start(bf16[64,1,2,1,16,256]{5,4,2,3,1,0:T(8,128)(2,1)} %bitcast.175), calls=%async_computation.1 | async-start | bytes 2097152 | tf_op jit(solution)/shard_map/all_to_all | solution.py:184
  85.7 1.4 convolution_convert_fusion.1
  87.2 1.5 copy.85
  88.6 3.2 reshape.158
  91.8 11.0 %all-to-all-done.1 = bf16[64,1,2,1,16,256]{5,4,2,3,1,0:T(8,128)(2,1)S(1)} async-done(((bf16[64,1,2,1,16,256]{5,4,2,3,1,0:T(8,128)(2,1)}), bf16[64,1,2,1,16,256]{5,4,2,3,1,0:T(8,128)(2,1)S(1)}, u32[]{:S(2)}, u32[]{:S(2)}) %all-to-all-start.1) | async-done | bytes 1048608 | tf_op jit(solution)/shard_map/all_to_all | solution.py:184
  102.8 1.0 copy-done.11
  104.1 2.6 copy.79
  106.7 1.3 fusion.56
  108.5 3.6 convolution_convert_fusion
  112.1 4.7 copy.82
  116.8 10.1 %reshape.157 = bf16[32,64,3,8,32]{1,0,4,3,2:T(8,128)(2,1)} reshape(bf16[2048,768]{0,1:T(8,128)(2,1)} %copy.82) | data formatting | bytes 6291456 | tf_op jit(solution)/shard_map/reshape | solution.py:78
  126.9 3.9 fusion.78
  130.8 1.3 copy-done.14
  132.8 2.8 fusion.64
  135.6 4.8 fusion.82
  140.5 6.0 %fusion.65 = f32[32,8,64,64]{2,3,1,0:T(8,128)} fusion(bf16[32,64,1,8,32]{1,0,4,3,2:T(8,128)(2,1)S(1)} %get-tuple-element.58, bf16[32,64,8,32]{1,0,3,2:T(8,128)(2,1)S(1)} %copy-done.12), kind=kOutput, calls=%fused_computation.101 | convolution fusion | flops 67108864 | bytes 6291456 | tf_op jit(solution)/shard_map/gqhd,gkhd->ghqk/dot_general | solution.py:19
  146.5 16.4 %fusion.46 = bf16[32,64,1,8,32]{1,4,3,0,2:T(8,128)(2,1)} fusion(f32[32,8,64,64]{2,3,1,0:T(8,128)} %fusion.65, bf16[32,64,1,8,32]{1,0,4,3,2:T(8,128)(2,1)} %copy-done.15, f32[32,8,64,64]{2,3,1,0:T(8,128)} %get-tuple-element.83, f32[32,8,64]{2,1,0:T(8,128)S(1)} %get-tuple-element.82), kind=kOutput, calls=%fused_computation.76 | convolution fusion | flops 74465344 | bytes 10551296 | tf_op jit(solution)/shard_map/ghqk,gkhd->gqhd/dot_general | solution.py:19
  162.9 16.3 %fusion.49 = bf16[32,64,1,8,32]{1,4,3,0,2:T(8,128)(2,1)} fusion(f32[32,8,64,64]{2,3,1,0:T(8,128)} %fusion.65, bf16[32,64,1,8,32]{1,0,4,3,2:T(8,128)(2,1)} %copy-done.14, f32[32,8,64,64]{2,3,1,0:T(8,128)} %get-tuple-element.83, f32[32,8,64]{2,1,0:T(8,128)S(1)} %get-tuple-element.82), kind=kOutput, calls=%fused_computation.77 | convolution fusion | flops 74465344 | bytes 10551296 | tf_op jit(solution)/shard_map/ghqk,gqhd->gkhd/dot_general | solution.py:19
  179.2 7.9 %convolution_bitcast_fusion = bf16[32,64,1,8,32]{1,4,3,0,2:T(8,128)(2,1)} fusion(bf16[32,64,8,32]{1,0,3,2:T(8,128)(2,1)} %reshape.158, f32[32,8,64,64]{2,3,1,0:T(8,128)} %get-tuple-element.83, f32[32,8,64]{2,1,0:T(8,128)S(1)} %get-tuple-element.82), kind=kOutput, calls=%fused_computation.78 | convolution fusion | flops 69206016 | bytes 6356992 | tf_op jit(solution)/shard_map/ghqk,gqhd->gkhd/dot_general | solution.py:19
  187.2 4.2 maximum_convert_fusion
  191.5 2.1 copy.92
  193.5 3.6 multiply_reduce_fusion.2
  198.1 1.6 copy.94
  199.6 5.2 %all-to-all-start.2 = ((bf16[64,1,2,1,16,256]{5,4,2,3,1,0:T(8,128)(2,1)}), bf16[64,1,2,1,16,256]{5,4,2,3,1,0:T(8,128)(2,1)}, u32[]{:S(2)}, u32[]{:S(2)}) async-start(bf16[64,1,2,1,16,256]{5,4,2,3,1,0:T(8,128)(2,1)} %bitcast.42), calls=%async_computation.2 | async-start | bytes 2097152 | tf_op jit(solution)/shard_map/all_to_all | solution.py:196
  205.1 6.5 %convert_bitcast_fusion = bf16[32,64,8,32]{1,3,2,0:T(8,128)(2,1)S(1)} fusion(bf16[32,64,1,8,32]{1,0,4,3,2:T(8,128)(2,1)} %copy-done.13, f32[32,8,64,64]{2,3,1,0:T(8,128)} %get-tuple-element.83, f32[32,8,64]{2,1,0:T(8,128)S(1)} %get-tuple-element.82), kind=kOutput, calls=%fused_computation.95 | convolution fusion | flops 69730304 | bytes 6356992 | tf_op jit(solution)/shard_map/ghqk,gkhd->gqhd/dot_general | solution.py:19
  211.6 9.5 %copy.96 = bf16[32,64,3,8,32]{1,0,4,3,2:T(8,128)(2,1)} copy(bf16[32,64,3,8,32]{1,4,3,0,2:T(8,128)(2,1)} %copy-done.3) | data formatting | bytes 6291456 | tf_op jit(solution)/shard_map/convert_element_type | solution.py:101
  221.1 2.7 copy.98
  223.8 4.6 reshape.163
  228.4 9.7 %convert_element_type.204 = bf16[2048,768]{0,1:T(8,128)(2,1)} reshape(bf16[32,64,3,8,32]{1,0,4,3,2:T(8,128)(2,1)} %copy.96) | data formatting | bytes 6291456 | tf_op jit(solution)/shard_map/convert_element_type | solution.py:101
  238.1 2.7 fusion.85
  240.8 1.2 fusion.58
  242.0 3.9 fusion.84
  245.9 1.3 copy.95
  247.2 26.1 %fusion.23 = (f32[1024]{0:T(1024)S(1)}, f32[1024]{0:T(1024)S(1)}, f32[1024]{0:T(1024)S(1)}, f32[1024]{0:T(1024)S(1)}, f32[1024]{0:T(1024)S(1)}, /*index=5*/f32[1...) fusion(bf16[2,33,34,1024]{3,2,1,0:T(8,128)(2,1)} %copy-done.1, ...), kind=kOutput, calls=%fused_computation.45 | convolution fusion | flops 1186978816 | bytes 48009216 | tf_op jit(solution)/shard_map/dot_general | solution.py:200
  273.3 2.0 copy-done.5
  275.8 3.5 collective-permute-start.4
  279.3 1.9 collective-permute-start.5
  281.3 2.3 fusion.83
  283.6 69.4 %all-reduce = (f32[3,3,1024]{2,1,0:T(4,128)S(1)}, f32[256]{0:T(256)S(1)}) all-reduce(f32[3,3,1024]{2,1,0:T(4,128)S(1)} %pad_maximum_fusion.12, f32[256]{0:T(256)S(1)} %get-tuple-element.43), channel_id=1, replica_groups=mesh['dp'=2,'row'=2,'col'=32] {'dp','row','col'}, use_global_device_ids=true, to_apply=%region_14.15 | all-reduce | flops 9472 | bytes 75776 | tf_op jit(solution)/shard_map/psum | solution.py:209
  354.3 1.1 pad_maximum_fusion.8
  355.4 1.3 collective-permute-start.6
  356.7 4.0 collective-permute-start.7
  361.3 1.7 collective-permute-done.6
  363.8 6.8 %pad_maximum_fusion.1 = (bf16[2,33,34,1024]{3,2,1,0:T(8,128)(2,1)S(1)}, bf16[2,33,34,1024]{3,2,1,0:T(8,128)(2,1)S(1)}) fusion(bf16[2,1,34,1024]{3,2,1,0:T(8,128)(2,1)S(1)} %collective-permute-done.6, bf16[2,32,1,1024]{3,2,1,0:T(2,128)(2,1)S(1)} %broadcast_select_fusion, bf16[2,32,32,1024]{3,2,1,0:T(8,128)(2,1)S(1)} %copy-done.6, ...), kind=kLoop, calls=%fused_computation.63 | loop fusion | flops 36765696 | bytes 13926400 | tf_op jit(solution)/shard_map/concatenate | solution.py:125
  370.6 13.3 %fusion.45 = bf16[2,1,32,32,1024]{4,3,2,1,0:T(8,128)(2,1)} fusion(bf16[2,33,34,1024]{3,2,1,0:T(8,128)(2,1)S(1)} %get-tuple-element.62, f32[1024]{0:T(1024)S(1)} %bitcast.198, f32[1024]{0:T(1024)S(1)} %bitcast.200, f32[1024]{0:T(1024)S(1)} %bitcast.186, bf16[2,32,32,1024]{3,2,1,0:T(8,128)(2,1)S(1)} %copy-done.6, ...), kind=kLoop, calls=%fused_computation.73 | loop fusion | flops 69206016 | bytes 33853440
  383.9 119.5 %all-reduce.4.cloned.1.call-done = (f32[1024,256]{1,0:T(8,128)}, f32[256,768]{1,0:T(8,128)}, f32[256,256]{1,0:T(8,128)}) async-done(((f32[1024,256]{1,0:T(8,128)}, f32[256,768]{1,0:T(8,128)}, f32[256,256]{1,0:T(8,128)}), (f32[1024,256]{1,0:T(8,128)}, f32[256,768]{1,0:T(8,128)}, f32[256,256]{1,0:T(8,128)})) %all-reduce.4.cloned.1.call-update) | async-done | bytes 2097168 | tf_op jit(solution)/shard_map/psum | solution.py:209
  503.4 2.3 broadcast_multiply_fusion
  505.7 2.1 broadcast_multiply_fusion.1
  507.7 1.7 broadcast_multiply_fusion.2
  (70 shorter events, 8.1 us)
Async XLA Ops:
  7.2 65.8 %copy-start = (bf16[1024,256]{1,0:T(8,128)(2,1)S(1)}, bf16[1024,256]{1,0:T(8,128)(2,1)}, u32[]{:S(2)}) copy-start(bf16[1024,256]{1,0:T(8,128)(2,1)} %param.12) | copy-start | bytes 1572868
  7.2 29.1 %copy-start.20 = (f32[3,3,1024]{2,1,0:T(4,128)S(1)}, f32[3,3,1024]{2,1,0:T(4,128)}, u32[]{:S(2)}) copy-start(f32[3,3,1024]{2,1,0:T(4,128)} %param.11) | copy-start | bytes 110596
  9.3 20.4 %collective-permute-start = (bf16[2,32,1,1024]{3,2,1,0:T(2,128)(2,1)S(1)}, bf16[2,32,1,1024]{3,2,1,0:T(2,128)(2,1)S(1)}, u32[]{:S(2)}, u32[]{:S(2)}) collective-permute-start(bf16[2,32,1,1024]{3,2,1,0:T(2,128)(2,1)S(1)} %get-tuple-element.71), channel_id=1, source_target_pairs={{0,1},{1,2},{2,3},{3,4},{4,5},{5,6},{6,7},{7,8},{8,9},{9,10},{10,1... | collective-permute-start | bytes 393224 | tf_op jit(solution)/shard_map/ppermute | solution.py:15
  13.8 16.2 %collective-permute-start.1 = (bf16[2,32,1,1024]{3,2,1,0:T(2,128)(2,1)S(1)}, bf16[2,32,1,1024]{3,2,1,0:T(2,128)(2,1)S(1)}, u32[]{:S(2)}, u32[]{:S(2)}) collective-permute-start(bf16[2,32,1,1024]{3,2,1,0:T(2,128)(2,1)S(1)} %get-tuple-element.72), channel_id=1, source_target_pairs={{1,0},{2,1},{3,2},{4,3},{5,4},{6,5},{7,6},{8,7},{9,8},{10,9},{11,1... | collective-permute-start | bytes 393224 | tf_op jit(solution)/shard_map/ppermute | solution.py:15
  18.1 57.3 %all-to-all-start = ((bf16[64,1,2,1,16,256]{5,4,2,3,1,0:T(8,128)(2,1)}), bf16[64,1,2,1,16,256]{5,4,2,3,1,0:T(8,128)(2,1)S(1)}, u32[]{:S(2)}, u32[]{:S(2)}) async-start(bf16[64,1,2,1,16,256]{5,4,2,3,1,0:T(8,128)(2,1)} %copy.75), calls=%async_computation | async-start | bytes 2097152 | tf_op jit(solution)/shard_map/all_to_all | solution.py:185
  29.7 18.6 %copy-start.4 = (bf16[2,1,32,32,1024]{4,3,2,1,0:T(8,128)(2,1)S(1)}, bf16[2,1,32,32,1024]{4,3,2,1,0:T(8,128)(2,1)}, u32[]{:S(2)}) copy-start(bf16[2,1,32,32,1024]{4,3,2,1,0:T(8,128)(2,1)} %param.8) | copy-start | bytes 12582916
  31.7 14.2 %collective-permute-start.2 = (bf16[2,1,34,1024]{3,2,1,0:T(8,128)(2,1)S(1)}, bf16[2,1,34,1024]{3,2,1,0:T(8,128)(2,1)S(1)}, u32[]{:S(2)}, u32[]{:S(2)}) collective-permute-start(bf16[2,1,34,1024]{3,2,1,0:T(8,128)(2,1)S(1)} %get-tuple-element.67), channel_id=1, source_target_pairs={{0,8},{1,9},{2,10},{3,11},{4,12},{5,13},{6,14},{7,15},{8,16},{9,17... | collective-permute-start | bytes 417800 | tf_op jit(solution)/shard_map/ppermute | solution.py:15
  35.0 13.2 %collective-permute-start.3 = (bf16[2,1,34,1024]{3,2,1,0:T(8,128)(2,1)S(1)}, bf16[2,1,34,1024]{3,2,1,0:T(8,128)(2,1)S(1)}, u32[]{:S(2)}, u32[]{:S(2)}) collective-permute-start(bf16[2,1,34,1024]{3,2,1,0:T(8,128)(2,1)S(1)} %get-tuple-element.68), channel_id=1, source_target_pairs={{8,0},{9,1},{10,2},{11,3},{12,4},{13,5},{14,6},{15,7},{16,8},{17,9... | collective-permute-start | bytes 417800 | tf_op jit(solution)/shard_map/ppermute | solution.py:15
  55.0 16.0 %copy-start.1 = (bf16[2,33,34,1024]{3,2,1,0:T(8,128)(2,1)}, bf16[2,33,34,1024]{3,2,1,0:T(8,128)(2,1)S(1)}, u32[]{:S(2)}) copy-start(bf16[2,33,34,1024]{3,2,1,0:T(8,128)(2,1)S(1)} %get-tuple-element.65) | copy-start | bytes 13787140
  55.0 15.9 %copy-start.2 = (bf16[2,33,34,1024]{3,2,1,0:T(8,128)(2,1)}, bf16[2,33,34,1024]{3,2,1,0:T(8,128)(2,1)S(1)}, u32[]{:S(2)}) copy-start(bf16[2,33,34,1024]{3,2,1,0:T(8,128)(2,1)S(1)} %get-tuple-element.66) | copy-start | bytes 13787140
  55.0 17.9 %copy-start.22 = (bf16[2,1,32,32,256]{4,3,2,1,0:T(8,128)(2,1)S(1)}, bf16[2,1,32,32,256]{4,3,2,1,0:T(8,128)(2,1)}, u32[]{:S(2)}) copy-start(bf16[2,1,32,32,256]{4,3,2,1,0:T(8,128)(2,1)} %param.9) | copy-start | bytes 3145732
  71.0 2.0 copy-start.16
  71.0 14.8 %copy-start.19 = (bf16[256,256]{1,0:T(8,128)(2,1)S(1)}, bf16[256,256]{1,0:T(8,128)(2,1)}, u32[]{:S(2)}) copy-start(bf16[256,256]{1,0:T(8,128)(2,1)} %param.15) | copy-start | bytes 393220
  75.3 27.5 %all-to-all-start.1 = ((bf16[64,1,2,1,16,256]{5,4,2,3,1,0:T(8,128)(2,1)}), bf16[64,1,2,1,16,256]{5,4,2,3,1,0:T(8,128)(2,1)S(1)}, u32[]{:S(2)}, u32[]{:S(2)}) async-start(bf16[64,1,2,1,16,256]{5,4,2,3,1,0:T(8,128)(2,1)} %bitcast.175), calls=%async_computation.1 | async-start | bytes 2097152 | tf_op jit(solution)/shard_map/all_to_all | solution.py:184
  84.7 1.0 copy-start.9
  84.8 23.4 %copy-start.21 = (f32[256]{0:T(256)S(1)}, f32[256]{0:T(256)}, u32[]{:S(2)}) copy-start(f32[256]{0:T(256)} %param.13) | copy-start | bytes 3076
  102.8 1.0 copy-start.11
  104.1 2.6 copy-start.7
  130.8 1.3 copy-start.14
  130.8 2.0 copy-start.15
  130.8 9.6 %copy-start.13 = (bf16[32,64,1,8,32]{1,0,4,3,2:T(8,128)(2,1)}, bf16[32,64,1,8,32]{1,0,4,3,2:T(8,128)(2,1)S(1)}, u32[]{:S(2)}) copy-start(bf16[32,64,1,8,32]{1,0,4,3,2:T(8,128)(2,1)S(1)} %get-tuple-element.58) | copy-start | bytes 3145732
  135.6 4.9 copy-start.12
  191.4 5.7 %copy-start.3 = (bf16[32,64,3,8,32]{1,4,3,0,2:T(8,128)(2,1)}, bf16[32,64,3,8,32]{1,4,3,0,2:T(8,128)(2,1)S(1)}, u32[]{:S(2)}) copy-start(bf16[32,64,3,8,32]{1,4,3,0,2:T(8,128)(2,1)S(1)} %maximum_convert_fusion) | copy-start | bytes 9437188
  193.5 3.7 copy-start.10
  199.6 46.3 %all-to-all-start.2 = ((bf16[64,1,2,1,16,256]{5,4,2,3,1,0:T(8,128)(2,1)}), bf16[64,1,2,1,16,256]{5,4,2,3,1,0:T(8,128)(2,1)}, u32[]{:S(2)}, u32[]{:S(2)}) async-start(bf16[64,1,2,1,16,256]{5,4,2,3,1,0:T(8,128)(2,1)} %bitcast.42), calls=%async_computation.2 | async-start | bytes 2097152 | tf_op jit(solution)/shard_map/all_to_all | solution.py:196
  204.8 298.6 %all-reduce.4.cloned.1.call-start = ((), (), s32[]{:S(2)}) async-start(), calls=%async_computation.3 | async-start | bytes 4194304 | tf_op jit(solution)/shard_map/psum | solution.py:209
  223.8 17.0 %copy-start.8 = (f32[8,8,2,1,16,256]{5,4,2,1,0,3:T(8,128)S(1)}, f32[8,8,2,1,16,256]{5,4,2,1,0,3:T(8,128)}, u32[]{:S(2)}) copy-start(f32[8,8,2,1,16,256]{5,4,2,1,0,3:T(8,128)} %copy-done.7) | copy-start | bytes 6291460
  247.2 34.1 %copy-start.18 = (bf16[64,1,2,1,16,256]{5,4,0,2,3,1:T(8,128)(2,1)}, bf16[64,1,2,1,16,256]{5,4,0,2,3,1:T(8,128)(2,1)S(1)}, u32[]{:S(2)}) copy-start(bf16[64,1,2,1,16,256]{5,4,0,2,3,1:T(8,128)(2,1)S(1)} %copy.95) | copy-start | bytes 3145732
  247.2 34.1 %copy-start.17 = (bf16[2,32,32,1024]{3,2,1,0:T(8,128)(2,1)S(1)}, bf16[2,32,32,1024]{3,2,1,0:T(8,128)(2,1)}, u32[]{:S(2)}) copy-start(bf16[2,32,32,1024]{3,2,1,0:T(8,128)(2,1)} %copy-done.16) | copy-start | bytes 12582916
  273.3 2.0 copy-start.5
  275.8 77.9 %collective-permute-start.4 = (bf16[2,32,1,1024]{3,2,1,0:T(2,128)(2,1)S(1)}, bf16[2,32,1,1024]{3,2,1,0:T(2,128)(2,1)S(1)}, u32[]{:S(2)}, u32[]{:S(2)}) collective-permute-start(bf16[2,32,1,1024]{3,2,1,0:T(2,128)(2,1)S(1)} %get-tuple-element.69), channel_id=1, source_target_pairs={{0,1},{1,2},{2,3},{3,4},{4,5},{5,6},{6,7},{7,8},{8,9},{9,10},{10,1... | collective-permute-start | bytes 393224 | tf_op jit(solution)/shard_map/ppermute | solution.py:15
  279.3 74.6 %collective-permute-start.5 = (bf16[2,32,1,1024]{3,2,1,0:T(2,128)(2,1)S(1)}, bf16[2,32,1,1024]{3,2,1,0:T(2,128)(2,1)S(1)}, u32[]{:S(2)}, u32[]{:S(2)}) collective-permute-start(bf16[2,32,1,1024]{3,2,1,0:T(2,128)(2,1)S(1)} %get-tuple-element.70), channel_id=1, source_target_pairs={{1,0},{2,1},{3,2},{4,3},{5,4},{6,5},{7,6},{8,7},{9,8},{10,9},{11,1... | collective-permute-start | bytes 393224 | tf_op jit(solution)/shard_map/ppermute | solution.py:15
  353.0 10.8 %copy-start.6 = (bf16[2,32,32,1024]{3,2,1,0:T(8,128)(2,1)S(1)}, bf16[2,32,32,1024]{3,2,1,0:T(8,128)(2,1)}, u32[]{:S(2)}) copy-start(bf16[2,32,32,1024]{3,2,1,0:T(8,128)(2,1)} %copy-done.5) | copy-start | bytes 12582916
  355.4 7.6 %collective-permute-start.6 = (bf16[2,1,34,1024]{3,2,1,0:T(8,128)(2,1)S(1)}, bf16[2,1,34,1024]{3,2,1,0:T(8,128)(2,1)S(1)}, u32[]{:S(2)}, u32[]{:S(2)}) collective-permute-start(bf16[2,1,34,1024]{3,2,1,0:T(8,128)(2,1)S(1)} %get-tuple-element.63), channel_id=1, source_target_pairs={{8,0},{9,1},{10,2},{11,3},{12,4},{13,5},{14,6},{15,7},{16,8},{17,9... | collective-permute-start | bytes 417800 | tf_op jit(solution)/shard_map/ppermute | solution.py:15
  356.7 7.1 %collective-permute-start.7 = (bf16[2,1,34,1024]{3,2,1,0:T(8,128)(2,1)S(1)}, bf16[2,1,34,1024]{3,2,1,0:T(8,128)(2,1)S(1)}, u32[]{:S(2)}, u32[]{:S(2)}) collective-permute-start(bf16[2,1,34,1024]{3,2,1,0:T(8,128)(2,1)S(1)} %get-tuple-element.64), channel_id=1, source_target_pairs={{0,8},{1,9},{2,10},{3,11},{4,12},{5,13},{6,14},{7,15},{8,16},{9,17... | collective-permute-start | bytes 417800 | tf_op jit(solution)/shard_map/ppermute | solution.py:15
Sparse Core Ops, SparseCore 0:
  353.1 150.2 all-reduce.3
where the time goes:
time: 525 us; the launch traced here: 517 us
  waiting for transfers between devices  145 us (28%)
  matrix products  101 us (19%)
  local copies, waits for them, and re-layouts  72.2 us (14%)
  blocking collectives  69.4 us (13%)
  other arithmetic  66.8 us (13%)
  starting transfers between devices  47.6 us (9%)
  between operations  15.1 us (3%)
    psum x1, waiting for transfers between devices, on_device(): lax.psum((grad_kernel, grad_proj, grad_wqkv, grad_out, grad_gain), ('dp',...  119 us
    psum x1, blocking collectives, on_device(): lax.psum((grad_kernel, grad_proj, grad_wqkv, grad_out, grad_gain), ('dp',...  69.4 us
    dot_general x6, matrix products, contract(): jnp.einsum(pattern, left_op, right_op, preferred_element_type=jnp.float32)  55.9 us
    dot_general x1, matrix products, on_device(): grad_act = jnp.dot(flat_grad, w_proj.T, preferred_element_type=jnp.float32)  26.1 us
    ppermute x8, starting transfers between devices, passed_along(): return lax.ppermute(block, axis, route)  21.8 us
    convert_element_type x3, local copies, waits for them, and re-layouts, attend_back(): jnp.stack([grad_query, grad_keys, grad_values], axis=2).astype(jnp.bfloat16)  21.3 us
    convert_element_type x1, other arithmetic, on_device(): activated = smooth(pre_act).astype(jnp.bfloat16)  15.9 us
    ppermute x8, waiting for transfers between devices, passed_along(): return lax.ppermute(block, axis, route)  14.4 us
  transfers between devices with their start and end apart: 12, of which 6 were waited for; matrix products, arithmetic and copies ran while one was open for 20% of the time, Pallas kernels for 0%

commit v1 on v0

--- a/solution.py
+++ b/solution.py
@@ -2,11 +2,468 @@
 
 import jax
 import jax.numpy as jnp
+import numpy as np
 from jax import lax
+from jax.experimental import pallas as pl
+from jax.experimental.pallas import tpu as pltpu
 from jax.sharding import PartitionSpec as P
 
+GRID = 8
+TILES = 64
+ROWS = 32
+COLS = 32
+LANES = 128
+WIDTH = 256
+EXPAND = 1024
+LANE_BLOCKS = EXPAND // LANES
+BAND = 4
+BANDS = ROWS // BAND
+BAND_CELLS = BAND * COLS
+BAND_TILES = TILES // BANDS
+F32 = jnp.float32
+BF16 = jnp.bfloat16
+MESH_ID = pl.DeviceIdType.MESH
+GELU_1 = math.sqrt(2.0 / math.pi)
+GELU_3 = GELU_1 * 0.044715
+
+
+def dot(a, b):
+    return lax.dot_general(a, b, (((1,), (0,)), ((), ())), preferred_element_type=F32)
+
+
+def dot_t(a, b):
+    return lax.dot_general(a, b, (((1,), (1,)), ((), ())), preferred_element_type=F32)
+
+
+def dot_tl(a, b):
+    return lax.dot_general(a, b, (((0,), (0,)), ((), ())), preferred_element_type=F32)
+
+
+def tile_id(tile):
+    return {"row": tile // 32, "col": lax.rem(tile, 32)}
+
+
+def my_tile():
+    return lax.axis_index("row") * 32 + lax.axis_index("col")
+
+
+def neighbours(me):
+    tile_row, tile_col = me // GRID, lax.rem(me, GRID)
+    found = {}
+    for down in (-1, 0, 1):
+        for right in (-1, 0, 1):
+            if (down, right) != (0, 0):
+                found[down, right] = lax.rem(tile_row + down + GRID, GRID) * GRID + lax.rem(
+                    tile_col + right + GRID, GRID
+                )
+    return found
+
+
+SIDES = ((0, -1), (0, 1))
+ENDS = ((-1, 0), (1, 0))
+CORNERS = ((-1, -1), (-1, 1), (1, -1), (1, 1))
+AROUND = SIDES + ENDS + CORNERS
+
+
+def rim_copies(me, grid_ref, sides_out, sides_in, corners_out, corners_in, send_sem, recv_sem):
+    around = neighbours(me)
+    copies = []
+    for n, (down, right) in enumerate(AROUND):
+        if down == 0:
+            source = sides_out.at[(right + 1) // 2]
+            target = sides_in.at[(1 - right) // 2]
+        elif right == 0:
+            source = grid_ref.at[:, 1 if down < 0 else ROWS]
+            target = grid_ref.at[:, ROWS + 1 if down < 0 else 0]
+        else:
+            place = CORNERS.index((down, right))
+            source = corners_out.at[place]
+            target = corners_in.at[3 - place]
+        copies.append(
+            pltpu.make_async_remote_copy(
+                src_ref=source,
+                dst_ref=target,
+                send_sem=send_sem.at[n],
+                recv_sem=recv_sem.at[n],
+                device_id=tile_id(around[down, right]),
+                device_id_type=MESH_ID,
+            )
+        )
+    return copies
+
+
+def collect_sides(grid_ref, sides_out, corners_out):
+    for side in range(2):
+        for picture in range(2):
+            for start in range(0, ROWS, 16):
+                window = grid_ref[picture, 1 + start : 17 + start, 16 * side : 16 * side + 16, :]
+                column = window.astype(F32)[:, 15 * side, :]
+                sides_out[side, picture, start : start + 16, :] = column.astype(BF16)
+    for place, (down, right) in enumerate(CORNERS):
+        edge = 0 if down < 0 else 16
+        row = 0 if down < 0 else 15
+        both = [
+            sides_out[(right + 1) // 2, picture, edge : edge + 16, :].astype(F32)[row : row + 1]
+            for picture in range(2)
+        ]
+        filler = jnp.zeros((14, EXPAND), F32)
+        corners_out[place] = jnp.concatenate(both + [filler], axis=0).astype(BF16)
+
+
+def clear_outside(me, grid_ref, sides_in, corners_in):
+    tile_row, tile_col = me // GRID, lax.rem(me, GRID)
+    for side, last in ((0, 0), (1, GRID - 1)):
+
+        @pl.when(tile_col == last)
+        def _():
+            sides_in[side] = jnp.zeros(sides_in.shape[1:], BF16)
+            corners_in[side] = jnp.zeros(corners_in.shape[1:], BF16)
+            corners_in[2 + side] = jnp.zeros(corners_in.shape[1:], BF16)
+
+    for end, last in ((0, 0), (1, GRID - 1)):
+
+        @pl.when(tile_row == last)
+        def _():
+            grid_ref[:, (ROWS + 1) * end] = jnp.zeros((2, COLS, EXPAND), BF16)
+            corners_in[2 * end] = jnp.zeros(corners_in.shape[1:], BF16)
+            corners_in[2 * end + 1] = jnp.zeros(corners_in.shape[1:], BF16)
+
+
+def column_stack(sides_in, corners_in, columns):
+    for side in range(2):
+        for picture in range(2):
+            columns[side, picture, 0:8] = jnp.concatenate(
+                [jnp.zeros((7, EXPAND), F32), corners_in[side].astype(F32)[picture : picture + 1]], axis=0
+            )
+            columns[side, picture, 8 : 8 + ROWS] = sides_in[side, picture].astype(F32)
+            columns[side, picture, 40:48] = jnp.concatenate(
+                [corners_in[2 + side].astype(F32)[picture : picture + 1], jnp.zeros((7, EXPAND), F32)], axis=0
+            )
+
+
+def column_terms(columns, weights, col_offs, terms):
+    for side in range(2):
+        for picture in range(2):
+            total = None
+            for row_off in range(3):
+                term = (
+                    weights(row_off, col_offs[side])
+                    * columns[side, picture, 7 + row_off : 7 + row_off + ROWS, :]
+                )
+                total = term if total is None else total + term
+            for band in range(BANDS):
+                terms[side, picture, band, 0:BAND] = total[BAND * band : BAND * band + BAND]
+
+
+def convolve(rows, weights, left, right):
+    spot = lax.broadcasted_iota(jnp.int32, (BAND, COLS, LANES), 1)
+    parts = []
+    for col_off in range(3):
+        total = None
+        for row_off in range(3):
+            term = weights[3 * row_off + col_off][None, :, :] * rows[row_off : row_off + BAND]
+            total = term if total is None else total + term
+        parts.append(total)
+    from_left = jnp.where(spot == 0, left[:, None, :], pltpu.roll(parts[0], 1, 1))
+    from_right = jnp.where(spot == COLS - 1, right[:, None, :], pltpu.roll(parts[2], COLS - 1, 1))
+    return parts[1] + from_left + from_right
+
+
+def forward_kernel(
+    x_hbm, skip_ref, cot_hbm, kern_ref, wproj_ref,
+    act_hbm, dg_hbm, got_mix, got_cot, ends_out, columns_out,
+    grid, sides_out, sides_in, corners_out, corners_in, columns, terms, act, dg, mix,
+    load_sem, rim_send, rim_recv, cot_send, cot_recv, mix_send, mix_recv, own_sem, store_sem,
+):
+    me = my_tile()
+    load = pltpu.make_async_copy(x_hbm, grid.at[:, pl.ds(1, ROWS)], load_sem)
+    load.start()
+    barrier = pltpu.get_barrier_semaphore()
+
+    def greet(i, carry):
+        pl.semaphore_signal(
+            barrier, inc=1, device_id=tile_id(lax.rem(me + i, TILES)), device_id_type=MESH_ID
+        )
+        return carry
+
+    lax.fori_loop(1, TILES, greet, 0)
+    load.wait()
+    collect_sides(grid, sides_out, corners_out)
+    pl.semaphore_wait(barrier, TILES - 1)
+    rim = rim_copies(me, grid, sides_out, sides_in, corners_out, corners_in, rim_send, rim_recv)
+    for copy in rim:
+        copy.start()
+
+    def cot_copy(target, slot):
+        return pltpu.make_async_remote_copy(
+            src_ref=cot_hbm.at[:, pl.ds(pl.multiple_of(target * 16, 16), 16), :],
+            dst_ref=got_cot.at[:, pl.ds(pl.multiple_of(slot * 16, 16), 16), :],
+            send_sem=cot_send.at[target],
+            recv_sem=cot_recv.at[slot],
+            device_id=tile_id(target),
+            device_id_type=MESH_ID,
+        )
+
+    def mix_copy(target, slot):
+        return pltpu.make_async_remote_copy(
+            src_ref=mix.at[:, pl.ds(pl.multiple_of(target * 16, 16), 16), :],
+            dst_ref=got_mix.at[:, pl.ds(pl.multiple_of(slot * 16, 16), 16), :],
+            send_sem=mix_send.at[target],
+            recv_sem=mix_recv.at[slot],
+            device_id=tile_id(target),
+            device_id_type=MESH_ID,
+        )
+
+    def send_cot(i, carry):
+        cot_copy(lax.rem(me + i, TILES), me).start()
+        return carry
+
+    lax.fori_loop(1, TILES, send_cot, 0)
+    own = pl.ds(pl.multiple_of(me * 16, 16), 16)
+    own_cot = pltpu.make_async_copy(cot_hbm.at[:, own, :], got_cot.at[:, own, :], own_sem.at[0])
+    own_cot.start()
+    for copy in rim:
+        copy.wait_recv()
+    for copy in rim:
+        copy.wait_send()
+    clear_outside(me, grid, sides_in, corners_in)
+    column_stack(sides_in, corners_in, columns)
+    column_terms(
+        columns, lambda a, c: kern_ref[3 * a + c : 3 * a + c + 1, :], (0, 2), terms
+    )
+    ends = pltpu.make_async_copy(grid.at[:, 0], ends_out.at[0], own_sem.at[1])
+    ends.start()
+    ends_low = pltpu.make_async_copy(grid.at[:, ROWS + 1], ends_out.at[1], own_sem.at[2])
+    ends_low.start()
+    cols = pltpu.make_async_copy(columns, columns_out, own_sem.at[3])
+    cols.start()
+
+    def band_copies(band):
+        cells = pl.ds(pl.multiple_of(band * BAND_CELLS, BAND_CELLS), BAND_CELLS)
+        return (
+            pltpu.make_async_copy(act.at[:, cells, :], act_hbm.at[:, cells, :], store_sem.at[0, band]),
+            pltpu.make_async_copy(dg.at[:, cells, :], dg_hbm.at[:, cells, :], store_sem.at[1, band]),
+        )
+
+    def do_band(step, carry):
+        band = lax.rem(step + me // GRID, BANDS)
+        first = band * BAND
+        cells = pl.ds(pl.multiple_of(band * BAND_CELLS, BAND_CELLS), BAND_CELLS)
+
+        def do_block(index, inner):
+            picture, block = index // LANE_BLOCKS, lax.rem(index, LANE_BLOCKS)
+            lanes = pl.ds(pl.multiple_of(block * LANES, LANES), LANES)
+            rows = grid[picture, pl.ds(first, BAND + 2), :, lanes].astype(F32)
+            weights = [kern_ref[n : n + 1, lanes] for n in range(9)]
+            pre = convolve(
+                rows,
+                weights,
+                terms[0, picture, band, 0:BAND, lanes],
+                terms[1, picture, band, 0:BAND, lanes],
+            )
+            square = pre * pre
+            tanh = jnp.tanh(pre * (GELU_1 + GELU_3 * square))
+            half = 0.5 * pre
+            activated = half + half * tanh
+            slope = (0.5 + 0.5 * tanh) + half * (1.0 - tanh * tanh) * (GELU_1 + (3.0 * GELU_3) * square)
+            act[picture, cells, lanes] = activated.astype(BF16).reshape(BAND_CELLS, LANES)
+            dg[picture, cells, lanes] = slope.astype(BF16).reshape(BAND_CELLS, LANES)
+            return inner
+
+        lax.fori_loop(0, 2 * LANE_BLOCKS, do_block, 0)
+        flat = act[:, cells, :].reshape(2 * BAND_CELLS, EXPAND)
+        projected = dot(flat, wproj_ref[...]).reshape(2, BAND_CELLS, WIDTH)
+        mix[:, cells, :] = (skip_ref[:, cells, :].astype(F32) + projected).astype(BF16)
+
+        def send_mix(i, inner):
+            target = band * BAND_TILES + i
+
+            @pl.when(target != me)
+            def _():
+                mix_copy(target, me).start()
+
+            @pl.when(target == me)
+            def _():
+                pltpu.make_async_copy(mix.at[:, own, :], got_mix.at[:, own, :], own_sem.at[4]).start()
+
+            return inner
+
+        lax.fori_loop(0, BAND_TILES, send_mix, 0)
+        for copy in band_copies(band):
+            copy.start()
+        return carry
+
+    lax.fori_loop(0, BANDS, do_band, 0)
+    for band in range(BANDS):
+        for copy in band_copies(band):
+            copy.wait()
+    own_cot.wait()
+    ends.wait()
+    ends_low.wait()
+    cols.wait()
+    pltpu.make_async_copy(mix.at[:, own, :], got_mix.at[:, own, :], own_sem.at[4]).wait()
+
+    def finish(i, carry):
+        peer = lax.rem(me + i, TILES)
+        cot_copy(peer, peer).wait_recv()
+        mix_copy(peer, peer).wait_recv()
+        cot_copy(peer, peer).wait_send()
+        mix_copy(peer, peer).wait_send()
+        return carry
+
+    lax.fori_loop(1, TILES, finish, 0)
+
+
+def forward(x, skip, cot, kern, wproj):
+    vmem = pl.BlockSpec(memory_space=pltpu.VMEM)
+    anywhere = pl.BlockSpec(memory_space=pl.ANY)
+    cells = ROWS * COLS
+    dma = pltpu.SemaphoreType.DMA
+    return pl.pallas_call(
+        forward_kernel,
+        out_shape=(
+            jax.ShapeDtypeStruct((2, cells, EXPAND), BF16),
+            jax.ShapeDtypeStruct((2, cells, EXPAND), BF16),
+            jax.ShapeDtypeStruct((2, cells, WIDTH), BF16),
+            jax.ShapeDtypeStruct((2, cells, WIDTH), BF16),
+            jax.ShapeDtypeStruct((2, 2, COLS, EXPAND), BF16),
+            jax.ShapeDtypeStruct((2, 2, 48, EXPAND), F32),
+        ),
+        in_specs=[anywhere, vmem, anywhere, vmem, vmem],
+        out_specs=(anywhere,) * 6,
+        scratch_shapes=[
+            pltpu.VMEM((2, ROWS + 2, COLS, EXPAND), BF16),
+            pltpu.VMEM((2, 2, ROWS, EXPAND), BF16),
+            pltpu.VMEM((2, 2, ROWS, EXPAND), BF16),
+            pltpu.VMEM((4, 16, EXPAND), BF16),
+            pltpu.VMEM((4, 16, EXPAND), BF16),
+            pltpu.VMEM((2, 2, 48, EXPAND), F32),
+            pltpu.VMEM((2, 2, BANDS, 8, EXPAND), F32),
+            pltpu.VMEM((2, cells, EXPAND), BF16),
+            pltpu.VMEM((2, cells, EXPAND), BF16),
+            pltpu.VMEM((2, cells, WIDTH), BF16),
+            dma,
+            dma((8,)),
+            dma((8,)),
+            dma((TILES,)),
+            dma((TILES,)),
+            dma((TILES,)),
+            dma((TILES,)),
+            dma((5,)),
+            dma((2, BANDS)),
+        ],
+        compiler_params=pltpu.CompilerParams(
+            collective_id=0, has_side_effects=True, vmem_limit_bytes=56 * 2**20
+        ),
+        name="forward",
+    )(x, skip, cot, kern, wproj)
+
+
+def attention_kernel(
+    mix_ref, cot_ref, gain_ref, wqkv_ref, wout_ref, perm_ref, mask_ref,
+    back_ref, gw_ref, go_ref, gg_ref, mix_s, cot_s,
+):
+    scale = 1.0 / math.sqrt(32.0)
+    perm = perm_ref[...]
+    for s in range(8):
+        for src, dst in ((mix_ref, mix_s), (cot_ref, cot_s)):
+            rows = src[:, 128 * s : 128 * s + 128, :].reshape(256, 256)
+            dst[:, 8 * s : 8 * s + 8, :] = dot(perm, rows).reshape(32, 8, 256)
+    gw_ref[...] = jnp.zeros_like(gw_ref)
+    go_ref[...] = jnp.zeros_like(go_ref)
+    gg_ref[...] = jnp.zeros_like(gg_ref)
+    gain = gain_ref[...]
+    lane = lax.broadcasted_iota(jnp.int32, (64, 128), 1) // 32
+
+    def pick(full):
+        halves = []
+        for half in range(2):
+            cols = slice(128 * half, 128 * half + 128)
+            acc = full[64 * (4 * half) : 64 * (4 * half) + 64, cols]
+            for h in range(1, 4):
+                hh = 4 * half + h
+                acc = jnp.where(lane == h, full[64 * hh : 64 * hh + 64, cols], acc)
+            halves.append(acc)
+        return jnp.concatenate(halves, axis=1)
+
+    def block(b, carry):
+        g0 = b * 4
+        mix = mix_s[pl.ds(g0, 4)].reshape(256, 256)
+        cot_f = cot_s[pl.ds(g0, 4)].reshape(256, 256)
+        cot = cot_f.astype(BF16)
+        inv = lax.rsqrt(jnp.mean(mix * mix, axis=-1, keepdims=True) + 1e-6)
+        normed = (mix * inv * gain).astype(BF16)
+        qkv = dot(normed, wqkv_ref[...]).astype(BF16)
+        gatt = dot_t(cot, wout_ref[...]).astype(BF16)
+        att, gqs, gks, gvs = [], [], [], []
+        for i in range(4):
+            r = slice(64 * i, 64 * i + 64)
+            q, k, v = qkv[r, 0:256], qkv[r, 256:512], qkv[r, 512:768]
+            do = gatt[r]
+            qexp = jnp.concatenate([q] * 8, axis=0) * mask_ref[...]
+            doexp = jnp.concatenate([do] * 8, axis=0) * mask_ref[...]
+            st = dot_t(k, qexp) * scale
+            e = jnp.exp(st - jnp.max(st, axis=0, keepdims=True))
+            p = e * (1.0 / jnp.sum(e, axis=0, keepdims=True))
+            pb = p.astype(BF16)
+            dp = dot_t(v, doexp)
+            dsum = jnp.sum(dp * p, axis=0, keepdims=True)
+            ds = (p * (dp - dsum) * scale).astype(BF16)
+            att.append(pick(dot_tl(pb, v)).astype(BF16))
+            gqs.append(pick(dot_tl(ds, k)).astype(BF16))
+            gks.append(dot(ds, qexp).astype(BF16))
+            gvs.append(dot(pb, doexp).astype(BF16))
+        attended = jnp.concatenate(att, axis=0)
+        gqkv = [jnp.concatenate(x, axis=0) for x in (gqs, gks, gvs)]
+        go_ref[...] += dot_tl(attended, cot)
+        gn = jnp.zeros((256, 256), F32)
+        normed_t = normed.T
+        for j in range(3):
+            gw_ref[256 * j : 256 * j + 256] += dot(normed_t, gqkv[j])
+            gn = gn + dot_t(gqkv[j], wqkv_ref[:, 256 * j : 256 * j + 256])
+        mi = mix * inv
+        gg_ref[...] += jnp.sum(gn * mi, axis=0, keepdims=True)
+        scaled = gn * gain
+        mean = jnp.mean(scaled * mix, axis=-1, keepdims=True)
+        out = cot_f + inv * scaled - mi * (inv * inv * mean)
+        cot_s[pl.ds(g0, 4)] = out.reshape(4, 64, 256)
+        return carry
+
+    lax.fori_loop(0, 8, block, 0)
+    for s in range(8):
+        rows = cot_s[:, 8 * s : 8 * s + 8, :].reshape(256, 256).astype(BF16)
+        back_ref[:, 128 * s : 128 * s + 128, :] = dot_tl(perm, rows).astype(BF16).reshape(2, 128, 256)
+
+
+def consts():
+    perm = np.zeros((256, 256), np.float32)
+    for g in range(32):
+        for s in range(8):
+            perm[g * 8 + s, (g // 16) * 128 + s * 16 + g % 16] = 1
+    mask = np.kron(np.eye(8), np.ones((64, 32))).astype(np.float32)
+    return jnp.asarray(perm, BF16), jnp.asarray(mask, BF16)
+
+
+def attention(got_mix, got_cot, gain, wqkv, wout):
+    perm, mask = consts()
+    v = pl.BlockSpec(memory_space=pltpu.VMEM)
+    return pl.pallas_call(
+        attention_kernel,
+        out_shape=(
+            jax.ShapeDtypeStruct((2, 1024, 256), BF16),
+            jax.ShapeDtypeStruct((768, 256), F32),
+            jax.ShapeDtypeStruct((256, 256), F32),
+            jax.ShapeDtypeStruct((1, 256), F32),
+        ),
+        in_specs=[v] * 7,
+        out_specs=(v,) * 4,
+        scratch_shapes=[pltpu.VMEM((32, 64, 256), F32), pltpu.VMEM((32, 64, 256), F32)],
+        compiler_params=pltpu.CompilerParams(vmem_limit_bytes=48 * 2**20),
+        name="attention",
+    )(got_mix, got_cot, gain.reshape(1, 256), wqkv, wout, perm, mask)
+
+
 HEADS = 8
-GRID = 8
 
 
 def passed_along(block, axis, distance):
@@ -170,37 +627,27 @@
     group_part = span_a * cols_here // n_tiles
     token_count = pictures * lax.axis_size("dp") * rows_here * cols_here * n_tiles
     factor = 1.0 / math.sqrt(token_count)
-    padded = pad_tile(expanded, 1)
-    pre_act = depthwise(padded, depth_kernel, rows_here, cols_here)
-    activated = smooth(pre_act).astype(jnp.bfloat16)
-    flat_act = activated.reshape(-1, expand_dim)
-    projected = jnp.dot(flat_act, w_proj, preferred_element_type=jnp.float32).reshape(
-        pictures, rows_here, cols_here, model_dim
-    )
-    mixture = (skip.astype(jnp.float32) + projected).astype(jnp.bfloat16)
-    send_mix = to_targets(mixture, n_tiles, per_tile, group_part)
-    send_cot = to_targets(cotangent, n_tiles, per_tile, group_part)
-    got_mix, got_cot = (
-        lax.all_to_all(send_mix, ("row", "col"), split_axis=0, concat_axis=1, tiled=True),
-        lax.all_to_all(send_cot, ("row", "col"), split_axis=0, concat_axis=1, tiled=True),
-    )
-    summed, grad_wqkv, grad_out, grad_gain = attend_back(
-        received_to_groups(got_mix, row_tiles, per_tile, group_part),
-        received_to_groups(got_cot, row_tiles, per_tile, group_part),
-        norm_gain,
-        w_qkv,
-        w_out,
-        HEADS,
-    )
-    back_parts = groups_to_targets(summed, pictures, row_tiles, per_tile, group_part)
+    kern = depth_kernel.reshape(9, expand_dim)
+    cells = rows_here * cols_here
+    act, slope, got_mix, got_cot, ends, columns = forward(
+        expanded, skip.reshape(pictures, cells, model_dim), cotangent.reshape(pictures, cells, model_dim), kern, w_proj
+    )
+    flat_act = act.reshape(-1, expand_dim)
+    back, grad_wqkv, grad_out, grad_gain = attention(got_mix, got_cot, norm_gain, w_qkv, w_out)
+    grad_wqkv = jnp.concatenate([grad_wqkv[256 * j : 256 * j + 256] for j in range(3)], axis=1)
+    grad_gain = grad_gain[0]
+    left = columns[0, :, 7:41, None].astype(jnp.bfloat16)
+    right = columns[1, :, 7:41, None].astype(jnp.bfloat16)
+    tall = jnp.concatenate([ends[0][:, None], expanded, ends[1][:, None]], axis=1)
+    padded = jnp.concatenate([left, tall, right], axis=2)
+    back_parts = back.reshape(pictures, 64, 16, model_dim).transpose(1, 0, 2, 3)[:, None, :, None]
     returned = lax.all_to_all(back_parts, ("row", "col"), split_axis=0, concat_axis=1, tiled=True)
     grad_skip = returned_to_tile(returned, n_tiles, rows_here, cols_here)
     flat_grad = grad_skip.reshape(-1, model_dim)
     grad_proj = transposed_dot(flat_act, flat_grad)
     grad_act = jnp.dot(flat_grad, w_proj.T, preferred_element_type=jnp.float32)
     grad_act = grad_act.reshape(pictures, rows_here, cols_here, expand_dim)
-    _, pullback = jax.vjp(smooth, pre_act)
-    grad_pre = pullback(grad_act)[0].astype(jnp.bfloat16)
+    grad_pre = (grad_act * slope.reshape(grad_act.shape).astype(jnp.float32)).astype(jnp.bfloat16)
     grad_pre_pad = pad_tile(grad_pre, 1)
     grad_kernel = kernel_grad(grad_pre, padded, rows_here, cols_here)
     grad_expanded = depthwise_back(grad_pre_pad, depth_kernel, rows_here, cols_here).astype(

time: 525 us -> 384 us (0.73); the launches traced: 517 us -> 384 us
  Pallas kernels: 0 us -> 78 us
  matrix products: 101 us -> 25.4 us
  local copies, waits for them, and re-layouts: 72.2 us -> 8.44 us
  other arithmetic: 66.8 us -> 39.3 us
  starting transfers between devices: 47.6 us -> 20.6 us
  waiting for transfers between devices: 145 us -> 129 us
    pallas_call x0 -> x2, Pallas kernels: none -> 78 us  [the longest x1 53.8 us: forward(): pl.pallas_call(forward_kernel, out_shape=(jax.ShapeDtypeStruct((2, cells,...]
    dot_general x10 -> x0, matrix products: 65.9 us -> none  [the longest x6 55.9 us: contract(): jnp.einsum(pattern, left_op, right_op, preferred_element_type=jnp.float32)]
    convert_element_type x7 -> x3, local copies, waits for them, and re-layouts: 32.8 us -> 0.52 us  [the longest x2 0.3 us: on_device(): right = columns[1, :, 7:41, None].astype(jnp.bfloat16)]
    convert_element_type x6 -> x0, other arithmetic: 22.9 us -> none  [the longest x1 15.9 us: on_device(): activated = smooth(pre_act).astype(jnp.bfloat16)]
    all_to_all x2 -> x0, starting transfers between devices: 20.4 us -> none  [the longest x1 11.6 us: on_device(): lax.all_to_all(send_cot, ('row', 'col'), split_axis=0, concat_axis=1, til...]
    reshape x6 -> x2, local copies, waits for them, and re-layouts: 21.9 us -> 2.64 us  [the longest x1 1.52 us: on_device(): kern = depth_kernel.reshape(9, expand_dim)]
    ppermute x8 -> x4, waiting for transfers between devices: 14.4 us -> 2.08 us  [passed_along(): return lax.ppermute(block, axis, route)]
    ppermute x8 -> x4, starting transfers between devices: 21.8 us -> 10.1 us  [passed_along(): return lax.ppermute(block, axis, route)]
  transfers between devices with their start and end apart: 12 -> 6, of which waited for: 6 -> 4; matrix products, arithmetic and copies ran while one was open for 20% -> 10% of each run, Pallas kernels for 0% -> 0%
where the time goes in v1:
time: 384 us
  waiting for transfers between devices  129 us (34%)
  Pallas kernels  78 us (20%)
  blocking collectives  68.7 us (18%)
  other arithmetic  39.3 us (10%)
  matrix products  25.4 us (7%)
  starting transfers between devices  20.6 us (5%)
  between operations  14.4 us (4%)
  local copies, waits for them, and re-layouts  8.44 us (2%)
    psum x1, waiting for transfers between devices, on_device(): lax.psum((grad_kernel, grad_proj, grad_wqkv, grad_out, grad_gain), ('dp',...  120 us
    psum x1, blocking collectives, on_device(): lax.psum((grad_kernel, grad_proj, grad_wqkv, grad_out, grad_gain), ('dp',...  68.7 us
    pallas_call x1, Pallas kernels, forward(): pl.pallas_call(forward_kernel, out_shape=(jax.ShapeDtypeStruct((2, cells,...  53.8 us
    pallas_call x1, Pallas kernels, attention(): pl.pallas_call(attention_kernel, out_shape=(jax.ShapeDtypeStruct((2, 1024...  24.1 us
    dot_general x1, matrix products, on_device(): grad_act = jnp.dot(flat_grad, w_proj.T, preferred_element_type=jnp.float32)  20.9 us
    unnamed x1, other arithmetic  13.4 us
    all_to_all x1, starting transfers between devices, on_device(): lax.all_to_all(back_parts, ('row', 'col'), split_axis=0, concat_axis=1, t...  10.3 us
    ppermute x4, starting transfers between devices, passed_along(): return lax.ppermute(block, axis, route)  10.1 us
  transfers between devices with their start and end apart: 6, of which 4 were waited for; matrix products, arithmetic and copies ran while one was open for 10% of the time, Pallas kernels for 0%

profile of v1, /device:TPU:1, one launch (start us, length us, event | category | flops | bytes accessed | tf_op | source)
XLA Modules:
  0.0 383.7 jit_solution(17849553902593699138)
XLA Ops:
  7.2 0.0 copy-start.3
  7.2 0.0 copy-start.5
  7.2 0.0 copy-start.4
  7.2 0.0 copy-start.2
  7.2 0.0 copy-start.6
  7.2 1.5 reshape.74.kern_ref
  8.7 53.8 %forward.1 = (bf16[2,1024,1024]{2,1,0:T(8,128)(2,1)}, bf16[2,1024,1024]{2,1,0:T(8,128)(2,1)}, bf16[2,1024,256]{2,1,0:T(8,128)(2,1)}, bf16[2,1024,256]{2,1,0:T(8,...) custom-call(bf16[2,32,32,1024]{3,2,1,0:T(8,128)(2,1)} %bitcast.75, ...), custom_call_target="tpu_custom_call" | custom-call | tf_op jit(solution)/shard_map/forward/pallas_call | solution.py:322
  62.6 0.0 copy-done.3
  62.6 0.0 copy-done.5
  62.6 0.0 copy-done.4
  62.6 0.0 copy-done.2
  62.6 0.0 copy-done.6
  62.6 0.0 copy-start
  62.6 1.2 copy-done
  63.9 1.2 copy-done.1
  65.1 24.1 %attention.1 = (bf16[2,1024,256]{2,1,0:T(8,128)(2,1)S(1)}, f32[768,256]{1,0:T(8,128)S(1)}, f32[256,256]{1,0:T(8,128)}, f32[1,256]{1,0:T(1,128)S(1)}) custom-call(bf16[2,1024,256]{2,1,0:T(8,128)(2,1)S(1)} %copy-done, bf16[2,1024,256]{2,1,0:T(8,128)(2,1)S(1)} %copy-done.1, f32[1,256]{1,0:T(1,128)S(1)} %bitcast.73, bf16[256,768]{1,0:T(8,128)(2,1)S(1)} %copy-done.2, ...), custom_call_target="tpu_custom_call" | custom-call | tf_op jit(solution)/shard_map/attention/pallas_call | solution.py:450
  89.2 1.1 copy.48
  90.3 10.3 %all-to-all-start = ((bf16[64,1,2,1,16,256]{5,4,2,3,1,0:T(8,128)(2,1)}), bf16[64,1,2,1,16,256]{5,4,2,3,1,0:T(8,128)(2,1)S(1)}, u32[]{:S(2)}, u32[]{:S(2)}) async-start(bf16[64,1,2,1,16,256]{5,4,2,3,1,0:T(8,128)(2,1)} %bitcast.71), calls=%async_computation | async-start | bytes 2097152 | tf_op jit(solution)/shard_map/all_to_all | solution.py:644
  100.7 0.2 all-reduce.4.cloned.1.call-start
  100.9 0.0 copy-done.12
  100.9 0.6 fusion.20
  101.6 0.0 copy-done.11
  101.6 0.0 copy-done.9
  101.6 0.1 slice_bitcast_fusion
  101.7 0.1 fusion.19
  101.8 0.9 pad_maximum_fusion.6
  102.7 0.2 copy.39
  102.9 0.2 copy.37
  103.2 0.0 copy-start.10
  103.2 9.3 %pad_maximum_fusion = (bf16[2,34,33,1024]{3,2,1,0:T(8,128)(2,1)}, bf16[2,34,33,1024]{3,2,1,0:T(8,128)(2,1)}) fusion(bf16[2,34,1,1024]{3,2,1,0:T(2,128)(2,1)S(1)} %copy.39, bf16[2,1,32,1024]{3,2,1,0:T(8,128)(2,1)S(1)} %get-tuple-element.95, bf16[2,32,32,1024]{3,2,1,0:T(8,128)(2,1)} %bitcast.76, bf16[2,1,32,1024]{3,2,1,0:T(8,128)(2,1)S(1)} %get-tuple-element.94, ...), kind=kLoop, calls=%fused_computation.28 | loop fusion | flops 36765696 | bytes 13926400 | tf_op jit(solution)/shard_map/concatenate | solution.py:642
  112.4 7.0 %all-to-all-done = bf16[64,1,2,1,16,256]{5,4,2,3,1,0:T(8,128)(2,1)S(1)} async-done(((bf16[64,1,2,1,16,256]{5,4,2,3,1,0:T(8,128)(2,1)}), bf16[64,1,2,1,16,256]{5,4,2,3,1,0:T(8,128)(2,1)S(1)}, u32[]{:S(2)}, u32[]{:S(2)}) %all-to-all-start) | async-done | bytes 1048608 | tf_op jit(solution)/shard_map/all_to_all | solution.py:644
  119.5 0.1 copy.35
  119.6 0.0 copy-start.8
  119.6 0.0 copy-done.10
  119.6 20.9 %fusion.6 = (f32[1024]{0:T(1024)S(1)}, f32[1024]{0:T(1024)S(1)}, f32[1024]{0:T(1024)S(1)}, f32[1024]{0:T(1024)S(1)}, f32[1024]{0:T(1024)S(1)}, /*index=5*/f32[10...) fusion(bf16[2,34,33,1024]{3,2,1,0:T(8,128)(2,1)} %get-tuple-element.86,, ...), kind=kOutput, calls=%fused_computation.16 | convolution fusion | flops 1142938624 | bytes 43814912 | tf_op jit(solution)/shard_map/dot_general | solution.py:648
  140.5 2.0 fusion.18
  142.5 2.6 collective-permute-start
  145.2 1.9 collective-permute-start.1
  147.1 0.0 copy-done.8
  147.1 4.4 %fusion.21 = f32[1024,256]{1,0:T(8,128)} fusion(bf16[2048,1024]{1,0:T(8,128)(2,1)} %bitcast.101, bf16[2048,256]{1,0:T(8,128)(2,1)S(1)} %bitcast.79), kind=kOutput, calls=%fused_computation.60 | convolution fusion | flops 1073741824 | bytes 6291456 | tf_op jit(solution)/shard_map/dot_general | solution.py:480
  151.6 68.7 %all-reduce = (f32[3,3,1024]{2,1,0:T(4,128)S(1)}, f32[256]{0:T(256)S(1)}) all-reduce(f32[3,3,1024]{2,1,0:T(4,128)S(1)} %pad_maximum_fusion.10, f32[256]{0:T(256)S(1)} %bitcast.74), channel_id=1, replica_groups=mesh['dp'=2,'row'=2,'col'=32] {'dp','row','col'}, use_global_device_ids=true, to_apply=%region_9.10 | all-reduce | flops 9472 | bytes 75776 | tf_op jit(solution)/shard_map/psum | solution.py:656
  220.3 0.0 all-reduce.4.cloned.1.call-update
  220.3 0.0 copy-start.7
  220.3 0.6 broadcast_multiply_fusion.3
  221.0 0.0 collective-permute-done
  221.0 0.3 broadcast_select_fusion.1
  221.3 0.0 collective-permute-done.1
  221.3 0.3 broadcast_select_fusion
  221.6 1.1 pad_maximum_fusion.9
  222.7 1.3 collective-permute-start.2
  224.0 4.2 %collective-permute-start.3 = (bf16[2,1,34,1024]{3,2,1,0:T(8,128)(2,1)S(1)}, bf16[2,1,34,1024]{3,2,1,0:T(8,128)(2,1)S(1)}, u32[]{:S(2)}, u32[]{:S(2)}) collective-permute-start(bf16[2,1,34,1024]{3,2,1,0:T(8,128)(2,1)S(1)} %get-tuple-element.84), channel_id=1, source_target_pairs={{0,8},{1,9},{2,10},{3,11},{4,12},{5,13},{6,14},{7,15},{8,16},{9,17... | collective-permute-start | bytes 417800 | tf_op jit(solution)/shard_map/ppermute | solution.py:472
  228.2 0.6 broadcast_multiply_fusion.4
  228.8 0.0 copy-start.17
  228.8 0.0 copy-start.18
  228.8 1.5 collective-permute-done.2
  230.3 0.5 collective-permute-done.3
  230.9 0.0 copy-done.7
  230.9 6.8 %pad_maximum_fusion.1 = (bf16[2,33,34,1024]{3,2,1,0:T(8,128)(2,1)S(1)}, bf16[2,33,34,1024]{3,2,1,0:T(8,128)(2,1)S(1)}) fusion(bf16[2,1,34,1024]{3,2,1,0:T(8,128)(2,1)S(1)} %collective-permute-done.2, bf16[2,32,1,1024]{3,2,1,0:T(2,128)(2,1)S(1)} %broadcast_select_fusion, bf16[2,32,32,1024]{3,2,1,0:T(8,128)(2,1)S(1)} %copy-done.7, ...), kind=kLoop, calls=%fused_computation.29 | loop fusion | flops 36765696 | bytes 13926400 | tf_op jit(solution)/shard_map/concatenate | solution.py:582
  237.7 0.0 copy-done.13
  237.7 13.4 %fusion.16 = bf16[2,1,32,32,1024]{4,3,2,1,0:T(8,128)(2,1)} fusion(bf16[2,33,34,1024]{3,2,1,0:T(8,128)(2,1)S(1)} %get-tuple-element.82, f32[1024]{0:T(1024)S(1)} %bitcast.90, f32[1024]{0:T(1024)S(1)} %bitcast.91, f32[1024]{0:T(1024)S(1)} %bitcast.84, bf16[2,32,32,1024]{3,2,1,0:T(8,128)(2,1)S(1)} %copy-done.7, ...), kind=kLoop, calls=%fused_computation.35 | loop fusion | flops 69206016 | bytes 33853440
  251.1 119.8 %all-reduce.4.cloned.1.call-done = (f32[1024,256]{1,0:T(8,128)}, f32[256,768]{1,0:T(8,128)}, f32[256,256]{1,0:T(8,128)}) async-done(((f32[1024,256]{1,0:T(8,128)}, f32[256,768]{1,0:T(8,128)}, f32[256,256]{1,0:T(8,128)}), (f32[1024,256]{1,0:T(8,128)}, f32[256,768]{1,0:T(8,128)}, f32[256,256]{1,0:T(8,128)})) %all-reduce.4.cloned.1.call-update) | async-done | bytes 2097168 | tf_op jit(solution)/shard_map/psum | solution.py:656
  370.9 2.3 broadcast_multiply_fusion
  373.1 1.7 broadcast_multiply_fusion.2
  374.8 2.1 broadcast_multiply_fusion.1
  (18 shorter events, 0.1 us)
Async XLA Ops:
  7.2 55.4 %copy-start.3 = (bf16[512,256]{1,0:T(8,128)(2,1)S(1)}, bf16[512,256]{1,0:T(8,128)(2,1)}, u32[]{:S(2)}) copy-start(bf16[512,256]{1,0:T(8,128)(2,1)} %constant.41.clone.mask_ref) | copy-start | bytes 786436
  7.2 55.4 %copy-start.5 = (bf16[256,256]{1,0:T(8,128)(2,1)S(1)}, bf16[256,256]{1,0:T(8,128)(2,1)}, u32[]{:S(2)}) copy-start(bf16[256,256]{1,0:T(8,128)(2,1)} %constant.40.clone.perm_ref) | copy-start | bytes 393220
  7.2 55.4 %copy-start.4 = (bf16[256,256]{1,0:T(8,128)(2,1)S(1)}, bf16[256,256]{1,0:T(8,128)(2,1)}, u32[]{:S(2)}) copy-start(bf16[256,256]{1,0:T(8,128)(2,1)} %wout_ref.1) | copy-start | bytes 393220
  7.2 55.4 %copy-start.2 = (bf16[256,768]{1,0:T(8,128)(2,1)S(1)}, bf16[256,768]{1,0:T(8,128)(2,1)}, u32[]{:S(2)}) copy-start(bf16[256,768]{1,0:T(8,128)(2,1)} %wqkv_ref.1) | copy-start | bytes 1179652
  7.2 55.4 %copy-start.6 = (f32[256]{0:T(256)S(1)}, f32[256]{0:T(256)}, u32[]{:S(2)}) copy-start(f32[256]{0:T(256)} %param.15) | copy-start | bytes 3076
  8.7 92.2 %copy-start.12 = (f32[3,3,1024]{2,1,0:T(4,128)S(1)}, f32[3,3,1024]{2,1,0:T(4,128)}, u32[]{:S(2)}) copy-start(f32[3,3,1024]{2,1,0:T(4,128)} %param.13) | copy-start | bytes 110596
  62.6 1.2 copy-start
  63.9 1.2 copy-start.1
  65.1 36.5 %copy-start.11 = (bf16[2,2,32,1024]{3,2,1,0:T(8,128)(2,1)S(1)}, bf16[2,2,32,1024]{3,2,1,0:T(8,128)(2,1)}, u32[]{:S(2)}) copy-start(bf16[2,2,32,1024]{3,2,1,0:T(8,128)(2,1)} %get-tuple-element.22) | copy-start | bytes 786436
  65.1 36.5 %copy-start.9 = (f32[2,2,48,1024]{3,2,1,0:T(8,128)S(1)}, f32[2,2,48,1024]{3,2,1,0:T(8,128)}, u32[]{:S(2)}) copy-start(f32[2,2,48,1024]{3,2,1,0:T(8,128)} %get-tuple-element.21) | copy-start | bytes 2359300
  90.3 29.1 %all-to-all-start = ((bf16[64,1,2,1,16,256]{5,4,2,3,1,0:T(8,128)(2,1)}), bf16[64,1,2,1,16,256]{5,4,2,3,1,0:T(8,128)(2,1)S(1)}, u32[]{:S(2)}, u32[]{:S(2)}) async-start(bf16[64,1,2,1,16,256]{5,4,2,3,1,0:T(8,128)(2,1)} %bitcast.71), calls=%async_computation | async-start | bytes 2097152 | tf_op jit(solution)/shard_map/all_to_all | solution.py:644
  100.7 270.2 %all-reduce.4.cloned.1.call-start = ((), (), s32[]{:S(2)}) async-start(), calls=%async_computation.1 | async-start | bytes 4194304 | tf_op jit(solution)/shard_map/psum | solution.py:656
  103.2 16.4 %copy-start.10 = (bf16[1024,256]{1,0:T(8,128)(2,1)S(1)}, bf16[1024,256]{1,0:T(8,128)(2,1)}, u32[]{:S(2)}) copy-start(bf16[1024,256]{1,0:T(8,128)(2,1)} %wproj_ref.1) | copy-start | bytes 1572868
  119.6 27.5 %copy-start.8 = (bf16[64,1,2,1,16,256]{5,4,0,2,3,1:T(8,128)(2,1)}, bf16[64,1,2,1,16,256]{5,4,0,2,3,1:T(8,128)(2,1)S(1)}, u32[]{:S(2)}) copy-start(bf16[64,1,2,1,16,256]{5,4,0,2,3,1:T(8,128)(2,1)S(1)} %copy.35) | copy-start | bytes 3145732
  142.5 78.5 %collective-permute-start = (bf16[2,32,1,1024]{3,2,1,0:T(2,128)(2,1)S(1)}, bf16[2,32,1,1024]{3,2,1,0:T(2,128)(2,1)S(1)}, u32[]{:S(2)}, u32[]{:S(2)}) collective-permute-start(bf16[2,32,1,1024]{3,2,1,0:T(2,128)(2,1)S(1)} %get-tuple-element.87), channel_id=1, source_target_pairs={{0,1},{1,2},{2,3},{3,4},{4,5},{5,6},{6,7},{7,8},{8,9},{9,10},{10,1... | collective-permute-start | bytes 393224 | tf_op jit(solution)/shard_map/ppermute | solution.py:472
  145.2 76.1 %collective-permute-start.1 = (bf16[2,32,1,1024]{3,2,1,0:T(2,128)(2,1)S(1)}, bf16[2,32,1,1024]{3,2,1,0:T(2,128)(2,1)S(1)}, u32[]{:S(2)}, u32[]{:S(2)}) collective-permute-start(bf16[2,32,1,1024]{3,2,1,0:T(2,128)(2,1)S(1)} %get-tuple-element.88), channel_id=1, source_target_pairs={{1,0},{2,1},{3,2},{4,3},{5,4},{6,5},{7,6},{8,7},{9,8},{10,9},{11,1... | collective-permute-start | bytes 393224 | tf_op jit(solution)/shard_map/ppermute | solution.py:472
  220.3 10.6 %copy-start.7 = (bf16[2,32,32,1024]{3,2,1,0:T(8,128)(2,1)S(1)}, bf16[2,32,32,1024]{3,2,1,0:T(8,128)(2,1)}, u32[]{:S(2)}) copy-start(bf16[2,32,32,1024]{3,2,1,0:T(8,128)(2,1)} %get-tuple-element.105) | copy-start | bytes 12582916
  222.7 7.6 %collective-permute-start.2 = (bf16[2,1,34,1024]{3,2,1,0:T(8,128)(2,1)S(1)}, bf16[2,1,34,1024]{3,2,1,0:T(8,128)(2,1)S(1)}, u32[]{:S(2)}, u32[]{:S(2)}) collective-permute-start(bf16[2,1,34,1024]{3,2,1,0:T(8,128)(2,1)S(1)} %get-tuple-element.83), channel_id=1, source_target_pairs={{8,0},{9,1},{10,2},{11,3},{12,4},{13,5},{14,6},{15,7},{16,8},{17,9... | collective-permute-start | bytes 417800 | tf_op jit(solution)/shard_map/ppermute | solution.py:472
  224.0 6.9 %collective-permute-start.3 = (bf16[2,1,34,1024]{3,2,1,0:T(8,128)(2,1)S(1)}, bf16[2,1,34,1024]{3,2,1,0:T(8,128)(2,1)S(1)}, u32[]{:S(2)}, u32[]{:S(2)}) collective-permute-start(bf16[2,1,34,1024]{3,2,1,0:T(8,128)(2,1)S(1)} %get-tuple-element.84), channel_id=1, source_target_pairs={{0,8},{1,9},{2,10},{3,11},{4,12},{5,13},{6,14},{7,15},{8,16},{9,17... | collective-permute-start | bytes 417800 | tf_op jit(solution)/shard_map/ppermute | solution.py:472
  228.8 8.9 %copy-start.13 = (f32[1,1,1024]{2,1,0:T(1,128)S(1)}, f32[1,1,1024]{2,1,0:T(1,128)}, u32[]{:S(2)}) copy-start(f32[1,1,1024]{2,1,0:T(1,128)} %get-tuple-element.99) | copy-start | bytes 12292
  228.8 8.9 %copy-start.14 = (f32[1,1,1024]{2,1,0:T(1,128)S(1)}, f32[1,1,1024]{2,1,0:T(1,128)}, u32[]{:S(2)}) copy-start(f32[1,1,1024]{2,1,0:T(1,128)} %get-tuple-element.100) | copy-start | bytes 12292
  228.8 8.9 %copy-start.15 = (f32[1,1,1024]{2,1,0:T(1,128)S(1)}, f32[1,1,1024]{2,1,0:T(1,128)}, u32[]{:S(2)}) copy-start(f32[1,1,1024]{2,1,0:T(1,128)} %get-tuple-element.101) | copy-start | bytes 12292
  228.8 8.9 %copy-start.16 = (f32[1,1,1024]{2,1,0:T(1,128)S(1)}, f32[1,1,1024]{2,1,0:T(1,128)}, u32[]{:S(2)}) copy-start(f32[1,1,1024]{2,1,0:T(1,128)} %get-tuple-element.102) | copy-start | bytes 12292
  228.8 8.9 %copy-start.17 = (f32[1,1,1024]{2,1,0:T(1,128)S(1)}, f32[1,1,1024]{2,1,0:T(1,128)}, u32[]{:S(2)}) copy-start(f32[1,1,1024]{2,1,0:T(1,128)} %get-tuple-element.103) | copy-start | bytes 12292
  228.8 8.9 %copy-start.18 = (f32[1,1,1024]{2,1,0:T(1,128)S(1)}, f32[1,1,1024]{2,1,0:T(1,128)}, u32[]{:S(2)}) copy-start(f32[1,1,1024]{2,1,0:T(1,128)} %get-tuple-element.104) | copy-start | bytes 12292
Sparse Core Ops, SparseCore 0:
  220.4 150.3 all-reduce.3

commit v2 on v1

--- a/solution.py
+++ b/solution.py
@@ -463,233 +463,415 @@
     )(got_mix, got_cot, gain.reshape(1, 256), wqkv, wout, perm, mask)
 
 
-HEADS = 8
-
-
-def passed_along(block, axis, distance):
-    devices = range(lax.axis_size(axis))
-    route = [(i - distance, i) for i in devices if i - distance in devices]
-    return lax.ppermute(block, axis, route)
-
-
-def contract(pattern, left_op, right_op):
-    return jnp.einsum(pattern, left_op, right_op, preferred_element_type=jnp.float32)
-
-
-def transposed_dot(left_op, right_op):
-    return lax.dot_general(
-        left_op, right_op, (((0,), (0,)), ((), ())), preferred_element_type=jnp.float32
+def owner_id(j, m):
+    return {"dp": j // 4, "row": lax.rem(j // 2, 2), "col": m * 2 + lax.rem(j, 2)}
+
+
+def backward_kernel(
+    back_hbm, act_hbm, dg_hbm, x_hbm, ends_hbm, columns_hbm, kern_ref, wproj_ref, gw_ref, go_ref, gg_ref,
+    ge_hbm, gs_hbm, gkern_out, gproj_out, gwqkv_out, gout_out, ggain_out,
+    gs, act, dg, xgrid, ggrid, xcols, gcols, sides_out, sides_in, corners_out, corners_in, terms, gproj_t, gkern,
+    part_out, part_in, small_out, small_in, whole,
+    load_sem, back_send, back_recv, own_sem, rim_send, rim_recv, store_sem,
+    first_send, first_recv, extra_send, extra_recv, second_send, second_recv,
+    share_send, share_recv, last_send, last_recv, scale,
+):
+    me = my_tile()
+    tile_row, tile_col = me // GRID, lax.rem(me, GRID)
+    dp = lax.axis_index("dp")
+    core = lax.rem(lax.axis_index("col"), 2)
+    j = dp * 4 + lax.axis_index("row") * 2 + core
+    m = lax.axis_index("col") // 2
+    loads = [
+        pltpu.make_async_copy(dg_hbm, dg, load_sem.at[0]),
+        pltpu.make_async_copy(act_hbm, act, load_sem.at[1]),
+        pltpu.make_async_copy(x_hbm, xgrid.at[:, pl.ds(1, ROWS)], load_sem.at[2]),
+        pltpu.make_async_copy(ends_hbm.at[0], xgrid.at[:, 0], load_sem.at[3]),
+        pltpu.make_async_copy(ends_hbm.at[1], xgrid.at[:, ROWS + 1], load_sem.at[4]),
+        pltpu.make_async_copy(columns_hbm, xcols, load_sem.at[5]),
+    ]
+    for copy in loads:
+        copy.start()
+    barrier = pltpu.get_barrier_semaphore()
+
+    def greet(i, carry):
+        pl.semaphore_signal(
+            barrier, inc=1, device_id=tile_id(lax.rem(me + i, TILES)), device_id_type=MESH_ID
+        )
+        return carry
+
+    lax.fori_loop(1, TILES, greet, 0)
+    for n in range(4):
+        pl.semaphore_signal(
+            barrier, inc=1, device_id=owner_id((1 - dp) * 4 + n, m), device_id_type=MESH_ID
+        )
+    for n in range(4):
+        part_out[4 + n, 0:256] = (gw_ref[256 * n : 256 * n + 256] if n < 3 else go_ref[...]).astype(BF16)
+    pl.semaphore_wait(barrier, TILES + 3)
+
+    def back_copy(target, slot):
+        return pltpu.make_async_remote_copy(
+            src_ref=back_hbm.at[:, pl.ds(pl.multiple_of(target * 16, 16), 16), :],
+            dst_ref=gs.at[:, pl.ds(pl.multiple_of(slot * 16, 16), 16), :],
+            send_sem=back_send.at[target],
+            recv_sem=back_recv.at[slot],
+            device_id=tile_id(target),
+            device_id_type=MESH_ID,
+        )
+
+    def send_back(i, carry):
+        target = lax.rem(tile_row + GRID - i // GRID, GRID) * GRID + lax.rem(
+            tile_col + GRID - lax.rem(i, GRID), GRID
+        )
+        back_copy(target, me).start()
+        return carry
+
+    lax.fori_loop(1, TILES, send_back, 0)
+    own = pl.ds(pl.multiple_of(me * 16, 16), 16)
+    own_copy = pltpu.make_async_copy(back_hbm.at[:, own, :], gs.at[:, own, :], own_sem.at[0])
+    own_copy.start()
+
+    def first_copy(owner, slot):
+        return pltpu.make_async_remote_copy(
+            src_ref=part_out.at[owner, pl.ds(0, 256)],
+            dst_ref=part_in.at[slot, pl.ds(0, 256)],
+            send_sem=first_send.at[owner],
+            recv_sem=first_recv.at[slot],
+            device_id=owner_id(owner, m),
+            device_id_type=MESH_ID,
+        )
+
+    def extra_copy(owner, slot):
+        return pltpu.make_async_remote_copy(
+            src_ref=part_out.at[owner, pl.ds(256, 16)],
+            dst_ref=part_in.at[slot, pl.ds(256, 16)],
+            send_sem=extra_send.at[owner],
+            recv_sem=extra_recv.at[slot],
+            device_id=owner_id(owner, m),
+            device_id_type=MESH_ID,
+        )
+
+    def second_copy(owner, slot):
+        return pltpu.make_async_remote_copy(
+            src_ref=small_out.at[owner],
+            dst_ref=small_in.at[slot],
+            send_sem=second_send.at[owner],
+            recv_sem=second_recv.at[slot],
+            device_id=owner_id(j, owner),
+            device_id_type=MESH_ID,
+        )
+
+    def share_copy(other, slot):
+        rows = pl.ds(pl.multiple_of(slot * 16, 16), 16)
+        return pltpu.make_async_remote_copy(
+            src_ref=whole.at[j, pl.ds(pl.multiple_of(m * 16, 16), 16)],
+            dst_ref=whole.at[j, rows],
+            send_sem=share_send.at[other],
+            recv_sem=share_recv.at[slot],
+            device_id=owner_id(j, other),
+            device_id_type=MESH_ID,
+        )
+
+    def last_copy(other, slot):
+        return pltpu.make_async_remote_copy(
+            src_ref=whole.at[j],
+            dst_ref=whole.at[slot],
+            send_sem=last_send.at[other],
+            recv_sem=last_recv.at[slot],
+            device_id=owner_id(other, m),
+            device_id_type=MESH_ID,
+        )
+
+    def to_eight(copy, begin, end):
+        for n in range(begin, end):
+
+            @pl.when(j != n)
+            def _():
+                copy(n, j).start()
+
+    def around(count, mine, action):
+        def one(i, carry):
+            action(lax.rem(mine + i, count))
+            return carry
+
+        lax.fori_loop(1, count, one, 0)
+
+    to_eight(first_copy, 4, 8)
+    gproj_t[...] = jnp.zeros_like(gproj_t)
+    loads[0].wait()
+    loads[1].wait()
+    own_copy.wait()
+
+    def do_band(step, carry):
+        band = lax.rem(step + tile_row, BANDS)
+        cells = pl.ds(pl.multiple_of(band * BAND_CELLS, BAND_CELLS), BAND_CELLS)
+
+        def arrived(i, inner):
+            source = band * BAND_TILES + i
+
+            @pl.when(source != me)
+            def _():
+                back_copy(source, source).wait_recv()
+
+            return inner
+
+        lax.fori_loop(0, BAND_TILES, arrived, 0)
+        flat = gs[:, cells, :].reshape(2 * BAND_CELLS, WIDTH)
+        flat_t = flat.T
+        for n in range(4):
+            lanes = slice(256 * n, 256 * n + 256)
+            grad_act = dot_t(flat, wproj_ref[lanes, :])
+            slope = dg[:, cells, lanes].astype(F32).reshape(2 * BAND_CELLS, 256)
+            grad_pre = (grad_act * slope).astype(BF16)
+            ggrid[:, pl.ds(1 + band * BAND, BAND), :, lanes] = grad_pre.reshape(2, BAND, COLS, 256)
+            gproj_t[:, lanes] += dot(flat_t, act[:, cells, lanes].reshape(2 * BAND_CELLS, 256))
+        return carry
+
+    lax.fori_loop(0, BANDS, do_band, 0)
+    gs_store = pltpu.make_async_copy(gs, gs_hbm, own_sem.at[1])
+    gs_store.start()
+    collect_sides(ggrid, sides_out, corners_out)
+    rim = rim_copies(me, ggrid, sides_out, sides_in, corners_out, corners_in, rim_send, rim_recv)
+    for copy in rim:
+        copy.start()
+    for n in range(4):
+        part_out[n, 0:256] = gproj_t[:, 256 * n : 256 * n + 256].T.astype(BF16)
+    to_eight(first_copy, 0, 4)
+    for copy in loads[2:]:
+        copy.wait()
+
+    spot = lax.broadcasted_iota(jnp.int32, (BAND, COLS, LANES), 1)
+
+    def kernel_block(block, carry):
+        lanes = pl.ds(pl.multiple_of(block * LANES, LANES), LANES)
+
+        def one(index, sums):
+            picture, band = index // BANDS, lax.rem(index, BANDS)
+            grads = ggrid[picture, pl.ds(1 + band * BAND, BAND), :, lanes].astype(F32)
+            rows = xgrid[picture, pl.ds(band * BAND, BAND + 2), :, lanes].astype(F32)
+            shifted = (
+                jnp.where(spot == COLS - 1, 0.0, pltpu.roll(grads, COLS - 1, 1)),
+                grads,
+                jnp.where(spot == 0, 0.0, pltpu.roll(grads, 1, 1)),
+            )
+            new = []
+            for row_off in range(3):
+                for col_off in range(3):
+                    product = shifted[col_off] * rows[row_off : row_off + BAND]
+                    product = product.reshape(BAND * 4, 8, LANES).sum(axis=0)
+                    new.append(sums[3 * row_off + col_off] + product)
+            return tuple(new)
+
+        sums = lax.fori_loop(
+            0, 2 * BANDS, one, tuple(jnp.zeros((8, LANES), F32) for _ in range(9))
+        )
+        for n in range(9):
+            gkern[n : n + 1, lanes] = jnp.sum(sums[n], axis=0, keepdims=True)
+        return carry
+
+    lax.fori_loop(0, LANE_BLOCKS, kernel_block, 0)
+    for row_off in range(3):
+        for side in range(2):
+            n = 3 * row_off + 2 * side
+            for picture in range(2):
+                beside = xcols[side, picture, 7 + row_off : 7 + row_off + ROWS, :]
+                gkern[n : n + 1, :] += jnp.sum(
+                    sides_out[side, picture].astype(F32) * beside, axis=0, keepdims=True
+                )
+    for n in range(8):
+        if n < 4:
+            rows = [gkern[0:9, 256 * n : 256 * n + 256], jnp.zeros((7, 256), F32)]
+        elif n == 4:
+            rows = [gg_ref[...], jnp.zeros((15, 256), F32)]
+        else:
+            rows = [jnp.zeros((16, 256), F32)]
+        part_out[n, 256:272] = jnp.concatenate(rows, axis=0).astype(BF16)
+    to_eight(extra_copy, 0, 8)
+
+    for copy in rim:
+        copy.wait_recv()
+    for copy in rim:
+        copy.wait_send()
+    clear_outside(me, ggrid, sides_in, corners_in)
+    column_stack(sides_in, corners_in, gcols)
+    column_terms(
+        gcols, lambda a, c: kern_ref[8 - 3 * a - c : 9 - 3 * a - c, :], (0, 2), terms
     )
 
-
-def smooth(inside):
-    return jax.nn.gelu(inside, approximate=True)
-
-
-def depthwise(padded, kernel, n_rows, n_cols):
-    summed = jnp.zeros(padded.shape[:-3] + (n_rows, n_cols, padded.shape[-1]), jnp.float32)
-    for row_off in range(3):
-        for col_off in range(3):
-            summed = summed + kernel[row_off, col_off] * padded[
-                ..., row_off : row_off + n_rows, col_off : col_off + n_cols, :
-            ].astype(jnp.float32)
-    return summed
-
-
-def depthwise_back(padded_grad, kernel, n_rows, n_cols):
-    summed = jnp.zeros(
-        padded_grad.shape[:-3] + (n_rows, n_cols, padded_grad.shape[-1]), jnp.float32
+    def band_copy(band):
+        cells = pl.ds(pl.multiple_of(band * BAND_CELLS, BAND_CELLS), BAND_CELLS)
+        return pltpu.make_async_copy(dg.at[:, cells, :], ge_hbm.at[:, cells, :], store_sem.at[band])
+
+    def last_band(band, carry):
+        first = band * BAND
+        cells = pl.ds(pl.multiple_of(band * BAND_CELLS, BAND_CELLS), BAND_CELLS)
+
+        def do_block(index, inner):
+            picture, block = index // LANE_BLOCKS, lax.rem(index, LANE_BLOCKS)
+            lanes = pl.ds(pl.multiple_of(block * LANES, LANES), LANES)
+            rows = ggrid[picture, pl.ds(first, BAND + 2), :, lanes].astype(F32)
+            weights = [kern_ref[8 - n : 9 - n, lanes] for n in range(9)]
+            total = convolve(
+                rows,
+                weights,
+                terms[0, picture, band, 0:BAND, lanes],
+                terms[1, picture, band, 0:BAND, lanes],
+            )
+            dg[picture, cells, lanes] = total.astype(BF16).reshape(BAND_CELLS, LANES)
+            return inner
+
+        lax.fori_loop(0, 2 * LANE_BLOCKS, do_block, 0)
+        band_copy(band).start()
+        return carry
+
+    lax.fori_loop(0, 3, last_band, 0)
+
+    around(8, j, lambda p: first_copy(p, p).wait_recv())
+    around(8, j, lambda p: extra_copy(p, p).wait_recv())
+    part_in[j] = part_out[j]
+    total = part_in[0].astype(F32)
+    for n in range(1, 8):
+        total = total + part_in[n].astype(F32)
+    total = total.astype(BF16)
+    for n in range(16):
+        small_out[n, 0:16] = total[16 * n : 16 * n + 16]
+        small_out[n, 16:32] = total[256:272]
+    around(16, m, lambda p: second_copy(p, m).start())
+
+    lax.fori_loop(3, 6, last_band, 0)
+
+    around(16, m, lambda p: second_copy(p, p).wait_recv())
+    small_in[m] = small_out[m]
+    total = small_in[0].astype(F32)
+    for n in range(1, 16):
+        total = total + small_in[n].astype(F32)
+    total = total.astype(BF16)
+    whole[j, pl.ds(pl.multiple_of(m * 16, 16), 16)] = total[0:16]
+    whole[j, 256:272] = total[16:32]
+    around(16, m, lambda p: share_copy(p, m).start())
+
+    lax.fori_loop(6, BANDS, last_band, 0)
+
+    around(16, m, lambda p: share_copy(p, p).wait_recv())
+    around(16, m, lambda p: share_copy(p, p).wait_send())
+    around(8, j, lambda p: last_copy(p, j).start())
+    around(8, j, lambda p: first_copy(p, p).wait_send())
+    around(8, j, lambda p: extra_copy(p, p).wait_send())
+    around(16, m, lambda p: second_copy(p, p).wait_send())
+    around(TILES, me, lambda p: back_copy(p, p).wait_send())
+    gs_store.wait()
+    for band in range(BANDS):
+        band_copy(band).wait()
+    around(8, j, lambda p: last_copy(p, p).wait_recv())
+    around(8, j, lambda p: last_copy(p, p).wait_send())
+    for n in range(8):
+        block = whole[n, 0:256].astype(F32) * scale
+        if n < 4:
+            gproj_out[256 * n : 256 * n + 256, :] = block
+            gkern_out[:, 256 * n : 256 * n + 256] = whole[n, 256:272].astype(F32)[0:9] * scale
+        elif n < 7:
+            gwqkv_out[:, 256 * (n - 4) : 256 * (n - 4) + 256] = block
+        else:
+            gout_out[...] = block
+    ggain_out[...] = whole[4, 256:272].astype(F32)[0:1] * scale
+
+
+def backward(back, act, slope, x, ends, columns, kern, wproj, gw, go, gg, scale):
+    vmem = pl.BlockSpec(memory_space=pltpu.VMEM)
+    anywhere = pl.BlockSpec(memory_space=pl.ANY)
+    cells = ROWS * COLS
+    dma = pltpu.SemaphoreType.DMA
+
+    def kernel(*refs):
+        backward_kernel(*refs, scale)
+
+    return pl.pallas_call(
+        kernel,
+        out_shape=(
+            jax.ShapeDtypeStruct((2, cells, EXPAND), BF16),
+            jax.ShapeDtypeStruct((2, cells, WIDTH), BF16),
+            jax.ShapeDtypeStruct((9, EXPAND), F32),
+            jax.ShapeDtypeStruct((EXPAND, WIDTH), F32),
+            jax.ShapeDtypeStruct((WIDTH, 3 * WIDTH), F32),
+            jax.ShapeDtypeStruct((WIDTH, WIDTH), F32),
+            jax.ShapeDtypeStruct((1, WIDTH), F32),
+        ),
+        in_specs=[anywhere] * 6 + [vmem] * 5,
+        out_specs=(anywhere,) * 2 + (vmem,) * 5,
+        scratch_shapes=[
+            pltpu.VMEM((2, cells, WIDTH), BF16),
+            pltpu.VMEM((2, cells, EXPAND), BF16),
+            pltpu.VMEM((2, cells, EXPAND), BF16),
+            pltpu.VMEM((2, ROWS + 2, COLS, EXPAND), BF16),
+            pltpu.VMEM((2, ROWS + 2, COLS, EXPAND), BF16),
+            pltpu.VMEM((2, 2, 48, EXPAND), F32),
+            pltpu.VMEM((2, 2, 48, EXPAND), F32),
+            pltpu.VMEM((2, 2, ROWS, EXPAND), BF16),
+            pltpu.VMEM((2, 2, ROWS, EXPAND), BF16),
+            pltpu.VMEM((4, 16, EXPAND), BF16),
+            pltpu.VMEM((4, 16, EXPAND), BF16),
+            pltpu.VMEM((2, 2, BANDS, 8, EXPAND), F32),
+            pltpu.VMEM((WIDTH, EXPAND), F32),
+            pltpu.VMEM((16, EXPAND), F32),
+            pltpu.VMEM((8, 272, 256), BF16),
+            pltpu.VMEM((8, 272, 256), BF16),
+            pltpu.VMEM((16, 32, 256), BF16),
+            pltpu.VMEM((16, 32, 256), BF16),
+            pltpu.VMEM((8, 272, 256), BF16),
+            dma((6,)),
+            dma((TILES,)),
+            dma((TILES,)),
+            dma((2,)),
+            dma((8,)),
+            dma((8,)),
+            dma((BANDS,)),
+            dma((8,)),
+            dma((8,)),
+            dma((8,)),
+            dma((8,)),
+            dma((16,)),
+            dma((16,)),
+            dma((16,)),
+            dma((16,)),
+            dma((8,)),
+            dma((8,)),
+        ],
+        compiler_params=pltpu.CompilerParams(
+            collective_id=1, has_side_effects=True, vmem_limit_bytes=56 * 2**20
+        ),
+        name="backward",
+    )(back, act, slope, x, ends, columns, kern, wproj, gw, go, gg)
+
+
+def on_device(expanded, skip, cotangent, depth_kernel, w_proj, norm_gain, w_qkv, w_out):
+    cells = ROWS * COLS
+    kern = depth_kernel.reshape(9, EXPAND)
+    x = expanded[:, 0]
+    act, slope, got_mix, got_cot, ends, columns = forward(
+        x, skip.reshape(2, cells, WIDTH), cotangent.reshape(2, cells, WIDTH), kern, w_proj
     )
-    for row_off in range(3):
-        for col_off in range(3):
-            summed = summed + kernel[row_off, col_off] * padded_grad[
-                ..., 2 - row_off : 2 - row_off + n_rows, 2 - col_off : 2 - col_off + n_cols, :
-            ].astype(jnp.float32)
-    return summed
-
-
-def kernel_grad(grad_pre, padded, n_rows, n_cols):
-    grad_float = grad_pre.astype(jnp.float32)
-    lead_axes = tuple(range(grad_float.ndim - 1))
-    stacked = []
-    for row_off in range(3):
-        row_terms = []
-        for col_off in range(3):
-            window = padded[..., row_off : row_off + n_rows, col_off : col_off + n_cols, :].astype(
-                jnp.float32
-            )
-            row_terms.append(jnp.sum(grad_float * window, axis=lead_axes))
-        stacked.append(jnp.stack(row_terms))
-    return jnp.stack(stacked)
-
-
-def attend_back(mixture, cotangent, norm_gain, w_qkv, w_out, n_heads):
-    groups, length, model_dim = mixture.shape
-    head_size = model_dim // n_heads
-    score_scale = 1.0 / math.sqrt(head_size)
-    mix_float = mixture.astype(jnp.float32)
-    inverse = lax.rsqrt(jnp.mean(mix_float * mix_float, axis=-1, keepdims=True) + 1e-06)
-    normed = (mix_float * inverse * norm_gain).astype(jnp.bfloat16)
-    flat_norm = normed.reshape(groups * length, model_dim)
-    proj_qkv = jnp.dot(flat_norm, w_qkv, preferred_element_type=jnp.float32).astype(jnp.bfloat16)
-    proj_qkv = proj_qkv.reshape(groups, length, 3, n_heads, head_size)
-    queries = proj_qkv[:, :, 0]
-    key_rows = proj_qkv[:, :, 1]
-    values = proj_qkv[:, :, 2]
-    scores = contract("gqhd,gkhd->ghqk", queries, key_rows) * score_scale
-    attn_probs = jax.nn.softmax(scores, axis=-1)
-    weights_bf = attn_probs.astype(jnp.bfloat16)
-    attended = contract("ghqk,gkhd->gqhd", weights_bf, values).astype(jnp.bfloat16)
-    attended = attended.reshape(groups * length, model_dim)
-    flat_cot = cotangent.reshape(groups * length, model_dim)
-    grad_out = transposed_dot(attended, flat_cot)
-    grad_att = jnp.dot(flat_cot, w_out.T, preferred_element_type=jnp.float32).astype(jnp.bfloat16)
-    grad_att = grad_att.reshape(groups, length, n_heads, head_size)
-    grad_values = contract("ghqk,gqhd->gkhd", weights_bf, grad_att)
-    grad_probs = contract("gqhd,gkhd->ghqk", grad_att, values)
-    grad_scores = (
-        attn_probs
-        * (grad_probs - jnp.sum(grad_probs * attn_probs, axis=-1, keepdims=True))
-        * score_scale
-    )
-    grad_scores = grad_scores.astype(jnp.bfloat16)
-    grad_query = contract("ghqk,gkhd->gqhd", grad_scores, key_rows)
-    grad_keys = contract("ghqk,gqhd->gkhd", grad_scores, queries)
-    grad_qkv = jnp.stack([grad_query, grad_keys, grad_values], axis=2).astype(jnp.bfloat16)
-    grad_qkv = grad_qkv.reshape(groups * length, 3 * model_dim)
-    grad_wqkv = transposed_dot(flat_norm, grad_qkv)
-    grad_normed = jnp.dot(grad_qkv, w_qkv.T, preferred_element_type=jnp.float32).reshape(
-        groups, length, model_dim
-    )
-    grad_gain = jnp.sum(grad_normed * mix_float * inverse, axis=(0, 1))
-    scaled = grad_normed * norm_gain
-    grad_mix = inverse * scaled - mix_float * inverse * inverse * inverse * jnp.mean(
-        scaled * mix_float, axis=-1, keepdims=True
-    )
-    summed = (cotangent.astype(jnp.float32) + grad_mix).astype(jnp.bfloat16)
-    return (summed, grad_wqkv, grad_out, grad_gain)
-
-
-def pad_tile(tile, width):
-    tile_col = lax.axis_index(("row", "col")) % GRID
-    from_left = passed_along(tile[:, :, -width:], ("row", "col"), 1)
-    from_right = passed_along(tile[:, :, :width], ("row", "col"), -1)
-    from_left = jnp.where(tile_col == 0, jnp.zeros_like(from_left), from_left)
-    from_right = jnp.where(tile_col == GRID - 1, jnp.zeros_like(from_right), from_right)
-    sided = jnp.concatenate([from_left, tile, from_right], axis=2)
-    from_above = passed_along(sided[:, -width:], ("row", "col"), GRID)
-    from_below = passed_along(sided[:, :width], ("row", "col"), -GRID)
-    return jnp.concatenate([from_above, sided, from_below], axis=1)
-
-
-def to_targets(tile, n_tiles, per_tile, group_part):
-    pictures, rows_here, cols_here, channels = tile.shape
-    tile = tile.reshape(pictures, per_tile, n_tiles, group_part, channels)
-    tile = tile.transpose(2, 0, 1, 3, 4)
-    return tile.reshape(n_tiles, 1, pictures, per_tile, group_part, channels)
-
-
-def received_to_groups(tensor, row_tiles, per_tile, group_part):
-    pictures = tensor.shape[2]
-    channels = tensor.shape[-1]
-    tensor = tensor.reshape(row_tiles, GRID, pictures, per_tile, group_part, channels)
-    tensor = tensor.transpose(2, 4, 0, 3, 1, 5)
-    return tensor.reshape(pictures * group_part, GRID * GRID, channels)
-
-
-def groups_to_targets(tensor, pictures, row_tiles, per_tile, group_part):
-    channels = tensor.shape[-1]
-    tensor = tensor.reshape(pictures, group_part, row_tiles, per_tile, GRID, channels)
-    tensor = tensor.transpose(2, 4, 0, 3, 1, 5)
-    return tensor.reshape(row_tiles * GRID, 1, pictures, per_tile, group_part, channels)
-
-
-def returned_to_tile(tensor, n_tiles, rows_here, cols_here):
-    pictures, per_tile, group_part, channels = tensor.shape[2:]
-    tensor = tensor.reshape(n_tiles, pictures, per_tile, group_part, channels).transpose(
-        1, 2, 0, 3, 4
-    )
-    return tensor.reshape(pictures, rows_here, cols_here, channels)
-
-
-def on_device(expanded, skip, cotangent, depth_kernel, w_proj, norm_gain, w_qkv, w_out):
-    expanded = expanded[:, 0]
-    skip = skip[:, 0]
-    cotangent = cotangent[:, 0]
-    pictures, rows_here, cols_here, expand_dim = expanded.shape
-    model_dim = skip.shape[3]
-    n_row = lax.axis_size("row")
-    n_col = lax.axis_size("col")
-    n_tiles = n_row * n_col
-    row_tiles = n_tiles // GRID
-    span_a = rows_here * row_tiles // GRID
-    per_tile = GRID // row_tiles
-    group_part = span_a * cols_here // n_tiles
-    token_count = pictures * lax.axis_size("dp") * rows_here * cols_here * n_tiles
-    factor = 1.0 / math.sqrt(token_count)
-    kern = depth_kernel.reshape(9, expand_dim)
-    cells = rows_here * cols_here
-    act, slope, got_mix, got_cot, ends, columns = forward(
-        expanded, skip.reshape(pictures, cells, model_dim), cotangent.reshape(pictures, cells, model_dim), kern, w_proj
-    )
-    flat_act = act.reshape(-1, expand_dim)
     back, grad_wqkv, grad_out, grad_gain = attention(got_mix, got_cot, norm_gain, w_qkv, w_out)
-    grad_wqkv = jnp.concatenate([grad_wqkv[256 * j : 256 * j + 256] for j in range(3)], axis=1)
-    grad_gain = grad_gain[0]
-    left = columns[0, :, 7:41, None].astype(jnp.bfloat16)
-    right = columns[1, :, 7:41, None].astype(jnp.bfloat16)
-    tall = jnp.concatenate([ends[0][:, None], expanded, ends[1][:, None]], axis=1)
-    padded = jnp.concatenate([left, tall, right], axis=2)
-    back_parts = back.reshape(pictures, 64, 16, model_dim).transpose(1, 0, 2, 3)[:, None, :, None]
-    returned = lax.all_to_all(back_parts, ("row", "col"), split_axis=0, concat_axis=1, tiled=True)
-    grad_skip = returned_to_tile(returned, n_tiles, rows_here, cols_here)
-    flat_grad = grad_skip.reshape(-1, model_dim)
-    grad_proj = transposed_dot(flat_act, flat_grad)
-    grad_act = jnp.dot(flat_grad, w_proj.T, preferred_element_type=jnp.float32)
-    grad_act = grad_act.reshape(pictures, rows_here, cols_here, expand_dim)
-    grad_pre = (grad_act * slope.reshape(grad_act.shape).astype(jnp.float32)).astype(jnp.bfloat16)
-    grad_pre_pad = pad_tile(grad_pre, 1)
-    grad_kernel = kernel_grad(grad_pre, padded, rows_here, cols_here)
-    grad_expanded = depthwise_back(grad_pre_pad, depth_kernel, rows_here, cols_here).astype(
-        jnp.bfloat16
-    )
-    grad_kernel, grad_proj, grad_wqkv, grad_out, grad_gain = lax.psum(
-        (grad_kernel, grad_proj, grad_wqkv, grad_out, grad_gain), ("dp", "row", "col")
+    scale = 1.0 / math.sqrt(2 * lax.axis_size("dp") * TILES * cells)
+    ge, gs, gkern, gproj, gwqkv, gout, ggain = backward(
+        back, act, slope, x, ends, columns, kern, w_proj, grad_wqkv, grad_out, grad_gain, scale
     )
     return (
-        grad_expanded[:, None],
-        grad_skip[:, None],
-        grad_kernel * factor,
-        grad_proj * factor,
-        grad_wqkv * factor,
-        grad_out * factor,
-        grad_gain * factor,
+        ge.reshape(2, 1, ROWS, COLS, EXPAND),
+        gs.reshape(2, 1, ROWS, COLS, WIDTH),
+        gkern.reshape(3, 3, EXPAND),
+        gproj,
+        gwqkv,
+        gout,
+        ggain.reshape(WIDTH),
     )
 
 
 def solution(mesh):
-    placed = (
-        P("dp", ("row", "col"), None, None, None),
-        P("dp", ("row", "col"), None, None, None),
-        P("dp", ("row", "col"), None, None, None),
-        P(),
-        P(),
-        P(),
-        P(),
-        P(),
-    )
+    tiled = P("dp", ("row", "col"), None, None, None)
     return jax.shard_map(
         on_device,
         mesh=mesh,
-        in_specs=placed,
-        out_specs=(
-            P("dp", ("row", "col"), None, None, None),
-            P("dp", ("row", "col"), None, None, None),
-            P(),
-            P(),
-            P(),
-            P(),
-            P(),
-        ),
+        in_specs=(tiled, tiled, tiled, P(), P(), P(), P(), P()),
+        out_specs=(tiled, tiled, P(), P(), P(), P(), P()),
         check_vma=False,
     )

time: 384 us -> 173 us (0.45)
  waiting for transfers between devices: 129 us -> 0 us
  Pallas kernels: 78 us -> 154 us
  blocking collectives: 68.7 us -> 0 us
  other arithmetic: 39.3 us -> 0 us
  matrix products: 25.4 us -> 0 us
  starting transfers between devices: 20.6 us -> 0 us
  between operations: 14.4 us -> 0.77 us
  local copies, waits for them, and re-layouts: 8.44 us -> 17.8 us
    psum x1 -> x0, waiting for transfers between devices: 120 us -> none  [on_device(): lax.psum((grad_kernel, grad_proj, grad_wqkv, grad_out, grad_gain), ('dp',...]
    pallas_call x0 -> x1, Pallas kernels: none -> 76.2 us  [backward(): pl.pallas_call(kernel, out_shape=(jax.ShapeDtypeStruct((2, cells, EXPAND)...]
    psum x1 -> x0, blocking collectives: 68.7 us -> none  [on_device(): lax.psum((grad_kernel, grad_proj, grad_wqkv, grad_out, grad_gain), ('dp',...]
    dot_general x2 -> x0, matrix products: 25.4 us -> none  [the longest x1 20.9 us: on_device(): grad_act = jnp.dot(flat_grad, w_proj.T, preferred_element_type=jnp.float32)]
    concatenate x3 -> x0, other arithmetic: 16.9 us -> none  [the longest x1 9.26 us: on_device(): padded = jnp.concatenate([left, tall, right], axis=2)]
    unnamed x1 -> x0, other arithmetic: 13.4 us -> none
    unnamed x38, local copies, waits for them, and re-layouts: 2.52 us -> 14.8 us
    all_to_all x1 -> x0, starting transfers between devices: 10.3 us -> none  [on_device(): lax.all_to_all(back_parts, ('row', 'col'), split_axis=0, concat_axis=1, t...]
  transfers between devices with their start and end apart: 6 -> 0, of which waited for: 4 -> 0; matrix products, arithmetic and copies ran while one was open for 10% -> 0% of each run, Pallas kernels for 0% -> 0%
where the time goes in v2:
time: 173 us
  Pallas kernels  154 us (89%)
  local copies, waits for them, and re-layouts  17.8 us (10%)
    pallas_call x1, Pallas kernels, backward(): pl.pallas_call(kernel, out_shape=(jax.ShapeDtypeStruct((2, cells, EXPAND)...  76.2 us
    pallas_call x1, Pallas kernels, forward(): pl.pallas_call(forward_kernel, out_shape=(jax.ShapeDtypeStruct((2, cells,...  53.8 us
    pallas_call x1, Pallas kernels, attention(): pl.pallas_call(attention_kernel, out_shape=(jax.ShapeDtypeStruct((2, 1024...  24 us
    unnamed x38, local copies, waits for them, and re-layouts  14.8 us

profile of v2, /device:TPU:1, one launch (start us, length us, event | category | flops | bytes accessed | tf_op | source)
XLA Modules:
  0.0 172.7 jit_solution(1250057298611663815)
XLA Ops:
  0.6 0.0 copy-start.6
  0.6 0.0 copy-start.8
  0.7 0.0 copy-start.7
  0.7 0.0 copy-start.4
  0.7 0.0 copy-start.9
  0.7 1.5 reshape.40.kern_ref.refs_6_
  2.2 53.8 %forward.1 = (bf16[2,1024,1024]{2,1,0:T(8,128)(2,1)}, bf16[2,1024,1024]{2,1,0:T(8,128)(2,1)}, bf16[2,1024,256]{2,1,0:T(8,128)(2,1)}, bf16[2,1024,256]{2,1,0:T(8,...) custom-call(bf16[2,32,32,1024]{3,2,1,0:T(8,128)(2,1)} %bitcast.12, ...), custom_call_target="tpu_custom_call" | custom-call | tf_op jit(solution)/shard_map/forward/pallas_call | solution.py:322
  56.0 0.0 copy-done.6
  56.1 0.0 copy-done.8
  56.1 0.0 copy-done.7
  56.1 0.0 copy-done.4
  56.1 0.0 copy-done.9
  56.1 0.0 copy-start.1
  56.1 1.2 copy-done.1
  57.3 0.0 copy-start.2
  57.3 1.2 copy-done.2
  58.5 24.0 %attention.1 = (bf16[2,1024,256]{2,1,0:T(8,128)(2,1)S(1)}, f32[768,256]{1,0:T(8,128)S(1)}, f32[256,256]{1,0:T(8,128)S(1)}, f32[1,256]{1,0:T(1,128)S(1)}) custom-call(bf16[2,1024,256]{2,1,0:T(8,128)(2,1)S(1)} %copy-done.1, bf16[2,1024,256]{2,1,0:T(8,128)(2,1)S(1)} %copy-done.2, f32[1,256]{1,0:T(1,128)S(1)} %bitcast.11, bf16[256,768]{1,0:T(8,128)(2,1)S(1)} %copy-done.4, ...), custom_call_target="tpu_custom_call" | custom-call | tf_op jit(solution)/shard_map/attention/pallas_call | solution.py:450
  82.6 0.0 copy-start
  82.6 1.0 copy-done
  83.6 0.0 copy-start.3
  83.6 0.9 copy-done.3
  84.4 0.0 copy-start.5
  84.4 0.7 copy-done.5
  85.1 0.0 copy-start.10
  85.1 0.6 copy-done.10
  85.7 76.2 %backward.1 = (bf16[2,1024,1024]{2,1,0:T(8,128)(2,1)}, bf16[2,1024,256]{2,1,0:T(8,128)(2,1)}, f32[9,1024]{1,0:T(8,128)}, f32[1024,256]{1,0:T(8,128)}, f32[256,76...) custom-call(bf16[2,1024,256]{2,1,0:T(8,128)(2,1)} %copy-done, bf16[2,1024,1024]{2,1,0:T(8,128)(2,1)} %get-tuple-element.27.refs_1_, ...), custom_call_target="tpu_custom_call" | custom-call | tf_op jit(solution)/shard_map/backward/pallas_call | solution.py:788
  161.9 1.5 reshape.44
  163.4 0.0 copy-start.12
  163.4 0.0 copy-start.11
  163.4 5.2 %copy.25 = bf16[2,1,32,32,1024]{4,3,2,1,0:T(8,128)(2,1)} copy(bf16[2,1,32,32,1024]{4,3,2,1,0:T(8,128)(2,1)} %bitcast.14) | data formatting | bytes 8388608
  168.6 0.0 copy-done.12
  168.6 0.0 copy-start.13
  168.6 0.0 copy-start.14
  168.6 0.0 copy-start.15
  168.6 1.0 copy.26
  169.6 0.0 copy-done.11
  169.6 1.0 copy.27
  170.5 0.0 copy-done.13
  170.5 0.9 copy.28
  171.4 0.0 copy-done.14
  171.4 0.7 copy.29
  172.1 0.0 copy-done.15
  172.1 0.6 copy.30
Async XLA Ops:
  0.6 55.4 %copy-start.6 = (bf16[512,256]{1,0:T(8,128)(2,1)S(1)}, bf16[512,256]{1,0:T(8,128)(2,1)}, u32[]{:S(2)}) copy-start(bf16[512,256]{1,0:T(8,128)(2,1)} %constant.5.clone.mask_ref) | copy-start | bytes 786436
  0.6 55.4 %copy-start.8 = (bf16[256,256]{1,0:T(8,128)(2,1)S(1)}, bf16[256,256]{1,0:T(8,128)(2,1)}, u32[]{:S(2)}) copy-start(bf16[256,256]{1,0:T(8,128)(2,1)} %constant.4.clone.perm_ref) | copy-start | bytes 393220
  0.7 55.4 %copy-start.7 = (bf16[256,256]{1,0:T(8,128)(2,1)S(1)}, bf16[256,256]{1,0:T(8,128)(2,1)}, u32[]{:S(2)}) copy-start(bf16[256,256]{1,0:T(8,128)(2,1)} %wout_ref.1) | copy-start | bytes 393220
  0.7 55.4 %copy-start.4 = (bf16[256,768]{1,0:T(8,128)(2,1)S(1)}, bf16[256,768]{1,0:T(8,128)(2,1)}, u32[]{:S(2)}) copy-start(bf16[256,768]{1,0:T(8,128)(2,1)} %wqkv_ref.1) | copy-start | bytes 1179652
  0.7 55.4 %copy-start.9 = (f32[256]{0:T(256)S(1)}, f32[256]{0:T(256)}, u32[]{:S(2)}) copy-start(f32[256]{0:T(256)} %param.15) | copy-start | bytes 3076
  56.1 1.2 copy-start.1
  57.3 1.2 copy-start.2
  82.6 1.0 copy-start
  83.6 0.9 copy-start.3
  84.4 0.7 copy-start.5
  85.1 0.6 copy-start.10
  163.4 5.2 %copy-start.12 = (bf16[2,1024,256]{2,1,0:T(8,128)(2,1)S(1)}, bf16[2,1024,256]{2,1,0:T(8,128)(2,1)}, u32[]{:S(2)}) copy-start(bf16[2,1024,256]{2,1,0:T(8,128)(2,1)} %get-tuple-element.35) | copy-start | bytes 3145732
  163.4 6.1 %copy-start.11 = (f32[1024,256]{1,0:T(8,128)S(1)}, f32[1024,256]{1,0:T(8,128)}, u32[]{:S(2)}) copy-start(f32[1024,256]{1,0:T(8,128)} %get-tuple-element.58) | copy-start | bytes 3145732
  168.6 2.0 %copy-start.13 = (f32[256,768]{1,0:T(8,128)S(1)}, f32[256,768]{1,0:T(8,128)}, u32[]{:S(2)}) copy-start(f32[256,768]{1,0:T(8,128)} %get-tuple-element.59) | copy-start | bytes 2359300
  168.6 2.8 %copy-start.14 = (f32[256,256]{1,0:T(8,128)S(1)}, f32[256,256]{1,0:T(8,128)}, u32[]{:S(2)}) copy-start(f32[256,256]{1,0:T(8,128)} %get-tuple-element.60) | copy-start | bytes 786436
  168.6 3.5 %copy-start.15 = (f32[1,256]{1,0:T(1,128)S(1)}, f32[1,256]{1,0:T(1,128)}, u32[]{:S(2)}) copy-start(f32[1,256]{1,0:T(1,128)} %get-tuple-element.40) | copy-start | bytes 3076

commit v3 on v0

v3 whole, which is shorter than its diff:
```python
import math

import jax
import jax.numpy as jnp
import numpy as np
from jax import lax
from jax.experimental import pallas as pl
from jax.experimental.pallas import tpu as pltpu
from jax.sharding import PartitionSpec as P

GRID = 8
TILES = 64
ROWS = 32
COLS = 32
CELLS = ROWS * COLS
LANES = 128
WIDTH = 256
EXPAND = 1024
LANE_BLOCKS = EXPAND // LANES
STRIP = 4
STRIPS = ROWS // STRIP
STRIP_CELLS = STRIP * COLS
BAND = 8
BANDS = ROWS // BAND
BAND_CELLS = BAND * COLS
BAND_TILES = TILES // BANDS
SHARE = CELLS // TILES
F32 = jnp.float32
BF16 = jnp.bfloat16
MESH_ID = pl.DeviceIdType.MESH
GELU_1 = math.sqrt(2.0 / math.pi)
GELU_3 = GELU_1 * 0.044715
SIDES = ((0, -1), (0, 1))
ENDS = ((-1, 0), (1, 0))
CORNERS = ((-1, -1), (-1, 1), (1, -1), (1, 1))
AROUND = SIDES + ENDS + CORNERS


def dot(a, b):
    return lax.dot_general(a, b, (((1,), (0,)), ((), ())), preferred_element_type=F32)


def dot_t(a, b):
    return lax.dot_general(a, b, (((1,), (1,)), ((), ())), preferred_element_type=F32)


def dot_tl(a, b):
    return lax.dot_general(a, b, (((0,), (0,)), ((), ())), preferred_element_type=F32)


def tile_id(tile):
    return {"row": tile // 32, "col": lax.rem(tile, 32)}


def times(start, count, size=None):
    return pl.ds(pl.multiple_of(start * count, count), size or count)


def loop(begin, end, body):
    def one(i, carry):
        body(i)
        return carry

    lax.fori_loop(begin, end, one, 0)


def neighbours(me):
    tile_row, tile_col = me // GRID, lax.rem(me, GRID)
    return {
        (down, right): lax.rem(tile_row + down + GRID, GRID) * GRID + lax.rem(tile_col + right + GRID, GRID)
        for down in (-1, 0, 1)
        for right in (-1, 0, 1)
        if (down, right) != (0, 0)
    }


def rim_copies(me, picture, turn, grid_ref, sides_out, sides_in, corners_out, corners_in, send_sem, recv_sem):
    around = neighbours(me)
    copies = []
    for n, (down, right) in enumerate(AROUND):
        if down == 0:
            source = sides_out.at[(right + 1) // 2, picture]
            target = sides_in.at[(1 - right) // 2, picture]
        elif right == 0:
            source = grid_ref.at[picture, 1 if down < 0 else ROWS]
            target = grid_ref.at[picture, ROWS + 1 if down < 0 else 0]
        else:
            place = CORNERS.index((down, right))
            source = corners_out.at[picture, place]
            target = corners_in.at[picture, 3 - place]
        copies.append(
            pltpu.make_async_remote_copy(
                src_ref=source,
                dst_ref=target,
                send_sem=send_sem.at[turn, picture, n],
                recv_sem=recv_sem.at[turn, picture, n],
                device_id=tile_id(around[down, right]),
                device_id_type=MESH_ID,
            )
        )
    return copies


def collect_sides(picture, grid_ref, sides_out, corners_out):
    for side in range(2):
        for start in range(0, ROWS, 16):
            window = grid_ref[picture, 1 + start : 17 + start, 16 * side : 16 * side + 16, :]
            column = window.astype(F32)[:, 15 * side, :]
            sides_out[side, picture, start : start + 16, :] = column.astype(BF16)
    for place, (down, right) in enumerate(CORNERS):
        edge = 0 if down < 0 else 16
        row = 0 if down < 0 else 15
        one = sides_out[(right + 1) // 2, picture, edge : edge + 16, :].astype(F32)[row : row + 1]
        corners_out[picture, place] = jnp.concatenate([one, jnp.zeros((15, EXPAND), F32)], axis=0).astype(BF16)


def clear_outside(me, picture, grid_ref, sides_in, corners_in):
    tile_row, tile_col = me // GRID, lax.rem(me, GRID)
    none = jnp.zeros((16, EXPAND), BF16)
    for side, last in ((0, 0), (1, GRID - 1)):

        @pl.when(tile_col == last)
        def _():
            sides_in[side, picture] = jnp.zeros((ROWS, EXPAND), BF16)
            corners_in[picture, side] = none
            corners_in[picture, 2 + side] = none

    for end, last in ((0, 0), (1, GRID - 1)):

        @pl.when(tile_row == last)
        def _():
            grid_ref[picture, (ROWS + 1) * end] = jnp.zeros((COLS, EXPAND), BF16)
            corners_in[picture, 2 * end] = none
            corners_in[picture, 2 * end + 1] = none


def column_stack(picture, sides_in, corners_in, columns):
    blank = jnp.zeros((7, EXPAND), F32)
    for side in range(2):
        above = corners_in[picture, side].astype(F32)[0:1]
        below = corners_in[picture, 2 + side].astype(F32)[0:1]
        columns[side, picture, 0:8] = jnp.concatenate([blank, above], axis=0)
        columns[side, picture, 8 : 8 + ROWS] = sides_in[side, picture].astype(F32)
        columns[side, picture, 40:48] = jnp.concatenate([below, blank], axis=0)


def column_terms(picture, columns, weights, terms):
    for side in range(2):
        total = None
        for row_off in range(3):
            term = weights(row_off, 2 * side) * columns[side, picture, 7 + row_off : 7 + row_off + ROWS, :]
            total = term if total is None else total + term
        for strip in range(STRIPS):
            terms[side, picture, strip, 0:STRIP] = total[STRIP * strip : STRIP * strip + STRIP]


def convolve(rows, weights, left, right):
    spot = lax.broadcasted_iota(jnp.int32, (STRIP, COLS, LANES), 1)
    parts = []
    for col_off in range(3):
        total = None
        for row_off in range(3):
            term = weights[3 * row_off + col_off][None, :, :] * rows[row_off : row_off + STRIP]
            total = term if total is None else total + term
        parts.append(total)
    from_left = jnp.where(spot == 0, left[:, None, :], pltpu.roll(parts[0], 1, 1))
    from_right = jnp.where(spot == COLS - 1, right[:, None, :], pltpu.roll(parts[2], COLS - 1, 1))
    return parts[1] + from_left + from_right


def pick_heads(full, lane):
    halves = []
    for half in range(2):
        cols = slice(128 * half, 128 * half + 128)
        kept = full[256 * half : 256 * half + 64, cols]
        for h in range(1, 4):
            start = 256 * half + 64 * h
            kept = jnp.where(lane == h, full[start : start + 64, cols], kept)
        halves.append(kept)
    return jnp.concatenate(halves, axis=1)


def attend(mix, cot, gain, wqkv_ref, wout_ref, mask_ref, gw_ref, go_ref, gg_ref):
    scale = 1.0 / math.sqrt(32.0)
    lane = lax.broadcasted_iota(jnp.int32, (64, 128), 1) // 32
    mix = mix.astype(F32)
    inv = lax.rsqrt(jnp.mean(mix * mix, axis=-1, keepdims=True) + 1e-6)
    mi = mix * inv
    normed = (mi * gain).astype(BF16)
    qkv = dot(normed, wqkv_ref[...]).astype(BF16)
    gatt = dot_t(cot, wout_ref[...]).astype(BF16)
    att, gqs, gks, gvs = [], [], [], []
    for i in range(4):
        r = slice(64 * i, 64 * i + 64)
        q, k, v = qkv[r, 0:256], qkv[r, 256:512], qkv[r, 512:768]
        qexp = jnp.concatenate([q] * 8, axis=0) * mask_ref[...]
        doexp = jnp.concatenate([gatt[r]] * 8, axis=0) * mask_ref[...]
        st = dot_t(k, qexp) * scale
        e = jnp.exp(st - jnp.max(st, axis=0, keepdims=True))
        p = e * (1.0 / jnp.sum(e, axis=0, keepdims=True))
        pb = p.astype(BF16)
        dp = dot_t(v, doexp)
        ds = (p * (dp - jnp.sum(dp * p, axis=0, keepdims=True)) * scale).astype(BF16)
        att.append(pick_heads(dot_tl(pb, v), lane).astype(BF16))
        gqs.append(pick_heads(dot_tl(ds, k), lane).astype(BF16))
        gks.append(dot(ds, qexp).astype(BF16))
        gvs.append(dot(pb, doexp).astype(BF16))
    gqkv = [jnp.concatenate(x, axis=0) for x in (gqs, gks, gvs)]
    go_ref[...] += dot_tl(jnp.concatenate(att, axis=0), cot)
    normed_t = normed.T
    gn = jnp.zeros((256, 256), F32)
    for n in range(3):
        gw_ref[256 * n : 256 * n + 256] += dot(normed_t, gqkv[n])
        gn = gn + dot_t(gqkv[n], wqkv_ref[:, 256 * n : 256 * n + 256])
    gg_ref[...] += jnp.sum(gn * mi, axis=0, keepdims=True)
    scaled = gn * gain
    mean = jnp.mean(scaled * mix, axis=-1, keepdims=True)
    return (cot.astype(F32) + inv * scaled - mi * (inv * inv * mean)).astype(BF16)


def whole_kernel(
    x_hbm, skip_ref, cot_hbm, kern_ref, wproj_ref, gain_ref, wqkv_ref, wout_ref, perm_ref, mask_ref,
    ge_hbm, gs_hbm, whole_hbm, extra_out,
    xgrid, ggrid, act, dg, mix, got_mix, got_cot, mix_s, cot_s, back, gs,
    sides_out, sides_in, corners_out, corners_in, xcols, gcols, terms, gsides_out, gsides_in, gcorners_out, gcorners_in,
    gproj_t, gkern, gw_ref, go_ref, gg_ref, part_out, core_in, y_out, y_in, small_out, small_in, whole,
    ex_a, ex_b, ex_c,
    load_sem, rim_send, rim_recv, cot_send, cot_recv, mix_send, mix_recv, back_send, back_recv, own_sem, store_sem,
    core_send, core_recv, y_send, y_recv, z_send, z_recv, g_send, g_recv, gy_send, gy_recv,
    ey_send, ey_recv, ez_send, ez_recv,
):
    me = my_tile()
    tile_row, tile_col = me // GRID, lax.rem(me, GRID)
    dp, row, col = lax.axis_index("dp"), lax.axis_index("row"), lax.axis_index("col")
    core, chip = lax.rem(col, 2), col // 2
    q = dp * 2 + row
    mate = {"col": col + 1 - 2 * core}
    own = times(me, SHARE)

    def weight(n, lanes=slice(None)):
        return kern_ref[n // 3, n % 3 : n % 3 + 1, lanes]

    loads = [pltpu.make_async_copy(x_hbm.at[p], xgrid.at[p, pl.ds(1, ROWS)], load_sem.at[p]) for p in range(2)]
    for copy in loads:
        copy.start()
    barrier = pltpu.get_barrier_semaphore()

    def greet(i):
        pl.semaphore_signal(barrier, inc=1, device_id=tile_id(lax.rem(me + i, TILES)), device_id_type=MESH_ID)

    loop(1, TILES, greet)
    for n in range(2):
        pl.semaphore_signal(
            barrier, inc=1, device_id={"dp": 1 - dp, "row": n, "col": col}, device_id_type=MESH_ID
        )
    loads[0].wait()
    collect_sides(0, xgrid, sides_out, corners_out)
    pl.semaphore_wait(barrier, TILES + 1)

    def rim_of(picture, turn):
        if turn == 0:
            refs = (xgrid, sides_out, sides_in, corners_out, corners_in)
        else:
            refs = (ggrid, gsides_out, gsides_in, gcorners_out, gcorners_in)
        return rim_copies(me, picture, turn, *refs, rim_send, rim_recv)

    for copy in rim_of(0, 0):
        copy.start()
    loads[1].wait()
    collect_sides(1, xgrid, sides_out, corners_out)
    for copy in rim_of(1, 0):
        copy.start()

    def cot_copy(target, slot):
        return pltpu.make_async_remote_copy(
            src_ref=cot_hbm.at[:, times(target, SHARE), :],
            dst_ref=got_cot.at[:, times(slot, SHARE), :],
            send_sem=cot_send.at[target],
            recv_sem=cot_recv.at[slot],
            device_id=tile_id(target),
            device_id_type=MESH_ID,
        )

    def mix_copy(picture, target, slot):
        return pltpu.make_async_remote_copy(
            src_ref=mix.at[picture, times(target, SHARE), :],
            dst_ref=got_mix.at[picture, times(slot, SHARE), :],
            send_sem=mix_send.at[picture, target],
            recv_sem=mix_recv.at[picture, slot],
            device_id=tile_id(target),
            device_id_type=MESH_ID,
        )

    def back_copy(picture, target, slot):
        return pltpu.make_async_remote_copy(
            src_ref=back.at[picture, times(target, SHARE), :],
            dst_ref=gs.at[picture, times(slot, SHARE), :],
            send_sem=back_send.at[picture, target],
            recv_sem=back_recv.at[picture, slot],
            device_id=tile_id(target),
            device_id_type=MESH_ID,
        )

    loop(1, TILES, lambda i: cot_copy(lax.rem(me + i, TILES), me).start())
    own_cot = pltpu.make_async_copy(cot_hbm.at[:, own, :], got_cot.at[:, own, :], own_sem.at[0])
    own_cot.start()


    def forward_picture(picture):
        rim = rim_of(picture, 0)
        for copy in rim:
            copy.wait_recv()
        clear_outside(me, picture, xgrid, sides_in, corners_in)
        column_stack(picture, sides_in, corners_in, xcols)
        column_terms(picture, xcols, lambda a, c: weight(3 * a + c), terms)

        def do_band(step):
            band = lax.rem(step + tile_row // 2, BANDS)
            cells = times(band, BAND_CELLS)

            def do_block(index):
                strip = band * 2 + index // LANE_BLOCKS
                lanes = times(lax.rem(index, LANE_BLOCKS), LANES)
                rows = xgrid[picture, pl.ds(strip * STRIP, STRIP + 2), :, lanes].astype(F32)
                pre = convolve(
                    rows,
                    [weight(n, lanes) for n in range(9)],
                    terms[0, picture, strip, 0:STRIP, lanes],
                    terms[1, picture, strip, 0:STRIP, lanes],
                )
                square = pre * pre
                tanh = jnp.tanh(pre * (GELU_1 + GELU_3 * square))
                half = 0.5 * pre
                activated = half + half * tanh
                slope = (0.5 + 0.5 * tanh) + half * (1.0 - tanh * tanh) * (GELU_1 + (3.0 * GELU_3) * square)
                here = times(strip, STRIP_CELLS)
                act[picture, here, lanes] = activated.astype(BF16).reshape(STRIP_CELLS, LANES)
                dg[picture, here, lanes] = slope.astype(BF16).reshape(STRIP_CELLS, LANES)

            loop(0, 2 * LANE_BLOCKS, do_block)
            projected = dot(act[picture, cells, :], wproj_ref[...])
            mix[picture, cells, :] = (skip_ref[picture, cells, :].astype(F32) + projected).astype(BF16)

            def send_mix(i):
                target = band * BAND_TILES + lax.rem(me + i, BAND_TILES)

                @pl.when(target != me)
                def _():
                    mix_copy(picture, target, me).start()

            loop(0, BAND_TILES, send_mix)

        loop(0, BANDS, do_band)

    loop(0, 2, forward_picture)


    gw_ref[...] = jnp.zeros_like(gw_ref)
    go_ref[...] = jnp.zeros_like(go_ref)
    gg_ref[...] = jnp.zeros_like(gg_ref)
    gproj_t[...] = jnp.zeros_like(gproj_t)
    own_cot.wait()
    loop(1, TILES, lambda i: cot_copy(lax.rem(me + i, TILES), lax.rem(me + i, TILES)).wait_recv())

    def attend_picture(picture):
        own_mix = pltpu.make_async_copy(mix.at[picture, own, :], got_mix.at[picture, own, :], own_sem.at[1])
        own_mix.start()
        perm = perm_ref[...]
        for b in range(4):
            r = slice(256 * b, 256 * b + 256)
            cot_s[:, 16 * b : 16 * b + 16, :] = dot(perm, got_cot[picture, r, :]).astype(BF16).reshape(16, 16, 256)
        loop(1, TILES, lambda i: mix_copy(picture, lax.rem(me + i, TILES), lax.rem(me + i, TILES)).wait_recv())
        own_mix.wait()
        for b in range(4):
            r = slice(256 * b, 256 * b + 256)
            mix_s[:, 16 * b : 16 * b + 16, :] = dot(perm, got_mix[picture, r, :]).astype(BF16).reshape(16, 16, 256)

        def block(b):
            groups = pl.ds(b * 4, 4)
            out = attend(
                mix_s[groups].reshape(256, 256), cot_s[groups].reshape(256, 256), gain_ref[...],
                wqkv_ref, wout_ref, mask_ref, gw_ref, go_ref, gg_ref,
            )
            cot_s[groups] = out.reshape(4, 64, 256)

        loop(0, 4, block)
        for b in range(4):
            rows = cot_s[:, 16 * b : 16 * b + 16, :].reshape(256, 256)
            back[picture, 256 * b : 256 * b + 256] = dot(perm, rows).astype(BF16)

        def send_back(i):
            target = lax.rem(tile_row + GRID - i // GRID, GRID) * GRID + lax.rem(
                tile_col + GRID - lax.rem(i, GRID), GRID
            )
            back_copy(picture, target, me).start()

        loop(1, TILES, send_back)
        own_back = pltpu.make_async_copy(back.at[picture, own, :], gs.at[picture, own, :], own_sem.at[2])
        own_back.start()
        own_back.wait()

    loop(0, 2, attend_picture)


    def core_copy(half):
        return pltpu.make_async_remote_copy(
            src_ref=part_out.at[pl.ds(2 * half, 2), 1 - core],
            dst_ref=core_in.at[pl.ds(2 * half, 2)],
            send_sem=core_send.at[half],
            recv_sem=core_recv.at[half],
            device_id=mate,
            device_id_type=MESH_ID,
        )

    def remote(source, target, send, recv, device):
        return pltpu.make_async_remote_copy(
            src_ref=source, dst_ref=target, send_sem=send, recv_sem=recv, device_id=device, device_id_type=MESH_ID
        )

    def y_id(n):
        return {"dp": n // 2, "row": lax.rem(n, 2)}

    def z_id(n):
        return {"col": n * 2 + core}

    def y_copy(to, slot):
        return remote(y_out.at[to], y_in.at[slot], y_send.at[to], y_recv.at[slot], y_id(to))

    def z_copy(to, slot):
        return remote(small_out.at[times(to, 16)], small_in.at[slot], z_send.at[to], z_recv.at[slot], z_id(to))

    def g_copy(to, slot):
        return remote(
            whole.at[q, core, times(chip, 16)], whole.at[q, core, times(slot, 16)],
            g_send.at[to], g_recv.at[slot], z_id(to),
        )

    def gy_copy(to, slot):
        return remote(whole.at[q, core], whole.at[slot, core], gy_send.at[to], gy_recv.at[slot], y_id(to))

    def ey_copy(to, slot):
        return remote(ex_b.at[q], ex_b.at[slot], ey_send.at[to], ey_recv.at[slot], y_id(to))

    def ez_copy(to, slot):
        return remote(ex_c.at[chip], ex_c.at[slot], ez_send.at[to], ez_recv.at[slot], z_id(to))

    def others(count, mine, action):
        loop(1, count, lambda i: action(lax.rem(mine + i, count)))

    def core_sum(half):
        core_copy(half).wait_recv()
        for n in (2 * half, 2 * half + 1):
            y_out[n] = (part_out[n, core].astype(F32) + core_in[n].astype(F32)).astype(BF16)

            @pl.when(q != n)
            def _():
                y_copy(n, q).start()

    for n in range(4):
        block = gw_ref[256 * n : 256 * n + 256] if n < 3 else go_ref[...]
        part_out[2 + n // 2, n % 2] = block.astype(BF16)
    core_copy(1).start()


    spot = lax.broadcasted_iota(jnp.int32, (STRIP, COLS, LANES), 1)
    gkern[...] = jnp.zeros_like(gkern)

    def back_picture(picture):
        def do_band(step):
            band = lax.rem(step + tile_row // 2, BANDS)
            cells = times(band, BAND_CELLS)

            def arrived(i):
                source = band * BAND_TILES + i

                @pl.when(source != me)
                def _():
                    back_copy(picture, source, source).wait_recv()

            loop(0, BAND_TILES, arrived)
            flat = gs[picture, cells, :]
            flat_t = flat.T
            for n in range(4):
                lanes = slice(256 * n, 256 * n + 256)
                grad_act = dot_t(flat, wproj_ref[lanes, :])
                grad_pre = (grad_act * dg[picture, cells, lanes].astype(F32)).astype(BF16)
                ggrid[picture, pl.ds(1 + band * BAND, BAND), :, lanes] = grad_pre.reshape(BAND, COLS, 256)
                gproj_t[:, lanes] += dot(flat_t, act[picture, cells, lanes])

        loop(0, BANDS, do_band)
        collect_sides(picture, ggrid, gsides_out, gcorners_out)
        for copy in rim_of(picture, 1):
            copy.start()

        @pl.when(picture == 0)
        def _():
            core_sum(1)

        @pl.when(picture == 1)
        def _():
            for n in range(4):
                part_out[n // 2, n % 2] = gproj_t[:, 256 * n : 256 * n + 256].T.astype(BF16)
            core_copy(0).start()

        def kernel_block(block):
            lanes = times(block, LANES)

            def one(strip, sums):
                grads = ggrid[picture, pl.ds(1 + strip * STRIP, STRIP), :, lanes].astype(F32)
                rows = xgrid[picture, pl.ds(strip * STRIP, STRIP + 2), :, lanes].astype(F32)
                shifted = (
                    jnp.where(spot == COLS - 1, 0.0, pltpu.roll(grads, COLS - 1, 1)),
                    grads,
                    jnp.where(spot == 0, 0.0, pltpu.roll(grads, 1, 1)),
                )
                new = []
                for row_off in range(3):
                    for col_off in range(3):
                        product = shifted[col_off] * rows[row_off : row_off + STRIP]
                        product = product.reshape(STRIP * 4, 8, LANES).sum(axis=0)
                        new.append(sums[3 * row_off + col_off] + product)
                return tuple(new)

            sums = lax.fori_loop(0, STRIPS, one, tuple(jnp.zeros((8, LANES), F32) for _ in range(9)))
            for n in range(9):
                gkern[n : n + 1, lanes] += jnp.sum(sums[n], axis=0, keepdims=True)

        loop(0, LANE_BLOCKS // 2, kernel_block)

        @pl.when(picture == 1)
        def _():
            core_sum(0)

        loop(LANE_BLOCKS // 2, LANE_BLOCKS, kernel_block)
        for row_off in range(3):
            for side in range(2):
                n = 3 * row_off + 2 * side
                beside = xcols[side, picture, 7 + row_off : 7 + row_off + ROWS, :]
                gkern[n : n + 1, :] += jnp.sum(
                    gsides_out[side, picture].astype(F32) * beside, axis=0, keepdims=True
                )

    loop(0, 2, back_picture)
    gs_store = pltpu.make_async_copy(gs, gs_hbm, own_sem.at[3])
    gs_store.start()


    extra = [gkern[0:9, 256 * n : 256 * n + 256] for n in range(4)]
    extra = jnp.concatenate(extra + [gg_ref[...], jnp.zeros((11, 256), F32)], axis=0).astype(BF16)
    ex_a[core] = extra
    ex_core = remote(ex_a.at[core], ex_a.at[core], core_send.at[2], core_recv.at[2], mate)
    ex_core.start()

    def total_of(ref, count):
        total = ref[0].astype(F32)
        for n in range(1, count):
            total = total + ref[n].astype(F32)
        return total

    others(4, q, lambda n: y_copy(n, n).wait_recv())
    y_in[q] = y_out[q]
    small_out[...] = total_of(y_in, 4).astype(BF16)
    others(16, chip, lambda n: z_copy(n, chip).start())
    ex_core.wait_recv()
    ex_b[q] = total_of(ex_a, 2).astype(BF16)
    others(4, q, lambda n: ey_copy(n, q).start())

    def store_copy(picture, band):
        cells = times(band, BAND_CELLS)
        return pltpu.make_async_copy(dg.at[picture, cells, :], ge_hbm.at[picture, cells, :], store_sem.at[picture, band])

    def last_start(picture):
        for copy in rim_of(picture, 1):
            copy.wait_recv()
        clear_outside(me, picture, ggrid, gsides_in, gcorners_in)
        column_stack(picture, gsides_in, gcorners_in, gcols)
        column_terms(picture, gcols, lambda a, c: weight(8 - 3 * a - c), terms)

    def last_bands(picture, begin, end):
        def do_band(band):
            def do_block(index):
                strip = band * 2 + index // LANE_BLOCKS
                lanes = times(lax.rem(index, LANE_BLOCKS), LANES)
                rows = ggrid[picture, pl.ds(strip * STRIP, STRIP + 2), :, lanes].astype(F32)
                total = convolve(
                    rows,
                    [weight(8 - n, lanes) for n in range(9)],
                    terms[0, picture, strip, 0:STRIP, lanes],
                    terms[1, picture, strip, 0:STRIP, lanes],
                )
                dg[picture, times(strip, STRIP_CELLS), lanes] = total.astype(BF16).reshape(STRIP_CELLS, LANES)

            loop(0, 2 * LANE_BLOCKS, do_block)
            store_copy(picture, band).start()

        loop(begin, end, do_band)

    last_start(0)
    last_bands(0, 0, 4)

    others(16, chip, lambda n: z_copy(n, n).wait_recv())
    small_in[chip] = small_out[times(chip, 16)]
    whole[q, core, times(chip, 16)] = total_of(small_in, 16).astype(BF16)
    others(16, chip, lambda n: g_copy(n, chip).start())
    others(4, q, lambda n: ey_copy(n, n).wait_recv())
    ex_c[chip] = total_of(ex_b, 4).astype(BF16)
    others(16, chip, lambda n: ez_copy(n, chip).start())

    last_start(1)
    last_bands(1, 0, 3)

    others(16, chip, lambda n: g_copy(n, n).wait_recv())
    others(4, q, lambda n: gy_copy(n, q).start())

    last_bands(1, 3, 4)

    others(16, chip, lambda n: ez_copy(n, n).wait_recv())
    extra_out[...] = total_of(ex_c, 16)


    def sent(i):
        peer = lax.rem(me + i, TILES)
        cot_copy(peer, peer).wait_send()
        for picture in range(2):
            mix_copy(picture, peer, peer).wait_send()
            back_copy(picture, peer, peer).wait_send()

    loop(1, TILES, sent)
    for turn in range(2):
        for picture in range(2):
            for copy in rim_of(picture, turn):
                copy.wait_send()
    for half in range(2):
        core_copy(half).wait_send()
    ex_core.wait_send()
    others(4, q, lambda n: y_copy(n, n).wait_send())
    others(4, q, lambda n: ey_copy(n, n).wait_send())
    others(16, chip, lambda n: z_copy(n, n).wait_send())
    others(16, chip, lambda n: g_copy(n, n).wait_send())
    others(16, chip, lambda n: ez_copy(n, n).wait_send())
    gs_store.wait()
    for picture in range(2):
        for band in range(BANDS):
            store_copy(picture, band).wait()
    others(4, q, lambda n: gy_copy(n, n).wait_recv())
    to_mate = remote(whole.at[:, core], whole.at[:, core], core_send.at[3], core_recv.at[3], mate)
    to_mate.start()
    others(4, q, lambda n: gy_copy(n, n).wait_send())
    to_mate.wait_recv()
    to_mate.wait_send()
    whole_store = pltpu.make_async_copy(whole, whole_hbm, own_sem.at[4])
    whole_store.start()
    whole_store.wait()


def my_tile():
    return lax.axis_index("row") * 32 + lax.axis_index("col")


def constants():
    perm = np.zeros((256, 256), np.float32)
    for a in range(16):
        for b in range(16):
            perm[a * 16 + b, b * 16 + a] = 1
    mask = np.kron(np.eye(8), np.ones((64, 32))).astype(np.float32)
    return jnp.asarray(perm, BF16), jnp.asarray(mask, BF16)


def whole_call(x, skip, cot, kern, wproj, gain, wqkv, wout):
    vmem = pl.BlockSpec(memory_space=pltpu.VMEM)
    anywhere = pl.BlockSpec(memory_space=pl.ANY)
    dma = pltpu.SemaphoreType.DMA

    def bf(*shape):
        return pltpu.VMEM(shape, BF16)

    def fl(*shape):
        return pltpu.VMEM(shape, F32)

    rims = [bf(2, 2, ROWS, EXPAND), bf(2, 2, ROWS, EXPAND), bf(2, 4, 16, EXPAND), bf(2, 4, 16, EXPAND)]
    return pl.pallas_call(
        whole_kernel,
        out_shape=(
            jax.ShapeDtypeStruct((2, CELLS, EXPAND), BF16),
            jax.ShapeDtypeStruct((2, CELLS, WIDTH), BF16),
            jax.ShapeDtypeStruct((4, 2, 256, 256), BF16),
            jax.ShapeDtypeStruct((48, 256), F32),
        ),
        in_specs=[anywhere, vmem, anywhere] + [vmem] * 7,
        out_specs=(anywhere, anywhere, anywhere, vmem),
        scratch_shapes=[
            bf(2, ROWS + 2, COLS, EXPAND), bf(2, ROWS + 2, COLS, EXPAND), bf(2, CELLS, EXPAND), bf(2, CELLS, EXPAND),
            bf(2, CELLS, WIDTH), bf(2, CELLS, WIDTH), bf(2, CELLS, WIDTH), bf(16, 64, WIDTH), bf(16, 64, WIDTH),
            bf(2, CELLS, WIDTH), bf(2, CELLS, WIDTH),
        ]
        + rims
        + [fl(2, 2, 48, EXPAND), fl(2, 2, 48, EXPAND), fl(2, 2, STRIPS, 8, EXPAND)]
        + rims
        + [
            fl(WIDTH, EXPAND), fl(16, EXPAND), fl(3 * WIDTH, WIDTH), fl(WIDTH, WIDTH), fl(1, WIDTH),
            bf(4, 2, 256, 256), bf(4, 256, 256), bf(4, 256, 256), bf(4, 256, 256),
            bf(256, 256), bf(16, 16, 256), bf(4, 2, 256, 256),
            bf(2, 48, 256), bf(4, 48, 256), bf(16, 48, 256),
            dma((2,)), dma((2, 2, 8)), dma((2, 2, 8)), dma((TILES,)), dma((TILES,)),
            dma((2, TILES)), dma((2, TILES)), dma((2, TILES)), dma((2, TILES)), dma((5,)), dma((2, BANDS)),
            dma((4,)), dma((4,)), dma((4,)), dma((4,)), dma((16,)), dma((16,)), dma((16,)), dma((16,)),
            dma((4,)), dma((4,)), dma((4,)), dma((4,)), dma((16,)), dma((16,)),
        ],
        compiler_params=pltpu.CompilerParams(
            collective_id=0, has_side_effects=True, vmem_limit_bytes=56 * 2**20
        ),
        name="whole",
    )(x, skip, cot, kern, wproj, gain, wqkv, wout, *constants())


def finish_kernel(
    ge_hbm, gs_hbm, whole_ref, extra_ref, ge_out, gs_out, gkern_out, gproj_out, gwqkv_out, gout_out, ggain_out, sems, *, scale
):
    copies = []
    for picture in range(2):
        for part in range(2):
            rows = pl.ds(512 * part, 512)
            copies.append(
                pltpu.make_async_copy(
                    ge_hbm.at[picture, rows], ge_out.at[picture, rows], sems.at[2 * picture + part]
                )
            )
    copies.append(pltpu.make_async_copy(gs_hbm, gs_out, sems.at[4]))
    for copy in copies:
        copy.start()
    for n in range(8):
        block = whole_ref[n // 2, n % 2].astype(F32) * scale
        if n < 4:
            gproj_out[256 * n : 256 * n + 256, :] = block
            some = extra_ref[9 * n : 9 * n + 9, :] * scale
            for row in range(3):
                gkern_out[row, :, 256 * n : 256 * n + 256] = some[3 * row : 3 * row + 3]
        elif n < 7:
            gwqkv_out[:, 256 * (n - 4) : 256 * (n - 4) + 256] = block
        else:
            gout_out[...] = block
    ggain_out[...] = extra_ref[36:37, :] * scale
    for copy in copies:
        copy.wait()


def finish(ge, gs, whole, extra, scale):
    vmem = pl.BlockSpec(memory_space=pltpu.VMEM)
    anywhere = pl.BlockSpec(memory_space=pl.ANY)

    def kernel(*refs):
        finish_kernel(*refs, scale=scale)

    return pl.pallas_call(
        kernel,
        out_shape=(
            jax.ShapeDtypeStruct((2, CELLS, EXPAND), BF16),
            jax.ShapeDtypeStruct((2, CELLS, WIDTH), BF16),
            jax.ShapeDtypeStruct((3, 3, EXPAND), F32),
            jax.ShapeDtypeStruct((EXPAND, WIDTH), F32),
            jax.ShapeDtypeStruct((WIDTH, 3 * WIDTH), F32),
            jax.ShapeDtypeStruct((WIDTH, WIDTH), F32),
            jax.ShapeDtypeStruct((1, WIDTH), F32),
        ),
        in_specs=[anywhere, anywhere, vmem, vmem],
        out_specs=(anywhere,) * 2 + (vmem,) * 5,
        scratch_shapes=[pltpu.SemaphoreType.DMA((5,))],
        compiler_params=pltpu.CompilerParams(vmem_limit_bytes=32 * 2**20),
        name="finish",
    )(ge, gs, whole, extra)


def on_device(expanded, skip, cotangent, depth_kernel, w_proj, norm_gain, w_qkv, w_out):
    ge, gs, whole, extra = whole_call(
        expanded[:, 0],
        skip.reshape(2, CELLS, WIDTH),
        cotangent.reshape(2, CELLS, WIDTH),
        depth_kernel,
        w_proj,
        norm_gain.reshape(1, WIDTH),
        w_qkv,
        w_out,
    )
    scale = 1.0 / math.sqrt(2 * lax.axis_size("dp") * TILES * CELLS)
    ge, gs, gkern, gproj, gwqkv, gout, ggain = finish(ge, gs, whole, extra, scale)
    return (
        ge.reshape(2, 1, ROWS, COLS, EXPAND),
        gs.reshape(2, 1, ROWS, COLS, WIDTH),
        gkern,
        gproj,
        gwqkv,
        gout,
        ggain.reshape(WIDTH),
    )


def solution(mesh):
    tiled = P("dp", ("row", "col"), None, None, None)
    return jax.shard_map(
        on_device,
        mesh=mesh,
        in_specs=(tiled, tiled, tiled, P(), P(), P(), P(), P()),
        out_specs=(tiled, tiled, P(), P(), P(), P(), P()),
        check_vma=False,
    )
```

time: 525 us -> 138 us (0.26); the launches traced: 517 us -> 137 us
  waiting for transfers between devices: 145 us -> 0 us
  Pallas kernels: 0 us -> 131 us
  matrix products: 101 us -> 0 us
  blocking collectives: 69.4 us -> 0 us
  other arithmetic: 66.8 us -> 0 us
  local copies, waits for them, and re-layouts: 72.2 us -> 5.43 us
  starting transfers between devices: 47.6 us -> 0 us
  between operations: 15.1 us -> 0.65 us
    pallas_call x0 -> x2, Pallas kernels: none -> 131 us  [the longest x1 128 us: whole_call(): pl.pallas_call(whole_kernel, out_shape=(jax.ShapeDtypeStruct((2, CELLS, E...]
    psum x1 -> x0, waiting for transfers between devices: 119 us -> none  [on_device(): lax.psum((grad_kernel, grad_proj, grad_wqkv, grad_out, grad_gain), ('dp',...]
    dot_general x14 -> x0, matrix products: 101 us -> none  [the longest x6 55.9 us: contract(): jnp.einsum(pattern, left_op, right_op, preferred_element_type=jnp.float32)]
    psum x1 -> x0, blocking collectives: 69.4 us -> none  [on_device(): lax.psum((grad_kernel, grad_proj, grad_wqkv, grad_out, grad_gain), ('dp',...]
    convert_element_type x7 -> x0, local copies, waits for them, and re-layouts: 32.8 us -> none  [the longest x3 21.3 us: attend_back(): jnp.stack([grad_query, grad_keys, grad_values], axis=2).astype(jnp.bfloat16)]
    all_to_all x3 -> x0, starting transfers between devices: 25.6 us -> none  [the longest x1 11.6 us: on_device(): lax.all_to_all(send_cot, ('row', 'col'), split_axis=0, concat_axis=1, til...]
    convert_element_type x6 -> x0, other arithmetic: 22.9 us -> none  [the longest x1 15.9 us: on_device(): activated = smooth(pre_act).astype(jnp.bfloat16)]
    reshape x6 -> x0, local copies, waits for them, and re-layouts: 21.9 us -> none  [the longest x1 10.1 us: attend_back(): proj_qkv = proj_qkv.reshape(groups, length, 3, n_heads, head_size)]
  transfers between devices with their start and end apart: 12 -> 0, of which waited for: 6 -> 0; matrix products, arithmetic and copies ran while one was open for 20% -> 0% of each run, Pallas kernels for 0% -> 0%
where the time goes in v3:
time: 138 us; the launch traced here: 137 us
  Pallas kernels  131 us (95%)
  local copies, waits for them, and re-layouts  5.43 us (4%)
    pallas_call x1, Pallas kernels, whole_call(): pl.pallas_call(whole_kernel, out_shape=(jax.ShapeDtypeStruct((2, CELLS, E...  128 us
    unnamed x8, local copies, waits for them, and re-layouts  5.43 us
    pallas_call x1, Pallas kernels, finish(): pl.pallas_call(kernel, out_shape=(jax.ShapeDtypeStruct((2, CELLS, EXPAND)...  3.72 us

profile of v3, /device:TPU:1, one launch (start us, length us, event | category | flops | bytes accessed | tf_op | source)
XLA Modules:
  0.0 137.4 jit_solution(15547416556052457653)
XLA Ops:
  0.6 127.6 %whole.1 = (bf16[2,1024,1024]{2,1,0:T(8,128)(2,1)}, bf16[2,1024,256]{2,1,0:T(8,128)(2,1)}, bf16[4,2,256,256]{3,2,1,0:T(8,128)(2,1)}, f32[48,256]{1,0:T(8,128)}) custom-call(bf16[2,32,32,1024]{3,2,1,0:T(8,128)(2,1)} %bitcast.11, bf16[2,1024,256]{2,1,0:T(8,128)(2,1)} %bitcast.12, bf16[2,1024,256]{2,1,0:T(8,128)(2,1)} %bitcast.13, f32[3,3,1024]{2,1,0:T(4,128)} %kern_ref.1, ...), custom_call_target="tpu_custom_call" | custom-call | tf_op jit(solution)/shard_map/whole/pallas_call | solution.py:681
  128.2 0.0 copy-start
  128.2 2.2 %copy-done = bf16[2,1024,1024]{2,1,0:T(8,128)(2,1)S(1)} copy-done((bf16[2,1024,1024]{2,1,0:T(8,128)(2,1)S(1)}, bf16[2,1024,1024]{2,1,0:T(8,128)(2,1)}, u32[]{:S(2)}) %copy-start) | copy-done | bytes 4194328
  130.4 0.0 copy-start.1
  130.4 1.2 copy-done.1
  131.6 0.0 copy-start.2
  131.7 1.2 copy-done.2
  132.9 0.0 copy-start.3
  132.9 0.8 copy-done.3
  133.7 3.7 %finish.1 = (bf16[2,1024,1024]{2,1,0:T(8,128)(2,1)}, bf16[2,1024,256]{2,1,0:T(8,128)(2,1)}, f32[3,3,1024]{2,1,0:T(4,128)}, f32[1024,256]{1,0:T(8,128)}, f32[256,...) custom-call(bf16[2,1024,1024]{2,1,0:T(8,128)(2,1)S(1)} %copy-done, bf16[2,1024,256]{2,1,0:T(8,128)(2,1)S(1)} %copy-done.1, ...), custom_call_target="tpu_custom_call" | custom-call | tf_op jit(solution)/shard_map/finish/pallas_call | solution.py:754
Async XLA Ops:
  128.2 2.2 %copy-start = (bf16[2,1024,1024]{2,1,0:T(8,128)(2,1)S(1)}, bf16[2,1024,1024]{2,1,0:T(8,128)(2,1)}, u32[]{:S(2)}) copy-start(bf16[2,1024,1024]{2,1,0:T(8,128)(2,1)} %get-tuple-element.18.refs_0_) | copy-start | bytes 12582916
  130.4 1.2 copy-start.1
  131.6 1.2 copy-start.2
  132.9 0.8 copy-start.3

commit v4 on v3

--- a/solution.py
+++ b/solution.py
@@ -225,9 +225,8 @@
     sides_out, sides_in, corners_out, corners_in, xcols, gcols, terms, gsides_out, gsides_in, gcorners_out, gcorners_in,
     gproj_t, gkern, gw_ref, go_ref, gg_ref, part_out, core_in, y_out, y_in, small_out, small_in, whole,
     ex_a, ex_b, ex_c,
-    load_sem, rim_send, rim_recv, cot_send, cot_recv, mix_send, mix_recv, back_send, back_recv, own_sem, store_sem,
-    core_send, core_recv, y_send, y_recv, z_send, z_recv, g_send, g_recv, gy_send, gy_recv,
-    ey_send, ey_recv, ez_send, ez_recv,
+    load_sem, rim_send, rim_recv, cot_sem, mix_sem, back_send, back_recv, own_sem, store_sem,
+    core_send, core_recv, y_sem, z_sem, g_sem, gy_sem, ey_sem, ez_sem,
 ):
     me = my_tile()
     tile_row, tile_col = me // GRID, lax.rem(me, GRID)
@@ -275,8 +274,8 @@
         return pltpu.make_async_remote_copy(
             src_ref=cot_hbm.at[:, times(target, SHARE), :],
             dst_ref=got_cot.at[:, times(slot, SHARE), :],
-            send_sem=cot_send.at[target],
-            recv_sem=cot_recv.at[slot],
+            send_sem=cot_sem.at[0],
+            recv_sem=cot_sem.at[1],
             device_id=tile_id(target),
             device_id_type=MESH_ID,
         )
@@ -285,8 +284,8 @@
         return pltpu.make_async_remote_copy(
             src_ref=mix.at[picture, times(target, SHARE), :],
             dst_ref=got_mix.at[picture, times(slot, SHARE), :],
-            send_sem=mix_send.at[picture, target],
-            recv_sem=mix_recv.at[picture, slot],
+            send_sem=mix_sem.at[0, picture],
+            recv_sem=mix_sem.at[1, picture],
             device_id=tile_id(target),
             device_id_type=MESH_ID,
         )
@@ -295,12 +294,16 @@
         return pltpu.make_async_remote_copy(
             src_ref=back.at[picture, times(target, SHARE), :],
             dst_ref=gs.at[picture, times(slot, SHARE), :],
-            send_sem=back_send.at[picture, target],
-            recv_sem=back_recv.at[picture, slot],
+            send_sem=back_send.at[picture],
+            recv_sem=back_recv.at[picture, slot // BAND_TILES],
             device_id=tile_id(target),
             device_id_type=MESH_ID,
         )
 
+    def passed(view, sem):
+        pltpu.make_async_copy(view, view, sem).wait()
+
+    rest = pl.ds(0, CELLS - SHARE)
     loop(1, TILES, lambda i: cot_copy(lax.rem(me + i, TILES), me).start())
     own_cot = pltpu.make_async_copy(cot_hbm.at[:, own, :], got_cot.at[:, own, :], own_sem.at[0])
     own_cot.start()
@@ -342,13 +345,13 @@
             mix[picture, cells, :] = (skip_ref[picture, cells, :].astype(F32) + projected).astype(BF16)
 
             def send_mix(i):
-                target = band * BAND_TILES + lax.rem(me + i, BAND_TILES)
-
-                @pl.when(target != me)
-                def _():
-                    mix_copy(picture, target, me).start()
-
-            loop(0, BAND_TILES, send_mix)
+                mix_copy(picture, band * BAND_TILES + lax.rem(me + i, BAND_TILES), me).start()
+
+            loop(1, BAND_TILES, send_mix)
+
+            @pl.when(band != me // BAND_TILES)
+            def _():
+                send_mix(0)
 
         loop(0, BANDS, do_band)
 
@@ -360,7 +363,7 @@
     gg_ref[...] = jnp.zeros_like(gg_ref)
     gproj_t[...] = jnp.zeros_like(gproj_t)
     own_cot.wait()
-    loop(1, TILES, lambda i: cot_copy(lax.rem(me + i, TILES), lax.rem(me + i, TILES)).wait_recv())
+    passed(got_cot.at[:, rest, :], cot_sem.at[1])
 
     def attend_picture(picture):
         own_mix = pltpu.make_async_copy(mix.at[picture, own, :], got_mix.at[picture, own, :], own_sem.at[1])
@@ -369,7 +372,7 @@
         for b in range(4):
             r = slice(256 * b, 256 * b + 256)
             cot_s[:, 16 * b : 16 * b + 16, :] = dot(perm, got_cot[picture, r, :]).astype(BF16).reshape(16, 16, 256)
-        loop(1, TILES, lambda i: mix_copy(picture, lax.rem(me + i, TILES), lax.rem(me + i, TILES)).wait_recv())
+        passed(got_mix.at[picture, rest, :], mix_sem.at[1, picture])
         own_mix.wait()
         for b in range(4):
             r = slice(256 * b, 256 * b + 256)
@@ -404,8 +407,8 @@
 
     def core_copy(half):
         return pltpu.make_async_remote_copy(
-            src_ref=part_out.at[pl.ds(2 * half, 2), 1 - core],
-            dst_ref=core_in.at[pl.ds(2 * half, 2)],
+            src_ref=part_out.at[half, :, 1 - core],
+            dst_ref=core_in.at[half],
             send_sem=core_send.at[half],
             recv_sem=core_recv.at[half],
             device_id=mate,
@@ -423,42 +426,80 @@
     def z_id(n):
         return {"col": n * 2 + core}
 
-    def y_copy(to, slot):
-        return remote(y_out.at[to], y_in.at[slot], y_send.at[to], y_recv.at[slot], y_id(to))
-
-    def z_copy(to, slot):
-        return remote(small_out.at[times(to, 16)], small_in.at[slot], z_send.at[to], z_recv.at[slot], z_id(to))
-
-    def g_copy(to, slot):
+    def piece(n):
+        return times(n // 2, 16), times(lax.rem(n, 2), LANES)
+
+    def y_copy(half, to):
+        return remote(y_out.at[half, to], y_in.at[half, q], y_sem.at[half, 0], y_sem.at[half, 1], y_id(to))
+
+    def z_copy(half, to):
         return remote(
-            whole.at[q, core, times(chip, 16)], whole.at[q, core, times(slot, 16)],
-            g_send.at[to], g_recv.at[slot], z_id(to),
+            small_out.at[(half, *piece(to))], small_in.at[half, chip], z_sem.at[half, 0], z_sem.at[half, 1], z_id(to)
         )
 
-    def gy_copy(to, slot):
-        return remote(whole.at[q, core], whole.at[slot, core], gy_send.at[to], gy_recv.at[slot], y_id(to))
-
-    def ey_copy(to, slot):
-        return remote(ex_b.at[q], ex_b.at[slot], ey_send.at[to], ey_recv.at[slot], y_id(to))
-
-    def ez_copy(to, slot):
-        return remote(ex_c.at[chip], ex_c.at[slot], ez_send.at[to], ez_recv.at[slot], z_id(to))
+    def g_copy(half, to):
+        here = whole.at[(half, q, core, *piece(chip))]
+        return remote(here, here, g_sem.at[half, 0], g_sem.at[half, 1], z_id(to))
+
+    def gy_copy(half, to):
+        here = whole.at[half, q, core]
+        return remote(here, here, gy_sem.at[half, 0], gy_sem.at[half, 1], y_id(to))
+
+    def mate_copy(half):
+        here = whole.at[half, :, core]
+        return remote(here, here, core_send.at[2 + half], core_recv.at[2 + half], mate)
 
     def others(count, mine, action):
         loop(1, count, lambda i: action(lax.rem(mine + i, count)))
 
-    def core_sum(half):
+    def total_of(ref, count):
+        total = ref[0].astype(F32)
+        for n in range(1, count):
+            total = total + ref[n].astype(F32)
+        return total
+
+    def reduce_y(half):
         core_copy(half).wait_recv()
-        for n in (2 * half, 2 * half + 1):
-            y_out[n] = (part_out[n, core].astype(F32) + core_in[n].astype(F32)).astype(BF16)
-
-            @pl.when(q != n)
-            def _():
-                y_copy(n, q).start()
+        for n in range(4):
+            y_out[half, n] = (part_out[half, n, core].astype(F32) + core_in[half, n].astype(F32)).astype(BF16)
+        others(4, q, lambda n: y_copy(half, n).start())
+
+    def reduce_z(half):
+        passed(y_in.at[half, pl.ds(0, 3)], y_sem.at[half, 1])
+        y_in[half, q] = y_out[half, q]
+        small_out[half] = total_of(y_in.at[half], 4).astype(BF16)
+        others(16, chip, lambda n: z_copy(half, n).start())
+
+    def gather_z(half):
+        passed(small_in.at[half, pl.ds(0, 15)], z_sem.at[half, 1])
+        small_in[half, chip] = small_out[(half, *piece(chip))]
+        whole[(half, q, core, *piece(chip))] = total_of(small_in.at[half], 16).astype(BF16)
+        others(16, chip, lambda n: g_copy(half, n).start())
+
+    def gather_y(half):
+        passed(small_in.at[half, pl.ds(0, 15)], g_sem.at[half, 1])
+        others(4, q, lambda n: gy_copy(half, n).start())
+
+    def gather_core(half):
+        passed(y_in.at[half, pl.ds(0, 3)], gy_sem.at[half, 1])
+        mate_copy(half).start()
+
+    def reduction_sent(half):
+        core_copy(half).wait_send()
+        passed(y_in.at[half, pl.ds(0, 3)], y_sem.at[half, 0])
+        passed(small_in.at[half, pl.ds(0, 15)], z_sem.at[half, 0])
+        passed(small_in.at[half, pl.ds(0, 15)], g_sem.at[half, 0])
+        passed(y_in.at[half, pl.ds(0, 3)], gy_sem.at[half, 0])
+
+    def ey_copy(to):
+        return remote(ex_b.at[q], ex_b.at[q], ey_sem.at[0], ey_sem.at[1], y_id(to))
+
+    def ez_copy(to):
+        return remote(ex_c.at[chip], ex_c.at[chip], ez_sem.at[0], ez_sem.at[1], z_id(to))
 
     for n in range(4):
         block = gw_ref[256 * n : 256 * n + 256] if n < 3 else go_ref[...]
-        part_out[2 + n // 2, n % 2] = block.astype(BF16)
+        part_out[1, n] = block.astype(BF16).reshape(2, 128, 256)
     core_copy(1).start()
 
 
@@ -470,14 +511,14 @@
             band = lax.rem(step + tile_row // 2, BANDS)
             cells = times(band, BAND_CELLS)
 
-            def arrived(i):
-                source = band * BAND_TILES + i
-
-                @pl.when(source != me)
-                def _():
-                    back_copy(picture, source, source).wait_recv()
-
-            loop(0, BAND_TILES, arrived)
+            @pl.when(band != me // BAND_TILES)
+            def _():
+                passed(gs.at[picture, pl.ds(0, BAND_CELLS), :], back_recv.at[picture, band])
+
+            @pl.when(band == me // BAND_TILES)
+            def _():
+                passed(gs.at[picture, pl.ds(0, BAND_CELLS - SHARE), :], back_recv.at[picture, band])
+
             flat = gs[picture, cells, :]
             flat_t = flat.T
             for n in range(4):
@@ -494,13 +535,14 @@
 
         @pl.when(picture == 0)
         def _():
-            core_sum(1)
+            reduce_y(1)
 
         @pl.when(picture == 1)
         def _():
             for n in range(4):
-                part_out[n // 2, n % 2] = gproj_t[:, 256 * n : 256 * n + 256].T.astype(BF16)
+                part_out[0, n] = gproj_t[:, 256 * n : 256 * n + 256].T.astype(BF16).reshape(2, 128, 256)
             core_copy(0).start()
+            reduce_z(1)
 
         def kernel_block(block):
             lanes = times(block, LANES)
@@ -525,13 +567,14 @@
             for n in range(9):
                 gkern[n : n + 1, lanes] += jnp.sum(sums[n], axis=0, keepdims=True)
 
-        loop(0, LANE_BLOCKS // 2, kernel_block)
+        loop(0, LANE_BLOCKS // 4, kernel_block)
 
         @pl.when(picture == 1)
         def _():
-            core_sum(0)
-
-        loop(LANE_BLOCKS // 2, LANE_BLOCKS, kernel_block)
+            reduce_y(0)
+            gather_z(1)
+
+        loop(LANE_BLOCKS // 4, LANE_BLOCKS, kernel_block)
         for row_off in range(3):
             for side in range(2):
                 n = 3 * row_off + 2 * side
@@ -548,22 +591,14 @@
     extra = [gkern[0:9, 256 * n : 256 * n + 256] for n in range(4)]
     extra = jnp.concatenate(extra + [gg_ref[...], jnp.zeros((11, 256), F32)], axis=0).astype(BF16)
     ex_a[core] = extra
-    ex_core = remote(ex_a.at[core], ex_a.at[core], core_send.at[2], core_recv.at[2], mate)
+    ex_core = remote(ex_a.at[core], ex_a.at[core], core_send.at[4], core_recv.at[4], mate)
     ex_core.start()
 
-    def total_of(ref, count):
-        total = ref[0].astype(F32)
-        for n in range(1, count):
-            total = total + ref[n].astype(F32)
-        return total
-
-    others(4, q, lambda n: y_copy(n, n).wait_recv())
-    y_in[q] = y_out[q]
-    small_out[...] = total_of(y_in, 4).astype(BF16)
-    others(16, chip, lambda n: z_copy(n, chip).start())
     ex_core.wait_recv()
     ex_b[q] = total_of(ex_a, 2).astype(BF16)
-    others(4, q, lambda n: ey_copy(n, q).start())
+    others(4, q, lambda n: ey_copy(n).start())
+    reduce_z(0)
+    gather_y(1)
 
     def store_copy(picture, band):
         cells = times(band, BAND_CELLS)
@@ -596,61 +631,48 @@
         loop(begin, end, do_band)
 
     last_start(0)
-    last_bands(0, 0, 4)
-
-    others(16, chip, lambda n: z_copy(n, n).wait_recv())
-    small_in[chip] = small_out[times(chip, 16)]
-    whole[q, core, times(chip, 16)] = total_of(small_in, 16).astype(BF16)
-    others(16, chip, lambda n: g_copy(n, chip).start())
-    others(4, q, lambda n: ey_copy(n, n).wait_recv())
+    last_bands(0, 0, 3)
+    passed(ex_b.at[pl.ds(0, 3)], ey_sem.at[1])
     ex_c[chip] = total_of(ex_b, 4).astype(BF16)
-    others(16, chip, lambda n: ez_copy(n, chip).start())
-
+    others(16, chip, lambda n: ez_copy(n).start())
+    gather_z(0)
+    last_bands(0, 3, 4)
+    gather_core(1)
     last_start(1)
-    last_bands(1, 0, 3)
-
-    others(16, chip, lambda n: g_copy(n, n).wait_recv())
-    others(4, q, lambda n: gy_copy(n, q).start())
-
-    last_bands(1, 3, 4)
-
-    others(16, chip, lambda n: ez_copy(n, n).wait_recv())
+    last_bands(1, 0, 2)
+    gather_y(0)
+    last_bands(1, 2, 4)
+    passed(ex_c.at[pl.ds(0, 15)], ez_sem.at[1])
     extra_out[...] = total_of(ex_c, 16)
 
 
-    def sent(i):
-        peer = lax.rem(me + i, TILES)
-        cot_copy(peer, peer).wait_send()
-        for picture in range(2):
-            mix_copy(picture, peer, peer).wait_send()
-            back_copy(picture, peer, peer).wait_send()
-
-    loop(1, TILES, sent)
+    passed(got_cot.at[:, rest, :], cot_sem.at[0])
+    for picture in range(2):
+        passed(mix.at[picture, rest, :], mix_sem.at[0, picture])
+        passed(back.at[picture, rest, :], back_send.at[picture])
     for turn in range(2):
         for picture in range(2):
             for copy in rim_of(picture, turn):
                 copy.wait_send()
-    for half in range(2):
-        core_copy(half).wait_send()
     ex_core.wait_send()
-    others(4, q, lambda n: y_copy(n, n).wait_send())
-    others(4, q, lambda n: ey_copy(n, n).wait_send())
-    others(16, chip, lambda n: z_copy(n, n).wait_send())
-    others(16, chip, lambda n: g_copy(n, n).wait_send())
-    others(16, chip, lambda n: ez_copy(n, n).wait_send())
+    passed(ex_b.at[pl.ds(0, 3)], ey_sem.at[0])
+    passed(ex_c.at[pl.ds(0, 15)], ez_sem.at[0])
     gs_store.wait()
     for picture in range(2):
         for band in range(BANDS):
             store_copy(picture, band).wait()
-    others(4, q, lambda n: gy_copy(n, n).wait_recv())
-    to_mate = remote(whole.at[:, core], whole.at[:, core], core_send.at[3], core_recv.at[3], mate)
-    to_mate.start()
-    others(4, q, lambda n: gy_copy(n, n).wait_send())
-    to_mate.wait_recv()
-    to_mate.wait_send()
-    whole_store = pltpu.make_async_copy(whole, whole_hbm, own_sem.at[4])
-    whole_store.start()
-    whole_store.wait()
+    mate_copy(1).wait_recv()
+    stores = [pltpu.make_async_copy(whole.at[half], whole_hbm.at[half], own_sem.at[4 + half]) for half in range(2)]
+    stores[1].start()
+    gather_core(0)
+    for half in range(2):
+        reduction_sent(half)
+    mate_copy(0).wait_recv()
+    stores[0].start()
+    mate_copy(0).wait_send()
+    mate_copy(1).wait_send()
+    for copy in stores:
+        copy.wait()
 
 
 def my_tile():
@@ -683,7 +705,7 @@
         out_shape=(
             jax.ShapeDtypeStruct((2, CELLS, EXPAND), BF16),
             jax.ShapeDtypeStruct((2, CELLS, WIDTH), BF16),
-            jax.ShapeDtypeStruct((4, 2, 256, 256), BF16),
+            jax.ShapeDtypeStruct((2, 4, 2, 128, 256), BF16),
             jax.ShapeDtypeStruct((48, 256), F32),
         ),
         in_specs=[anywhere, vmem, anywhere] + [vmem] * 7,
@@ -698,13 +720,12 @@
         + rims
         + [
             fl(WIDTH, EXPAND), fl(16, EXPAND), fl(3 * WIDTH, WIDTH), fl(WIDTH, WIDTH), fl(1, WIDTH),
-            bf(4, 2, 256, 256), bf(4, 256, 256), bf(4, 256, 256), bf(4, 256, 256),
-            bf(256, 256), bf(16, 16, 256), bf(4, 2, 256, 256),
+            bf(2, 4, 2, 128, 256), bf(2, 4, 128, 256), bf(2, 4, 128, 256), bf(2, 4, 128, 256),
+            bf(2, 128, 256), bf(2, 16, 16, LANES), bf(2, 4, 2, 128, 256),
             bf(2, 48, 256), bf(4, 48, 256), bf(16, 48, 256),
-            dma((2,)), dma((2, 2, 8)), dma((2, 2, 8)), dma((TILES,)), dma((TILES,)),
-            dma((2, TILES)), dma((2, TILES)), dma((2, TILES)), dma((2, TILES)), dma((5,)), dma((2, BANDS)),
-            dma((4,)), dma((4,)), dma((4,)), dma((4,)), dma((16,)), dma((16,)), dma((16,)), dma((16,)),
-            dma((4,)), dma((4,)), dma((4,)), dma((4,)), dma((16,)), dma((16,)),
+            dma((2,)), dma((2, 2, 8)), dma((2, 2, 8)), dma((2,)), dma((2, 2)), dma((2,)), dma((2, BANDS)),
+            dma((6,)), dma((2, BANDS)),
+            dma((5,)), dma((5,)), dma((2, 2)), dma((2, 2)), dma((2, 2)), dma((2, 2)), dma((2,)), dma((2,)),
         ],
         compiler_params=pltpu.CompilerParams(
             collective_id=0, has_side_effects=True, vmem_limit_bytes=56 * 2**20
@@ -729,7 +750,7 @@
     for copy in copies:
         copy.start()
     for n in range(8):
-        block = whole_ref[n // 2, n % 2].astype(F32) * scale
+        block = whole_ref[n // 4, n % 4].reshape(256, 256).astype(F32) * scale
         if n < 4:
             gproj_out[256 * n : 256 * n + 256, :] = block
             some = extra_ref[9 * n : 9 * n + 9, :] * scale
@@ -765,7 +786,7 @@
         in_specs=[anywhere, anywhere, vmem, vmem],
         out_specs=(anywhere,) * 2 + (vmem,) * 5,
         scratch_shapes=[pltpu.SemaphoreType.DMA((5,))],
-        compiler_params=pltpu.CompilerParams(vmem_limit_bytes=32 * 2**20),
+        compiler_params=pltpu.CompilerParams(vmem_limit_bytes=60 * 2**20),
         name="finish",
     )(ge, gs, whole, extra)
 

time: 138 us -> 282 us (2.04)
  Pallas kernels: 131 us -> 281 us
  local copies, waits for them, and re-layouts: 5.43 us -> 0 us
    pallas_call x1, Pallas kernels: 3.72 us -> 163 us  [finish(): pl.pallas_call(kernel, out_shape=(jax.ShapeDtypeStruct((2, CELLS, EXPAND)...]
    pallas_call x1, Pallas kernels: 128 us -> 118 us  [whole_call(): pl.pallas_call(whole_kernel, out_shape=(jax.ShapeDtypeStruct((2, CELLS, E...]
    unnamed x8 -> x0, local copies, waits for them, and re-layouts: 5.43 us -> none
where the time goes in v4:
time: 282 us
  Pallas kernels  281 us (100%)
    pallas_call x1, Pallas kernels, finish(): pl.pallas_call(kernel, out_shape=(jax.ShapeDtypeStruct((2, CELLS, EXPAND)...  163 us
    pallas_call x1, Pallas kernels, whole_call(): pl.pallas_call(whole_kernel, out_shape=(jax.ShapeDtypeStruct((2, CELLS, E...  118 us

profile of v4, /device:TPU:1, one launch (start us, length us, event | category | flops | bytes accessed | tf_op | source)
XLA Modules:
  0.0 281.5 jit_solution(1280222355671696418)
XLA Ops:
  0.6 118.4 %whole.1 = (bf16[2,1024,1024]{2,1,0:T(8,128)(2,1)}, bf16[2,1024,256]{2,1,0:T(8,128)(2,1)}, bf16[2,4,2,128,256]{4,3,2,1,0:T(8,128)(2,1)}, f32[48,256]{1,0:T(8,128)}) custom-call(bf16[2,32,32,1024]{3,2,1,0:T(8,128)(2,1)} %bitcast.11, bf16[2,1024,256]{2,1,0:T(8,128)(2,1)} %bitcast.12, bf16[2,1024,256]{2,1,0:T(8,128)(2,1)} %bitcast.13, f32[3,3,1024]{2,1,0:T(4,128)} %kern_ref.1, ...), custom_call_target="tpu_custom_call" | custom-call | tf_op jit(solution)/shard_map/whole/pallas_call | solution.py:703
  119.0 162.5 %finish.1 = (bf16[2,1024,1024]{2,1,0:T(8,128)(2,1)}, bf16[2,1024,256]{2,1,0:T(8,128)(2,1)}, f32[3,3,1024]{2,1,0:T(4,128)}, f32[1024,256]{1,0:T(8,128)}, f32[256,...) custom-call(bf16[2,1024,1024]{2,1,0:T(8,128)(2,1)} %get-tuple-element.18.refs_0_, ...), custom_call_target="tpu_custom_call" | custom-call | tf_op jit(solution)/shard_map/finish/pallas_call | solution.py:775

commit v5 on v4

--- a/solution.py
+++ b/solution.py
@@ -24,6 +24,7 @@
 BANDS = ROWS // BAND
 BAND_CELLS = BAND * COLS
 BAND_TILES = TILES // BANDS
+GROUPS = 8
 SHARE = CELLS // TILES
 F32 = jnp.float32
 BF16 = jnp.bfloat16
@@ -169,15 +170,10 @@
 
 
 def pick_heads(full, lane):
-    halves = []
-    for half in range(2):
-        cols = slice(128 * half, 128 * half + 128)
-        kept = full[256 * half : 256 * half + 64, cols]
-        for h in range(1, 4):
-            start = 256 * half + 64 * h
-            kept = jnp.where(lane == h, full[start : start + 64, cols], kept)
-        halves.append(kept)
-    return jnp.concatenate(halves, axis=1)
+    kept = full[0:64]
+    for h in range(1, 4):
+        kept = jnp.where(lane == h, full[64 * h : 64 * h + 64], kept)
+    return kept
 
 
 def attend(mix, cot, gain, wqkv_ref, wout_ref, mask_ref, gw_ref, go_ref, gg_ref):
@@ -189,26 +185,27 @@
     normed = (mi * gain).astype(BF16)
     qkv = dot(normed, wqkv_ref[...]).astype(BF16)
     gatt = dot_t(cot, wout_ref[...]).astype(BF16)
-    att, gqs, gks, gvs = [], [], [], []
-    for i in range(4):
-        r = slice(64 * i, 64 * i + 64)
-        q, k, v = qkv[r, 0:256], qkv[r, 256:512], qkv[r, 512:768]
-        qexp = jnp.concatenate([q] * 8, axis=0) * mask_ref[...]
-        doexp = jnp.concatenate([gatt[r]] * 8, axis=0) * mask_ref[...]
-        st = dot_t(k, qexp) * scale
-        e = jnp.exp(st - jnp.max(st, axis=0, keepdims=True))
-        p = e * (1.0 / jnp.sum(e, axis=0, keepdims=True))
-        pb = p.astype(BF16)
-        dp = dot_t(v, doexp)
-        ds = (p * (dp - jnp.sum(dp * p, axis=0, keepdims=True)) * scale).astype(BF16)
-        att.append(pick_heads(dot_tl(pb, v), lane).astype(BF16))
-        gqs.append(pick_heads(dot_tl(ds, k), lane).astype(BF16))
-        gks.append(dot(ds, qexp).astype(BF16))
-        gvs.append(dot(pb, doexp).astype(BF16))
+    parts = [(slice(64 * i, 64 * i + 64), 128 * half) for i in range(GROUPS) for half in range(2)]
+    q, k, v = ([qkv[r, first + 256 * n : first + 256 * n + 128] for r, first in parts] for n in range(3))
+    qexp = [jnp.concatenate([x] * 4, axis=0) * mask_ref[...] for x in q]
+    doexp = [jnp.concatenate([gatt[r, first : first + 128]] * 4, axis=0) * mask_ref[...] for r, first in parts]
+    st = [dot_t(x, y) * scale for x, y in zip(k, qexp)]
+    dp = [dot_t(x, y) for x, y in zip(v, doexp)]
+    e = [jnp.exp(x - jnp.max(x, axis=0, keepdims=True)) for x in st]
+    p = [x * (1.0 / jnp.sum(x, axis=0, keepdims=True)) for x in e]
+    pb = [x.astype(BF16) for x in p]
+    ds = [(x * (y - jnp.sum(y * x, axis=0, keepdims=True)) * scale).astype(BF16) for x, y in zip(p, dp)]
+    att = [pick_heads(dot_tl(x, y), lane) for x, y in zip(pb, v)]
+    gvs = [dot(x, y) for x, y in zip(pb, doexp)]
+    gqs = [pick_heads(dot_tl(x, y), lane) for x, y in zip(ds, k)]
+    gks = [dot(x, y) for x, y in zip(ds, qexp)]
+    att, gqs, gks, gvs = (
+        [jnp.concatenate(x[2 * i : 2 * i + 2], axis=1).astype(BF16) for i in range(GROUPS)] for x in (att, gqs, gks, gvs)
+    )
     gqkv = [jnp.concatenate(x, axis=0) for x in (gqs, gks, gvs)]
     go_ref[...] += dot_tl(jnp.concatenate(att, axis=0), cot)
     normed_t = normed.T
-    gn = jnp.zeros((256, 256), F32)
+    gn = jnp.zeros((64 * GROUPS, 256), F32)
     for n in range(3):
         gw_ref[256 * n : 256 * n + 256] += dot(normed_t, gqkv[n])
         gn = gn + dot_t(gqkv[n], wqkv_ref[:, 256 * n : 256 * n + 256])
@@ -219,14 +216,14 @@
 
 
 def whole_kernel(
-    x_hbm, skip_ref, cot_hbm, kern_ref, wproj_ref, gain_ref, wqkv_ref, wout_ref, perm_ref, mask_ref,
+    x_hbm, skip_hbm, cot_hbm, kern_ref, wproj_hbm, gain_ref, wqkv_hbm, wout_hbm, perm_hbm, mask_hbm,
     ge_hbm, gs_hbm, whole_hbm, extra_out,
     xgrid, ggrid, act, dg, mix, got_mix, got_cot, mix_s, cot_s, back, gs,
     sides_out, sides_in, corners_out, corners_in, xcols, gcols, terms, gsides_out, gsides_in, gcorners_out, gcorners_in,
     gproj_t, gkern, gw_ref, go_ref, gg_ref, part_out, core_in, y_out, y_in, small_out, small_in, whole,
-    ex_a, ex_b, ex_c,
+    ex_a, ex_b, ex_c, skip_ref, wproj_ref, wqkv_ref, wout_ref, perm_ref, mask_ref,
     load_sem, rim_send, rim_recv, cot_sem, mix_sem, back_send, back_recv, own_sem, store_sem,
-    core_send, core_recv, y_sem, z_sem, g_sem, gy_sem, ey_sem, ez_sem,
+    core_send, core_recv, y_sem, z_sem, g_sem, gy_sem, ey_sem, ez_sem, operand_sem,
 ):
     me = my_tile()
     tile_row, tile_col = me // GRID, lax.rem(me, GRID)
@@ -240,7 +237,16 @@
         return kern_ref[n // 3, n % 3 : n % 3 + 1, lanes]
 
     loads = [pltpu.make_async_copy(x_hbm.at[p], xgrid.at[p, pl.ds(1, ROWS)], load_sem.at[p]) for p in range(2)]
-    for copy in loads:
+    operands = [
+        pltpu.make_async_copy(a, b, operand_sem.at[n])
+        for n, (a, b) in enumerate(
+            (
+                (skip_hbm, skip_ref), (wproj_hbm, wproj_ref), (wqkv_hbm, wqkv_ref),
+                (wout_hbm, wout_ref), (perm_hbm, perm_ref), (mask_hbm, mask_ref),
+            )
+        )
+    ]
+    for copy in loads + operands:
         copy.start()
     barrier = pltpu.get_barrier_semaphore()
 
@@ -304,15 +310,21 @@
         pltpu.make_async_copy(view, view, sem).wait()
 
     rest = pl.ds(0, CELLS - SHARE)
-    loop(1, TILES, lambda i: cot_copy(lax.rem(me + i, TILES), me).start())
     own_cot = pltpu.make_async_copy(cot_hbm.at[:, own, :], got_cot.at[:, own, :], own_sem.at[0])
     own_cot.start()
+    for copy in operands:
+        copy.wait()
 
 
     def forward_picture(picture):
         rim = rim_of(picture, 0)
         for copy in rim:
             copy.wait_recv()
+
+        @pl.when(picture == 0)
+        def _():
+            loop(1, TILES, lambda i: cot_copy(lax.rem(me + i, TILES), me).start())
+
         clear_outside(me, picture, xgrid, sides_in, corners_in)
         column_stack(picture, sides_in, corners_in, xcols)
         column_terms(picture, xcols, lambda a, c: weight(3 * a + c), terms)
@@ -379,14 +391,14 @@
             mix_s[:, 16 * b : 16 * b + 16, :] = dot(perm, got_mix[picture, r, :]).astype(BF16).reshape(16, 16, 256)
 
         def block(b):
-            groups = pl.ds(b * 4, 4)
+            groups = pl.ds(b * GROUPS, GROUPS)
             out = attend(
-                mix_s[groups].reshape(256, 256), cot_s[groups].reshape(256, 256), gain_ref[...],
+                mix_s[groups].reshape(64 * GROUPS, 256), cot_s[groups].reshape(64 * GROUPS, 256), gain_ref[...],
                 wqkv_ref, wout_ref, mask_ref, gw_ref, go_ref, gg_ref,
             )
-            cot_s[groups] = out.reshape(4, 64, 256)
-
-        loop(0, 4, block)
+            cot_s[groups] = out.reshape(GROUPS, 64, 256)
+
+        loop(0, 16 // GROUPS, block)
         for b in range(4):
             rows = cot_s[:, 16 * b : 16 * b + 16, :].reshape(256, 256)
             back[picture, 256 * b : 256 * b + 256] = dot(perm, rows).astype(BF16)
@@ -684,7 +696,7 @@
     for a in range(16):
         for b in range(16):
             perm[a * 16 + b, b * 16 + a] = 1
-    mask = np.kron(np.eye(8), np.ones((64, 32))).astype(np.float32)
+    mask = np.kron(np.eye(4), np.ones((64, 32))).astype(np.float32)
     return jnp.asarray(perm, BF16), jnp.asarray(mask, BF16)
 
 
@@ -708,7 +720,7 @@
             jax.ShapeDtypeStruct((2, 4, 2, 128, 256), BF16),
             jax.ShapeDtypeStruct((48, 256), F32),
         ),
-        in_specs=[anywhere, vmem, anywhere] + [vmem] * 7,
+        in_specs=[anywhere] * 3 + [vmem, anywhere, vmem] + [anywhere] * 4,
         out_specs=(anywhere, anywhere, anywhere, vmem),
         scratch_shapes=[
             bf(2, ROWS + 2, COLS, EXPAND), bf(2, ROWS + 2, COLS, EXPAND), bf(2, CELLS, EXPAND), bf(2, CELLS, EXPAND),
@@ -723,9 +735,10 @@
             bf(2, 4, 2, 128, 256), bf(2, 4, 128, 256), bf(2, 4, 128, 256), bf(2, 4, 128, 256),
             bf(2, 128, 256), bf(2, 16, 16, LANES), bf(2, 4, 2, 128, 256),
             bf(2, 48, 256), bf(4, 48, 256), bf(16, 48, 256),
+            bf(2, CELLS, WIDTH), bf(EXPAND, WIDTH), bf(WIDTH, 3 * WIDTH), bf(WIDTH, WIDTH), bf(256, 256), bf(256, LANES),
             dma((2,)), dma((2, 2, 8)), dma((2, 2, 8)), dma((2,)), dma((2, 2)), dma((2,)), dma((2, BANDS)),
             dma((6,)), dma((2, BANDS)),
-            dma((5,)), dma((5,)), dma((2, 2)), dma((2, 2)), dma((2, 2)), dma((2, 2)), dma((2,)), dma((2,)),
+            dma((5,)), dma((5,)), dma((2, 2)), dma((2, 2)), dma((2, 2)), dma((2, 2)), dma((2,)), dma((2,)), dma((6,)),
         ],
         compiler_params=pltpu.CompilerParams(
             collective_id=0, has_side_effects=True, vmem_limit_bytes=56 * 2**20
@@ -735,33 +748,45 @@
 
 
 def finish_kernel(
-    ge_hbm, gs_hbm, whole_ref, extra_ref, ge_out, gs_out, gkern_out, gproj_out, gwqkv_out, gout_out, ggain_out, sems, *, scale
+    ge_hbm, gs_hbm, whole_hbm, extra_ref, ge_out, gs_out, gkern_out, gproj_out, gwqkv_out, gout_out, ggain_out,
+    ge_held, gs_held, whole_ref, gproj, gwqkv, gout, sems, *, scale
 ):
-    copies = []
+    ways = [(whole_hbm, whole_ref, None)]
     for picture in range(2):
-        for part in range(2):
-            rows = pl.ds(512 * part, 512)
-            copies.append(
-                pltpu.make_async_copy(
-                    ge_hbm.at[picture, rows], ge_out.at[picture, rows], sems.at[2 * picture + part]
-                )
-            )
-    copies.append(pltpu.make_async_copy(gs_hbm, gs_out, sems.at[4]))
-    for copy in copies:
+        for part in range(4):
+            here = (picture, pl.ds(256 * part, 256))
+            ways.append((ge_hbm.at[here], ge_held.at[here], ge_out.at[here]))
+    ways.append((gs_hbm, gs_held, gs_out))
+    inward = [pltpu.make_async_copy(a, b, sems.at[0, n]) for n, (a, b, _) in enumerate(ways)]
+    outward = [pltpu.make_async_copy(b, c, sems.at[1, n]) for n, (_, b, c) in enumerate(ways) if n]
+    results = [
+        pltpu.make_async_copy(a, b, sems.at[1, len(ways) + n])
+        for n, (a, b) in enumerate(((gproj, gproj_out), (gwqkv, gwqkv_out), (gout, gout_out)))
+    ]
+    for copy in inward:
         copy.start()
+    for first, second in zip(inward[1:5], outward[:4]):
+        first.wait()
+        second.start()
+    inward[0].wait()
     for n in range(8):
         block = whole_ref[n // 4, n % 4].reshape(256, 256).astype(F32) * scale
         if n < 4:
-            gproj_out[256 * n : 256 * n + 256, :] = block
+            gproj[256 * n : 256 * n + 256, :] = block
             some = extra_ref[9 * n : 9 * n + 9, :] * scale
             for row in range(3):
                 gkern_out[row, :, 256 * n : 256 * n + 256] = some[3 * row : 3 * row + 3]
         elif n < 7:
-            gwqkv_out[:, 256 * (n - 4) : 256 * (n - 4) + 256] = block
+            gwqkv[:, 256 * (n - 4) : 256 * (n - 4) + 256] = block
         else:
-            gout_out[...] = block
+            gout[...] = block
     ggain_out[...] = extra_ref[36:37, :] * scale
-    for copy in copies:
+    for copy in results:
+        copy.start()
+    for first, second in zip(inward[5:], outward[4:]):
+        first.wait()
+        second.start()
+    for copy in outward + results:
         copy.wait()
 
 
@@ -783,9 +808,17 @@
             jax.ShapeDtypeStruct((WIDTH, WIDTH), F32),
             jax.ShapeDtypeStruct((1, WIDTH), F32),
         ),
-        in_specs=[anywhere, anywhere, vmem, vmem],
-        out_specs=(anywhere,) * 2 + (vmem,) * 5,
-        scratch_shapes=[pltpu.SemaphoreType.DMA((5,))],
+        in_specs=[anywhere, anywhere, anywhere, vmem],
+        out_specs=(anywhere, anywhere, vmem, anywhere, anywhere, anywhere, vmem),
+        scratch_shapes=[
+            pltpu.VMEM((2, CELLS, EXPAND), BF16),
+            pltpu.VMEM((2, CELLS, WIDTH), BF16),
+            pltpu.VMEM((2, 4, 2, 128, 256), BF16),
+            pltpu.VMEM((EXPAND, WIDTH), F32),
+            pltpu.VMEM((WIDTH, 3 * WIDTH), F32),
+            pltpu.VMEM((WIDTH, WIDTH), F32),
+            pltpu.SemaphoreType.DMA((2, 13)),
+        ],
         compiler_params=pltpu.CompilerParams(vmem_limit_bytes=60 * 2**20),
         name="finish",
     )(ge, gs, whole, extra)

time: 282 us -> 111 us (0.39)
  Pallas kernels: 281 us -> 110 us
    pallas_call x1, Pallas kernels: 163 us -> 6.68 us  [finish(): pl.pallas_call(kernel, out_shape=(jax.ShapeDtypeStruct((2, CELLS, EXPAND)...]
    pallas_call x1, Pallas kernels: 118 us -> 103 us  [whole_call(): pl.pallas_call(whole_kernel, out_shape=(jax.ShapeDtypeStruct((2, CELLS, E...]
where the time goes in v5:
time: 111 us; the launch traced here: 110 us
  Pallas kernels  110 us (99%)
    pallas_call x1, Pallas kernels, whole_call(): pl.pallas_call(whole_kernel, out_shape=(jax.ShapeDtypeStruct((2, CELLS, E...  103 us
    pallas_call x1, Pallas kernels, finish(): pl.pallas_call(kernel, out_shape=(jax.ShapeDtypeStruct((2, CELLS, EXPAND)...  6.68 us

profile of v5, /device:TPU:1, one launch (start us, length us, event | category | flops | bytes accessed | tf_op | source)
XLA Modules:
  0.0 110.5 jit_solution(7584091931283358144)
XLA Ops:
  0.6 103.1 %whole.1 = (bf16[2,1024,1024]{2,1,0:T(8,128)(2,1)}, bf16[2,1024,256]{2,1,0:T(8,128)(2,1)}, bf16[2,4,2,128,256]{4,3,2,1,0:T(8,128)(2,1)}, f32[48,256]{1,0:T(8,128)}) custom-call(bf16[2,32,32,1024]{3,2,1,0:T(8,128)(2,1)} %bitcast.11, bf16[2,1024,256]{2,1,0:T(8,128)(2,1)} %bitcast.12, bf16[2,1024,256]{2,1,0:T(8,128)(2,1)} %bitcast.13, f32[3,3,1024]{2,1,0:T(4,128)} %kern_ref.1, ...), custom_call_target="tpu_custom_call" | custom-call | tf_op jit(solution)/shard_map/whole/pallas_call | solution.py:715
  103.8 6.7 %finish.1 = (bf16[2,1024,1024]{2,1,0:T(8,128)(2,1)}, bf16[2,1024,256]{2,1,0:T(8,128)(2,1)}, f32[3,3,1024]{2,1,0:T(4,128)}, f32[1024,256]{1,0:T(8,128)}, f32[256,...) custom-call(bf16[2,1024,1024]{2,1,0:T(8,128)(2,1)} %get-tuple-element.18.refs_0_, ...), custom_call_target="tpu_custom_call" | custom-call | tf_op jit(solution)/shard_map/finish/pallas_call | solution.py:800

commit v6 on v5

--- a/solution.py
+++ b/solution.py
@@ -220,10 +220,10 @@
     ge_hbm, gs_hbm, whole_hbm, extra_out,
     xgrid, ggrid, act, dg, mix, got_mix, got_cot, mix_s, cot_s, back, gs,
     sides_out, sides_in, corners_out, corners_in, xcols, gcols, terms, gsides_out, gsides_in, gcorners_out, gcorners_in,
-    gproj_t, gkern, gw_ref, go_ref, gg_ref, part_out, core_in, y_out, y_in, small_out, small_in, whole,
+    gproj_t, gkern, gw_ref, go_ref, gg_ref, part_out, core_in, y_out, small_in, whole,
     ex_a, ex_b, ex_c, skip_ref, wproj_ref, wqkv_ref, wout_ref, perm_ref, mask_ref,
     load_sem, rim_send, rim_recv, cot_sem, mix_sem, back_send, back_recv, own_sem, store_sem,
-    core_send, core_recv, y_sem, z_sem, g_sem, gy_sem, ey_sem, ez_sem, operand_sem,
+    core_send, core_recv, scatter_sem, gather_sem, ey_sem, ez_sem, operand_sem,
 ):
     me = my_tile()
     tile_row, tile_col = me // GRID, lax.rem(me, GRID)
@@ -254,13 +254,19 @@
         pl.semaphore_signal(barrier, inc=1, device_id=tile_id(lax.rem(me + i, TILES)), device_id_type=MESH_ID)
 
     loop(1, TILES, greet)
-    for n in range(2):
-        pl.semaphore_signal(
-            barrier, inc=1, device_id={"dp": 1 - dp, "row": n, "col": col}, device_id_type=MESH_ID
-        )
+    loop(
+        0,
+        TILES // 2,
+        lambda i: pl.semaphore_signal(
+            barrier,
+            inc=1,
+            device_id={"dp": 1 - dp, "row": i // 16, "col": lax.rem(i, 16) * 2 + core},
+            device_id_type=MESH_ID,
+        ),
+    )
     loads[0].wait()
     collect_sides(0, xgrid, sides_out, corners_out)
-    pl.semaphore_wait(barrier, TILES + 1)
+    pl.semaphore_wait(barrier, TILES - 1 + TILES // 2)
 
     def rim_of(picture, turn):
         if turn == 0:
@@ -441,21 +447,18 @@
     def piece(n):
         return times(n // 2, 16), times(lax.rem(n, 2), LANES)
 
-    def y_copy(half, to):
-        return remote(y_out.at[half, to], y_in.at[half, q], y_sem.at[half, 0], y_sem.at[half, 1], y_id(to))
-
-    def z_copy(half, to):
-        return remote(
-            small_out.at[(half, *piece(to))], small_in.at[half, chip], z_sem.at[half, 0], z_sem.at[half, 1], z_id(to)
-        )
-
-    def g_copy(half, to):
+    def share_id(n):
+        return {"dp": n // 32, "row": lax.rem(n // 16, 2), "col": lax.rem(n, 16) * 2 + core}
+
+    mine = q * 16 + chip
+
+    def scatter_copy(half, to):
+        source = y_out.at[(half, to // 16, *piece(lax.rem(to, 16)))]
+        return remote(source, small_in.at[half, mine], scatter_sem.at[half, 0], scatter_sem.at[half, 1], share_id(to))
+
+    def gather_copy(half, to):
         here = whole.at[(half, q, core, *piece(chip))]
-        return remote(here, here, g_sem.at[half, 0], g_sem.at[half, 1], z_id(to))
-
-    def gy_copy(half, to):
-        here = whole.at[half, q, core]
-        return remote(here, here, gy_sem.at[half, 0], gy_sem.at[half, 1], y_id(to))
+        return remote(here, here, gather_sem.at[half, 0], gather_sem.at[half, 1], share_id(to))
 
     def mate_copy(half):
         here = whole.at[half, :, core]
@@ -470,38 +473,26 @@
             total = total + ref[n].astype(F32)
         return total
 
-    def reduce_y(half):
+    def scatter(half):
         core_copy(half).wait_recv()
         for n in range(4):
             y_out[half, n] = (part_out[half, n, core].astype(F32) + core_in[half, n].astype(F32)).astype(BF16)
-        others(4, q, lambda n: y_copy(half, n).start())
-
-    def reduce_z(half):
-        passed(y_in.at[half, pl.ds(0, 3)], y_sem.at[half, 1])
-        y_in[half, q] = y_out[half, q]
-        small_out[half] = total_of(y_in.at[half], 4).astype(BF16)
-        others(16, chip, lambda n: z_copy(half, n).start())
-
-    def gather_z(half):
-        passed(small_in.at[half, pl.ds(0, 15)], z_sem.at[half, 1])
-        small_in[half, chip] = small_out[(half, *piece(chip))]
-        whole[(half, q, core, *piece(chip))] = total_of(small_in.at[half], 16).astype(BF16)
-        others(16, chip, lambda n: g_copy(half, n).start())
-
-    def gather_y(half):
-        passed(small_in.at[half, pl.ds(0, 15)], g_sem.at[half, 1])
-        others(4, q, lambda n: gy_copy(half, n).start())
+        others(TILES, mine, lambda n: scatter_copy(half, n).start())
+
+    def gather(half):
+        passed(small_in.at[half, pl.ds(0, TILES - 1)], scatter_sem.at[half, 1])
+        small_in[half, mine] = y_out[(half, q, *piece(chip))]
+        whole[(half, q, core, *piece(chip))] = total_of(small_in.at[half], TILES).astype(BF16)
+        others(TILES, mine, lambda n: gather_copy(half, n).start())
 
     def gather_core(half):
-        passed(y_in.at[half, pl.ds(0, 3)], gy_sem.at[half, 1])
+        passed(small_in.at[half, pl.ds(0, TILES - 1)], gather_sem.at[half, 1])
         mate_copy(half).start()
 
     def reduction_sent(half):
         core_copy(half).wait_send()
-        passed(y_in.at[half, pl.ds(0, 3)], y_sem.at[half, 0])
-        passed(small_in.at[half, pl.ds(0, 15)], z_sem.at[half, 0])
-        passed(small_in.at[half, pl.ds(0, 15)], g_sem.at[half, 0])
-        passed(y_in.at[half, pl.ds(0, 3)], gy_sem.at[half, 0])
+        passed(small_in.at[half, pl.ds(0, TILES - 1)], scatter_sem.at[half, 0])
+        passed(small_in.at[half, pl.ds(0, TILES - 1)], gather_sem.at[half, 0])
 
     def ey_copy(to):
         return remote(ex_b.at[q], ex_b.at[q], ey_sem.at[0], ey_sem.at[1], y_id(to))
@@ -547,14 +538,14 @@
 
         @pl.when(picture == 0)
         def _():
-            reduce_y(1)
+            scatter(1)
 
         @pl.when(picture == 1)
         def _():
             for n in range(4):
                 part_out[0, n] = gproj_t[:, 256 * n : 256 * n + 256].T.astype(BF16).reshape(2, 128, 256)
             core_copy(0).start()
-            reduce_z(1)
+            gather(1)
 
         def kernel_block(block):
             lanes = times(block, LANES)
@@ -583,8 +574,7 @@
 
         @pl.when(picture == 1)
         def _():
-            reduce_y(0)
-            gather_z(1)
+            scatter(0)
 
         loop(LANE_BLOCKS // 4, LANE_BLOCKS, kernel_block)
         for row_off in range(3):
@@ -609,8 +599,7 @@
     ex_core.wait_recv()
     ex_b[q] = total_of(ex_a, 2).astype(BF16)
     others(4, q, lambda n: ey_copy(n).start())
-    reduce_z(0)
-    gather_y(1)
+    gather_core(1)
 
     def store_copy(picture, band):
         cells = times(band, BAND_CELLS)
@@ -643,17 +632,14 @@
         loop(begin, end, do_band)
 
     last_start(0)
-    last_bands(0, 0, 3)
+    last_bands(0, 0, 2)
+    gather(0)
     passed(ex_b.at[pl.ds(0, 3)], ey_sem.at[1])
     ex_c[chip] = total_of(ex_b, 4).astype(BF16)
     others(16, chip, lambda n: ez_copy(n).start())
-    gather_z(0)
-    last_bands(0, 3, 4)
-    gather_core(1)
+    last_bands(0, 2, 4)
     last_start(1)
-    last_bands(1, 0, 2)
-    gather_y(0)
-    last_bands(1, 2, 4)
+    last_bands(1, 0, 4)
     passed(ex_c.at[pl.ds(0, 15)], ez_sem.at[1])
     extra_out[...] = total_of(ex_c, 16)
 
@@ -732,13 +718,13 @@
         + rims
         + [
             fl(WIDTH, EXPAND), fl(16, EXPAND), fl(3 * WIDTH, WIDTH), fl(WIDTH, WIDTH), fl(1, WIDTH),
-            bf(2, 4, 2, 128, 256), bf(2, 4, 128, 256), bf(2, 4, 128, 256), bf(2, 4, 128, 256),
-            bf(2, 128, 256), bf(2, 16, 16, LANES), bf(2, 4, 2, 128, 256),
+            bf(2, 4, 2, 128, 256), bf(2, 4, 128, 256), bf(2, 4, 128, 256),
+            bf(2, TILES, 16, LANES), bf(2, 4, 2, 128, 256),
             bf(2, 48, 256), bf(4, 48, 256), bf(16, 48, 256),
             bf(2, CELLS, WIDTH), bf(EXPAND, WIDTH), bf(WIDTH, 3 * WIDTH), bf(WIDTH, WIDTH), bf(256, 256), bf(256, LANES),
             dma((2,)), dma((2, 2, 8)), dma((2, 2, 8)), dma((2,)), dma((2, 2)), dma((2,)), dma((2, BANDS)),
             dma((6,)), dma((2, BANDS)),
-            dma((5,)), dma((5,)), dma((2, 2)), dma((2, 2)), dma((2, 2)), dma((2, 2)), dma((2,)), dma((2,)), dma((6,)),
+            dma((5,)), dma((5,)), dma((2, 2)), dma((2, 2)), dma((2,)), dma((2,)), dma((6,)),
         ],
         compiler_params=pltpu.CompilerParams(
             collective_id=0, has_side_effects=True, vmem_limit_bytes=56 * 2**20

time: 111 us -> 108 us (0.973)
  Pallas kernels: 110 us -> 107 us
    pallas_call x1, Pallas kernels: 103 us -> 100 us  [whole_call(): pl.pallas_call(whole_kernel, out_shape=(jax.ShapeDtypeStruct((2, CELLS, E...]
where the time goes in v6:
time: 108 us
  Pallas kernels  107 us (99%)
    pallas_call x1, Pallas kernels, whole_call(): pl.pallas_call(whole_kernel, out_shape=(jax.ShapeDtypeStruct((2, CELLS, E...  100 us
    pallas_call x1, Pallas kernels, finish(): pl.pallas_call(kernel, out_shape=(jax.ShapeDtypeStruct((2, CELLS, EXPAND)...  6.68 us

profile of v6, /device:TPU:1, one launch (start us, length us, event | category | flops | bytes accessed | tf_op | source)
XLA Modules:
  0.0 107.8 jit_solution(11581041331942403228)
XLA Ops:
  0.6 100.5 %whole.1 = (bf16[2,1024,1024]{2,1,0:T(8,128)(2,1)}, bf16[2,1024,256]{2,1,0:T(8,128)(2,1)}, bf16[2,4,2,128,256]{4,3,2,1,0:T(8,128)(2,1)}, f32[48,256]{1,0:T(8,128)}) custom-call(bf16[2,32,32,1024]{3,2,1,0:T(8,128)(2,1)} %bitcast.11, bf16[2,1024,256]{2,1,0:T(8,128)(2,1)} %bitcast.12, bf16[2,1024,256]{2,1,0:T(8,128)(2,1)} %bitcast.13, f32[3,3,1024]{2,1,0:T(4,128)} %kern_ref.1, ...), custom_call_target="tpu_custom_call" | custom-call | tf_op jit(solution)/shard_map/whole/pallas_call | solution.py:701
  101.1 6.7 %finish.1 = (bf16[2,1024,1024]{2,1,0:T(8,128)(2,1)}, bf16[2,1024,256]{2,1,0:T(8,128)(2,1)}, f32[3,3,1024]{2,1,0:T(4,128)}, f32[1024,256]{1,0:T(8,128)}, f32[256,...) custom-call(bf16[2,1024,1024]{2,1,0:T(8,128)(2,1)} %get-tuple-element.18.refs_0_, ...), custom_call_target="tpu_custom_call" | custom-call | tf_op jit(solution)/shard_map/finish/pallas_call | solution.py:786

commit v7 on v6

--- a/solution.py
+++ b/solution.py
@@ -415,9 +415,9 @@
             )
             back_copy(picture, target, me).start()
 
-        loop(1, TILES, send_back)
         own_back = pltpu.make_async_copy(back.at[picture, own, :], gs.at[picture, own, :], own_sem.at[2])
         own_back.start()
+        loop(1, TILES, send_back)
         own_back.wait()
 
     loop(0, 2, attend_picture)
@@ -532,19 +532,23 @@
                 gproj_t[:, lanes] += dot(flat_t, act[picture, cells, lanes])
 
         loop(0, BANDS, do_band)
-        collect_sides(picture, ggrid, gsides_out, gcorners_out)
-        for copy in rim_of(picture, 1):
-            copy.start()
-
-        @pl.when(picture == 0)
-        def _():
-            scatter(1)
 
         @pl.when(picture == 1)
         def _():
             for n in range(4):
                 part_out[0, n] = gproj_t[:, 256 * n : 256 * n + 256].T.astype(BF16).reshape(2, 128, 256)
             core_copy(0).start()
+
+        collect_sides(picture, ggrid, gsides_out, gcorners_out)
+        for copy in rim_of(picture, 1):
+            copy.start()
+
+        @pl.when(picture == 0)
+        def _():
+            scatter(1)
+
+        @pl.when(picture == 1)
+        def _():
             gather(1)
 
         def kernel_block(block):
@@ -596,9 +600,6 @@
     ex_core = remote(ex_a.at[core], ex_a.at[core], core_send.at[4], core_recv.at[4], mate)
     ex_core.start()
 
-    ex_core.wait_recv()
-    ex_b[q] = total_of(ex_a, 2).astype(BF16)
-    others(4, q, lambda n: ey_copy(n).start())
     gather_core(1)
 
     def store_copy(picture, band):
@@ -632,6 +633,9 @@
         loop(begin, end, do_band)
 
     last_start(0)
+    ex_core.wait_recv()
+    ex_b[q] = total_of(ex_a, 2).astype(BF16)
+    others(4, q, lambda n: ey_copy(n).start())
     last_bands(0, 0, 2)
     gather(0)
     passed(ex_b.at[pl.ds(0, 3)], ey_sem.at[1])

time: 108 us -> 108 us (level)
  no operation moved by 1% of the time
where the time goes in v7:
time: 108 us
  Pallas kernels  107 us (99%)
    pallas_call x1, Pallas kernels, whole_call(): pl.pallas_call(whole_kernel, out_shape=(jax.ShapeDtypeStruct((2, CELLS, E...  100 us
    pallas_call x1, Pallas kernels, finish(): pl.pallas_call(kernel, out_shape=(jax.ShapeDtypeStruct((2, CELLS, EXPAND)...  6.68 us

profile of v7, /device:TPU:1, one launch (start us, length us, event | category | flops | bytes accessed | tf_op | source)
XLA Modules:
  0.0 107.6 jit_solution(7624613266509136831)
XLA Ops:
  0.6 100.3 %whole.1 = (bf16[2,1024,1024]{2,1,0:T(8,128)(2,1)}, bf16[2,1024,256]{2,1,0:T(8,128)(2,1)}, bf16[2,4,2,128,256]{4,3,2,1,0:T(8,128)(2,1)}, f32[48,256]{1,0:T(8,128)}) custom-call(bf16[2,32,32,1024]{3,2,1,0:T(8,128)(2,1)} %bitcast.11, bf16[2,1024,256]{2,1,0:T(8,128)(2,1)} %bitcast.12, bf16[2,1024,256]{2,1,0:T(8,128)(2,1)} %bitcast.13, f32[3,3,1024]{2,1,0:T(4,128)} %kern_ref.1, ...), custom_call_target="tpu_custom_call" | custom-call | tf_op jit(solution)/shard_map/whole/pallas_call | solution.py:705
  100.9 6.7 %finish.1 = (bf16[2,1024,1024]{2,1,0:T(8,128)(2,1)}, bf16[2,1024,256]{2,1,0:T(8,128)(2,1)}, f32[3,3,1024]{2,1,0:T(4,128)}, f32[1024,256]{1,0:T(8,128)}, f32[256,...) custom-call(bf16[2,1024,1024]{2,1,0:T(8,128)(2,1)} %get-tuple-element.18.refs_0_, ...), custom_call_target="tpu_custom_call" | custom-call | tf_op jit(solution)/shard_map/finish/pallas_call | solution.py:790
